TPU v7x, 128 devices: a whole 4x4x4 slice. The times are simulated.
128 devices in a mesh: win: 4 (over y_lo, core), chan: 32 (over x, y_hi, z).
Axes of the slice: x: 4, y: 4 (y_hi: 2, y_lo: 2; y = y_hi * 2 + y_lo), z: 4, core: 2. Of those that a mesh axis runs over, the one named last changes fastest.
Arguments:
- spectra: float32 [4, 2, 512, 8192], P('win', None, 'chan'), may hold values from -6 to 6
Outputs:
- stack: float32 [512, 64, 256], P('chan')
All inputs are finite; a program needn't handle non-finite values.
Results may differ from a plain program's by a relative error of at most 0.000065.
Values sent between devices are 32-bit elements; how exact they have to be, the bound alone decides.
No kernel may reach another device: no remote copies, remote signals or barrier semaphores. Data moves between devices by JAX's collectives and lax.ppermute only.
A program may use at most 64 MiB of HBM per device.

v0:
```python
import math

import jax
import jax.numpy as jnp
from jax import lax
from jax.sharding import PartitionSpec as P

LAGS = 256
STEPS = 4


def broadcast(value, axis, source):
    kept = jnp.where(lax.axis_index(axis) == source, value, 0).astype(value.dtype)
    return lax.psum(kept, axis)


def correlate(real_part, imag_part, src_real, src_imag):
    channel_count = real_part.shape[0]
    bins = real_part.shape[1]
    block_size = min(bins, 1024)
    half_lags = LAGS // 2
    lag_values = jnp.arange(LAGS, dtype=jnp.int32) - half_lags

    def one_block(total, block_index):
        start = block_index * block_size
        own_real = lax.dynamic_slice_in_dim(real_part, start, block_size, 1)
        own_imag = lax.dynamic_slice_in_dim(imag_part, start, block_size, 1)
        far_real = lax.dynamic_slice_in_dim(src_real, start, block_size, 1)
        far_imag = lax.dynamic_slice_in_dim(src_imag, start, block_size, 1)
        cross_real = own_real[:, None, :] * far_real[None] + own_imag[:, None, :] * far_imag[None]
        cross_imag = own_imag[:, None, :] * far_real[None] - own_real[:, None, :] * far_imag[None]
        paired = jnp.concatenate(
            [cross_real.reshape(-1, block_size), -cross_imag.reshape(-1, block_size)], axis=1
        )
        freq_index = start + jnp.arange(block_size, dtype=jnp.int32)
        phase = freq_index[:, None] * lag_values[None, :] % bins
        angle = phase.astype(jnp.float32) * (2.0 * math.pi / bins)
        table = jnp.concatenate([jnp.cos(angle), jnp.sin(angle)], axis=0)
        total = total + jnp.dot(
            paired, table, precision=lax.Precision.HIGHEST, preferred_element_type=jnp.float32
        )
        return (total, None)

    start_total = jnp.zeros((channel_count * channel_count, LAGS), jnp.float32)
    total, unused = lax.scan(
        one_block, start_total, jnp.arange(bins // block_size, dtype=jnp.int32)
    )
    total = total * (1.0 / math.sqrt(bins))
    return total.reshape(channel_count, channel_count, LAGS)


def shards(spectra):
    local = spectra[0]
    real_part = local[0]
    imag_part = local[1]
    stride = lax.axis_size("chan") // STEPS
    windows_count = lax.axis_size("win")
    results = []
    for step in range(STEPS):
        source = broadcast(local, "chan", step * stride)
        lagged = correlate(real_part, imag_part, source[0], source[1])
        results.append(lagged)
    joined = jnp.concatenate(results, axis=1)
    joined = lax.psum(joined, "win") / windows_count
    return joined


def solution(mesh):
    in_specs = (P("win", None, "chan", None),)
    out_specs = P("chan", None, None)
    return jax.shard_map(shards, mesh=mesh, in_specs=in_specs, out_specs=out_specs, check_vma=False)
```

profile of v0, /device:TPU:25, one launch (start us, length us, event | category | flops | bytes accessed | tf_op | source)
XLA Modules:
  0.0 832.9 jit_solution(803246555342933798)
XLA Ops:
  12.2 335.9 %all-reduce.6.cloned.1.call-done = (f32[2,16,8192]{2,1,0:T(8,128)}, f32[2,16,8192]{2,1,0:T(8,128)}, f32[2,16,8192]{2,1,0:T(8,128)}, f32[2,16,8192]{2,1,0:T(8,128)}) async-done(((f32[2,16,8192]{2,1,0:T(8,128)}, f32[2,16,8192]{2,1,0:T(8,128)}, f32[2,16,8192]{2,1,0:T(8,128)}, f32[2,16,8192]{2,1,0:T(8,128)}), (f32[2,16,8192]{2,1,0:T(8,128)}, f32[2,16,8192]{2,1,0:T(8,128)}, f32[2,16,8192]{2,1,0:T(8,128)}, ...) | async-done | bytes 4194320 | tf_op jit(solution)/shard_map/psum | solution.py:14
  351.0 99.0 %while.52 = (s32[]{:T(128)}, f32[256,256]{1,0:T(8,128)}, s32[8]{0:T(128)S(1)}, f32[16,8192]{1,0:T(8,128)}, f32[16,8192]{1,0:T(8,128)}, /*index=5*/f32[16,8192]{1...) while((s32[]{:T(128)}, f32[256,256]{1,0:T(8,128)}, ...), condition=%wide.region_2.3_spmd.clone, body=%wide.region_1.2_spmd.clone.sunk | while | flops 1617298688 | bytes 9709757 | solution.py:45
  354.3 5.2 fusion.98
  366.7 5.2 fusion.98
  379.1 5.2 fusion.98
  391.4 5.2 fusion.98
  403.8 5.2 fusion.98
  416.2 5.2 fusion.98
  428.6 5.2 fusion.98
  441.0 5.2 fusion.98
  451.7 99.2 %while.53 = (s32[]{:T(128)}, f32[256,256]{1,0:T(8,128)}, s32[8]{0:T(128)S(1)}, f32[16,8192]{1,0:T(8,128)}, f32[16,8192]{1,0:T(8,128)}, /*index=5*/f32[16,8192]{1...) while((s32[]{:T(128)}, f32[256,256]{1,0:T(8,128)}, ...), condition=%wide.region_5.6_spmd.clone, body=%wide.region_4.5_spmd.clone.sunk | while | flops 1617298688 | bytes 9709757 | solution.py:45
  455.1 5.2 fusion.102
  467.4 5.2 fusion.102
  479.8 5.2 fusion.102
  492.2 5.2 fusion.102
  504.6 5.2 fusion.102
  517.0 5.2 fusion.102
  555.4 99.2 %while.54 = (s32[]{:T(128)}, f32[256,256]{1,0:T(8,128)}, s32[8]{0:T(128)S(1)}, f32[16,8192]{1,0:T(8,128)}, f32[16,8192]{1,0:T(8,128)}, /*index=5*/f32[16,8192]{1...) while((s32[]{:T(128)}, f32[256,256]{1,0:T(8,128)}, ...), condition=%wide.region_8.9_spmd.clone, body=%wide.region_7.8_spmd.clone.sunk | while | flops 1617298688 | bytes 9709757 | solution.py:45
  608.3 5.2 fusion.106
  656.3 94.0 %while.55 = (s32[]{:T(128)}, f32[256,256]{1,0:T(8,128)S(1)}, s32[8]{0:T(128)S(1)}, f32[16,8192]{1,0:T(8,128)}, f32[16,8192]{1,0:T(8,128)}, /*index=5*/f32[16,819...) while((s32[]{:T(128)}, f32[256,256]{1,0:T(8,128)S(1)}, ...), condition=%wide.region_11.12_spmd.clone, body=%wide.region_10.11_spmd.clone.sunk | while | flops 1617298688 | bytes 9709757 | solution.py:45
  694.9 5.2 fusion.110
  730.1 5.2 fusion.110
  741.9 5.2 fusion.110
  752.5 71.2 %all-reduce.4.cloned.1.call-done = f32[16,64,256]{2,1,0:T(8,128)} async-done(((f32[16,64,256]{2,1,0:T(8,128)}), f32[16,64,256]{2,1,0:T(8,128)}) %all-reduce.4.cloned.1.call-update) | async-done | bytes 1048592 | tf_op jit(solution)/shard_map/psum | solution.py:64
  (262 shorter events, 296.8 us)
Async XLA Ops:
  6.5 341.6 %all-reduce.6.cloned.1.call-start = ((), (), s32[]{:S(2)}) async-start(), calls=%async_computation.1 | async-start | bytes 8388608 | tf_op jit(solution)/shard_map/psum | solution.py:14
  9.8 1.2 copy-start
  9.9 813.9 %all-reduce.4.cloned.1.call-start = ((), (), s32[]{:S(2)}) async-start(), calls=%async_computation | async-start | bytes 2097152 | tf_op jit(solution)/shard_map/psum | solution.py:64
Sparse Core Ops, SparseCore 0:
  10.1 337.9 all-reduce.5
  752.6 71.0 all-reduce.3
where the time goes:
time: 839 us; the launch traced here: 833 us
  waiting for transfers between devices  407 us (49%)
  other arithmetic  188 us (22%)
  matrix products  118 us (14%)
  local copies, waits for them, and re-layouts  83.5 us (10%)
  loops' own time  22.1 us (3%)
  between operations  13.5 us (2%)
    psum x1, waiting for transfers between devices, broadcast(): return lax.psum(kept, axis)  336 us
    cos x32, other arithmetic, one_block(): table = jnp.concatenate([jnp.cos(angle), jnp.sin(angle)], axis=0)  166 us
    dot_general x32, matrix products, one_block(): jnp.dot(paired, table, precision=lax.Precision.HIGHEST, preferred_element...  118 us
    psum x1, waiting for transfers between devices, shards(): joined = lax.psum(joined, 'win') / windows_count  71.2 us
    dynamic_slice x32, local copies, waits for them, and re-layouts, one_block(): far_real = lax.dynamic_slice_in_dim(src_real, start, block_size, 1)  28.5 us
    dynamic_slice x32, local copies, waits for them, and re-layouts, one_block(): far_imag = lax.dynamic_slice_in_dim(src_imag, start, block_size, 1)  28.4 us
    another operation x4, loops' own time, correlate(): lax.scan(one_block, start_total, jnp.arange(bins // block_size, dtype=jnp...  22.1 us
    dynamic_slice x32, local copies, waits for them, and re-layouts, correlate(): lax.scan(one_block, start_total, jnp.arange(bins // block_size, dtype=jnp...  18.7 us
  transfers between devices with their start and end apart: 2, of which 2 were waited for; matrix products, arithmetic and copies ran while one was open for 0% of the time, Pallas kernels for 0%

commit v1 on v0

v1 whole, which is shorter than its diff:
```python
import functools
import math

import jax
import jax.numpy as jnp
import numpy as np
from jax import lax
from jax.experimental import pallas as pl
from jax.experimental.pallas import tpu as pltpu
from jax.sharding import PartitionSpec as P

LAGS = 256
BINS = 8192
HALF = BINS // 2
CH = 16
WINDOWS = 4
PARTS = 8
W = HALF // PARTS
VMEM = pl.BlockSpec(memory_space=pltpu.VMEM)
SHIFTS = (1, -1, 2)


def tables():
    lag = np.arange(LAGS) - LAGS // 2
    turns = (np.arange(HALF)[:, None] * lag[None, :]) % BINS
    angle = 2.0 * np.pi * turns / BINS
    cosine, sine = np.cos(angle), -np.sin(angle)
    cosine[0], sine[0] = lag % 2 == 0, lag % 2 != 0
    table = np.concatenate([cosine.reshape(PARTS, W, LAGS), sine.reshape(PARTS, W, LAGS)], axis=1)
    table = table / (math.sqrt(BINS) * WINDOWS)
    high = table.astype(jnp.bfloat16)
    low = (table - high.astype(np.float64)).astype(jnp.bfloat16)
    return high, low


def fold_kernel(x_ref, all_ref, *quarter_refs):
    lane = lax.broadcasted_iota(jnp.int32, (8, 128), 1)
    mirror = lax.rem(128 - lane, 128)
    for part in range(2):
        for rows in (slice(0, 8), slice(8, 16)):
            for tile in range(HALF // 128):
                piece, offset = divmod(tile * 128, W)
                ahead = x_ref[part, rows, tile * 128 : tile * 128 + 128]
                last = BINS - tile * 128
                back = jnp.take_along_axis(x_ref[part, rows, last - 128 : last], mirror, axis=1)
                edge = last if tile else HALF
                back = jnp.where(lane == 0, x_ref[part, rows, edge : edge + 128] if edge < BINS else 0.0, back)
                columns = slice(offset, offset + 128)
                for row, value in ((part, ahead), (2 + part, back)):
                    all_ref[piece, row, rows, columns] = value
                    if piece >= 2:
                        quarter_refs[piece // 2 - 1][piece % 2, row, rows, columns] = value


def fold(x):
    shape = lambda n: jax.ShapeDtypeStruct((n, 4, CH, W), jnp.float32)
    return pl.pallas_call(
        fold_kernel,
        out_shape=[shape(PARTS)] + [shape(2)] * 3,
        in_specs=[VMEM],
        out_specs=[VMEM] * 4,
    )(x)


def correlate_kernel(ids, x_ref, a_ref, b0, b1, b2, b3, high_ref, low_ref, keep_ref, send_ref, y_ref, total, lh, ll):
    step = pl.program_id(0)
    piece = ids[step]

    @pl.when(step == 0)
    def _():
        total[...] = jnp.zeros_like(total)
        y_ref[0:4] = a_ref[...]
        for place, ref in enumerate((b0, b1, b2, b3)):
            y_ref[4 + place] = ref[...]

    y = [y_ref[step, k] for k in range(4)]
    first = jnp.logical_and(lax.broadcasted_iota(jnp.int32, (CH, 128), 1) == 0, piece == 0)
    for channel in range(CH):
        x = [x_ref[piece, k, channel : channel + 1, :] for k in range(4)]
        ahead = x[0] * y[0] + x[1] * y[1]
        back = x[2] * y[2] + x[3] * y[3]
        even = ahead + back
        odd = (x[1] * y[0] - x[0] * y[1]) + (x[2] * y[3] - x[3] * y[2])
        edge = jnp.where(first, ahead[:, :128] - back[:, :128], odd[:, :128])
        odd = jnp.concatenate([edge, odd[:, 128:]], axis=1)
        rows = slice(CH * channel, CH * channel + CH)
        for columns, value in ((slice(0, W), even), (slice(W, 2 * W), odd)):
            top = value.astype(jnp.bfloat16)
            lh[rows, columns] = top
            ll[rows, columns] = (value - top.astype(jnp.float32)).astype(jnp.bfloat16)
    dot = functools.partial(jnp.dot, preferred_element_type=jnp.float32)
    top, rest = lh[...], ll[...]
    got = dot(top, high_ref[0]) + dot(rest, high_ref[0]) + dot(top, low_ref[0])
    total[...] += got.reshape(CH, CH, LAGS)

    @pl.when(step == PARTS - 1)
    def _():
        core = ids[PARTS]
        keep_ref[...] = total[pl.ds(core * 8, 8)]
        send_ref[...] = total[pl.ds((1 - core) * 8, 8)]


def correlate(ids, x, a, b, high, low):
    whole = lambda *shape: pl.BlockSpec(shape, lambda i, ids: (0,) * len(shape))
    by_piece = pl.BlockSpec((1, 2 * W, LAGS), lambda i, ids: (ids[i], 0, 0))
    half = jax.ShapeDtypeStruct((CH // 2, CH, LAGS), jnp.float32)
    return pl.pallas_call(
        correlate_kernel,
        out_shape=[half, half],
        grid_spec=pltpu.PrefetchScalarGridSpec(
            num_scalar_prefetch=1,
            grid=(PARTS,),
            in_specs=[whole(PARTS, 4, CH, W), whole(4, 4, CH, W)] + [whole(4, CH, W)] * 4 + [by_piece] * 2,
            out_specs=[whole(CH // 2, CH, LAGS)] * 2,
            scratch_shapes=[
                pltpu.VMEM((PARTS, 4, CH, W), jnp.float32),
                pltpu.VMEM((CH, CH, LAGS), jnp.float32),
                pltpu.VMEM((CH * CH, 2 * W), jnp.bfloat16),
                pltpu.VMEM((CH * CH, 2 * W), jnp.bfloat16),
            ],
        ),
        compiler_params=pltpu.CompilerParams(vmem_limit_bytes=32 * 2**20),
        cost_estimate=pl.CostEstimate(
            flops=6 * CH * CH * 2 * HALF * LAGS, bytes_accessed=12 * 2**20, transcendentals=0
        ),
    )(ids, x, a, *b, high, low)


def place_kernel(where_ref, *refs):
    out_ref = refs[-1]
    core = where_ref[4]
    for block in range(4):
        at = where_ref[block]
        out_ref[pl.ds(core * 8, 8), at] = refs[2 * block][...]
        out_ref[pl.ds((1 - core) * 8, 8), at] = refs[2 * block + 1][...]


def place(where, pieces):
    return pl.pallas_call(
        place_kernel,
        out_shape=jax.ShapeDtypeStruct((CH, 4, CH, LAGS), jnp.float32),
        in_specs=[pl.BlockSpec(memory_space=pltpu.SMEM)] + [VMEM] * 8,
        out_specs=VMEM,
    )(where, *pieces)


def shards(spectra):
    me = lax.axis_index("chan")
    at_x, at_h, at_z = me // 8, me // 4 % 2, me % 4
    core = lax.axis_index("win") % 2
    along_x = lambda value, d: lax.ppermute(value, "chan", [(c, (c + 8 * d) % 32) for c in range(32)])
    along_z = lambda value, d: lax.ppermute(value, "chan", [(c, c // 4 * 4 + (c + d) % 4) for c in range(32)])
    other_core = lambda value: lax.ppermute(value, "win", [(w, w ^ 1) for w in range(4)])
    other_chip = lambda value: lax.ppermute(value, "win", [(w, w ^ 2) for w in range(4)])

    high, low = (jnp.asarray(t) for t in tables())
    x, *quarters = fold(spectra[0])
    got = [lax.ppermute(quarters[z - 1], "chan", [(8 * s, 8 * s + z) for s in range(4)]) for z in (1, 2, 3)]
    mine = jnp.where(at_z == 0, x[0:2], got[0] + got[1] + got[2])
    over = lax.ppermute(mine, "chan", [(8 * s + z, 8 * s + 4 + z) for s in range(4) for z in range(4)])
    mine = jnp.where(at_h == 0, mine, over)
    a, b = mine[0], mine[1]
    a_parts, b_blocks = [a], [b]
    for d in SHIFTS:
        a_parts.append(along_z(a, d))
        b_blocks.append(along_x(b, d))
    a_own = jnp.stack(a_parts)
    a_blocks = [a_own] + [along_x(a_own, d) for d in SHIFTS]
    b_parts = [[block] + [along_z(block, d) for d in SHIFTS] for block in b_blocks]

    back = jnp.array((0,) + SHIFTS, jnp.int32)
    from_z = (at_z - back) % 4
    ids = jnp.concatenate([2 * from_z, 2 * from_z + 1, core[None]]).astype(jnp.int32)
    placed = []
    for a_block, b_block in zip(a_blocks, b_parts):
        keep, send = correlate(ids, x, a_block, b_block, high, low)
        pair = keep + other_core(send)
        both = pair + other_chip(pair)
        placed += [both, other_core(both)]
    where = jnp.concatenate([(at_x - back) % 4, core[None]]).astype(jnp.int32)
    return place(where, placed).reshape(CH, 4 * CH, LAGS)


def solution(mesh):
    return jax.shard_map(
        shards,
        mesh=mesh,
        in_specs=(P("win", None, "chan", None),),
        out_specs=P("chan", None, None),
        check_vma=False,
    )
```

time: 839 us -> 120 us (0.14)
  waiting for transfers between devices: 407 us -> 27.1 us
  other arithmetic: 188 us -> 1.97 us
  matrix products: 118 us -> 0 us
  local copies, waits for them, and re-layouts: 83.5 us -> 6.67 us
  starting transfers between devices: 0.04 us -> 51.5 us
  Pallas kernels: 0 us -> 31.8 us
  loops' own time: 22.1 us -> 0 us
  between operations: 13.5 us -> 0.35 us
    psum x2 -> x0, waiting for transfers between devices: 407 us -> none  [the longest x1 336 us: broadcast(): return lax.psum(kept, axis)]
    cos x32 -> x0, other arithmetic: 166 us -> none  [one_block(): table = jnp.concatenate([jnp.cos(angle), jnp.sin(angle)], axis=0)]
    dot_general x32 -> x0, matrix products: 118 us -> none  [one_block(): jnp.dot(paired, table, precision=lax.Precision.HIGHEST, preferred_element...]
    dynamic_slice x96 -> x0, local copies, waits for them, and re-layouts: 75.5 us -> none  [the longest x32 28.5 us: one_block(): far_real = lax.dynamic_slice_in_dim(src_real, start, block_size, 1)]
    ppermute x0 -> x37, starting transfers between devices: none -> 51.5 us  [the longest x15 19.5 us: shards(): lax.ppermute(value, 'chan', [(c, c // 4 * 4 + (c + d) % 4) for c in range...]
    pallas_call x0 -> x6, Pallas kernels: none -> 31.8 us  [the longest x4 26.8 us: correlate(): pl.pallas_call(correlate_kernel, out_shape=[half, half], grid_spec=pltpu....]
    ppermute x0 -> x37, waiting for transfers between devices: none -> 27.1 us  [the longest x1 21.7 us: shards(): lax.ppermute(mine, 'chan', [(8 * s + z, 8 * s + 4 + z) for s in range(4)...]
    another operation x4 -> x0, loops' own time: 22.1 us -> none  [correlate(): lax.scan(one_block, start_total, jnp.arange(bins // block_size, dtype=jnp...]
  transfers between devices with their start and end apart: 2 -> 37, of which waited for: 2 -> 7; matrix products, arithmetic and copies ran while one was open for 0% -> 1% of each run, Pallas kernels for 0% -> 22%
where the time goes in v1:
time: 120 us; the launch traced here: 119 us
  starting transfers between devices  51.5 us (43%)
  Pallas kernels  31.8 us (26%)
  waiting for transfers between devices  27.1 us (23%)
  local copies, waits for them, and re-layouts  6.67 us (6%)
  other arithmetic  1.97 us (2%)
    pallas_call x4, Pallas kernels, correlate(): pl.pallas_call(correlate_kernel, out_shape=[half, half], grid_spec=pltpu....  26.8 us
    ppermute x1, waiting for transfers between devices, shards(): lax.ppermute(mine, 'chan', [(8 * s + z, 8 * s + 4 + z) for s in range(4)...  21.7 us
    ppermute x15, starting transfers between devices, shards(): lax.ppermute(value, 'chan', [(c, c // 4 * 4 + (c + d) % 4) for c in range...  19.5 us
    ppermute x8, starting transfers between devices, shards(): lax.ppermute(value, 'win', [(w, w ^ 1) for w in range(4)])  15.5 us
    ppermute x6, starting transfers between devices, shards(): lax.ppermute(value, 'chan', [(c, (c + 8 * d) % 32) for c in range(32)])  9.98 us
    unnamed x24, local copies, waits for them, and re-layouts  6.64 us
    ppermute x4, waiting for transfers between devices, shards(): lax.ppermute(value, 'win', [(w, w ^ 2) for w in range(4)])  4.15 us
    ppermute x4, starting transfers between devices, shards(): lax.ppermute(value, 'win', [(w, w ^ 2) for w in range(4)])  3.23 us
  transfers between devices with their start and end apart: 37, of which 7 were waited for; matrix products, arithmetic and copies ran while one was open for 1% of the time, Pallas kernels for 22%

profile of v1, /device:TPU:25, one launch (start us, length us, event | category | flops | bytes accessed | tf_op | source)
XLA Modules:
  0.0 119.4 jit_solution(12431602218742635345)
XLA Ops:
  0.0 2.7 %shard_map.46 = (f32[8,4,16,512]{3,2,1,0:T(8,128)}, f32[2,4,16,512]{3,2,1,0:T(8,128)}, f32[2,4,16,512]{3,2,1,0:T(8,128)}, f32[2,4,16,512]{3,2,1,0:T(8,128)}) custom-call(f32[2,16,8192]{2,1,0:T(8,128)} %bitcast.10), custom_call_target="tpu_custom_call" | custom-call | tf_op jit(solution)/shard_map/pallas_call | solution.py:57
  7.1 21.7 %collective-permute-done.3 = f32[2,4,16,512]{3,2,1,0:T(8,128)S(1)} collective-permute-done((f32[2,4,16,512]{3,2,1,0:T(8,128)S(1)}, f32[2,4,16,512]{3,2,1,0:T(8,128)S(1)}, u32[]{:S(2)}, u32[]{:S(2)}) %collective-permute-start.3) | collective-permute-done | bytes 262176 | tf_op jit(solution)/shard_map/ppermute | solution.py:160
  28.9 3.7 %collective-permute-start.6 = (f32[4,16,512]{2,1,0:T(8,128)S(1)}, f32[4,16,512]{2,1,0:T(8,128)S(1)}, u32[]{:S(2)}, u32[]{:S(2)}) collective-permute-start(f32[4,16,512]{2,1,0:T(8,128)S(1)} %get-tuple-element.32), channel_id=1, source_target_pairs={{0,2},{1,3},{2,0},{3,1},{4,6},{5,7},{6,4},{7,5},{8,10},{9,11},{10,... | collective-permute-start | bytes 393224 | tf_op jit(solution)/shard_map/ppermute | solution.py:152
  34.1 2.6 %collective-permute-start.8 = (f32[4,16,512]{2,1,0:T(8,128)S(1)}, f32[4,16,512]{2,1,0:T(8,128)S(1)}, u32[]{:S(2)}, u32[]{:S(2)}) collective-permute-start(f32[4,16,512]{2,1,0:T(8,128)S(1)} %get-tuple-element.31.b0), channel_id=1, source_target_pairs={{0,3},{1,0},{2,1},{3,2},{4,7},{5,4},{6,5},{7,6},{8,11},{9,8},{10,9... | collective-permute-start | bytes 393224 | tf_op jit(solution)/shard_map/ppermute | solution.py:152
  39.3 2.1 %collective-permute-start.22 = (f32[4,16,512]{2,1,0:T(8,128)S(1)}, f32[4,16,512]{2,1,0:T(8,128)S(1)}, u32[]{:S(2)}, u32[]{:S(2)}) collective-permute-start(f32[4,16,512]{2,1,0:T(8,128)S(1)} %get-tuple-element.31.b0), channel_id=1, source_target_pairs={{0,24},{1,25},{2,26},{3,27},{4,28},{5,29},{6,30},{7,31},{8,0},{9,1... | collective-permute-start | bytes 393224 | tf_op jit(solution)/shard_map/ppermute | solution.py:151
  42.2 2.7 %collective-permute-start.30 = (f32[4,16,512]{2,1,0:T(8,128)S(1)}, f32[4,16,512]{2,1,0:T(8,128)S(1)}, u32[]{:S(2)}, u32[]{:S(2)}) collective-permute-start(f32[4,16,512]{2,1,0:T(8,128)S(1)} %get-tuple-element.31.b0), channel_id=1, source_target_pairs={{0,16},{1,17},{2,18},{3,19},{4,20},{5,21},{6,22},{7,23},{8,24},{9,... | collective-permute-start | bytes 393224 | tf_op jit(solution)/shard_map/ppermute | solution.py:151
  45.4 2.4 %collective-permute-start.21 = (f32[4,4,16,512]{3,2,1,0:T(8,128)S(1)}, f32[4,4,16,512]{3,2,1,0:T(8,128)S(1)}, u32[]{:S(2)}, u32[]{:S(2)}) collective-permute-start(f32[4,4,16,512]{3,2,1,0:T(8,128)S(1)} %pad_maximum_fusion.a_ref), channel_id=1, source_target_pairs={{0,24},{1,25},{2,26},{3,27},{4,28},{5,29},{6,30},{7,31},{8,0},{9,1... | collective-permute-start | bytes 1572872 | tf_op jit(solution)/shard_map/ppermute | solution.py:151
  47.8 2.7 %collective-permute-start.16 = (f32[4,16,512]{2,1,0:T(8,128)S(1)}, f32[4,16,512]{2,1,0:T(8,128)S(1)}, u32[]{:S(2)}, u32[]{:S(2)}) collective-permute-start(f32[4,16,512]{2,1,0:T(8,128)S(1)} %collective-permute-done.14.b0), channel_id=1, source_target_pairs={{0,3},{1,0},{2,1},{3,2},{4,7},{5,4},{6,5},{7,6},{8,11},{9,8},{10,9... | collective-permute-start | bytes 393224 | tf_op jit(solution)/shard_map/ppermute | solution.py:152
  52.8 2.2 %copy-done.1 = bf16[8,1024,256]{2,1,0:T(8,128)(2,1)S(1)} copy-done((bf16[8,1024,256]{2,1,0:T(8,128)(2,1)S(1)}, bf16[8,1024,256]{2,1,0:T(8,128)(2,1)}, u32[]{:S(2)}) %copy-start.1) | copy-done | bytes 4194328
  55.0 2.2 %copy-done.2 = bf16[8,1024,256]{2,1,0:T(8,128)(2,1)S(1)} copy-done((bf16[8,1024,256]{2,1,0:T(8,128)(2,1)S(1)}, bf16[8,1024,256]{2,1,0:T(8,128)(2,1)}, u32[]{:S(2)}) %copy-start.2) | copy-done | bytes 4194328
  57.2 6.7 %shard_map.47 = (f32[8,16,256]{2,1,0:T(8,128)S(1)}, f32[8,16,256]{2,1,0:T(8,128)S(1)}) custom-call(s32[9]{0:T(128)S(1)} %pad_add_fusion.1.ids, f32[8,4,16,512]{3,2,1,0:T(8,128)S(1)} %copy-done, f32[4,4,16,512]{3,2,1,0:T(8,128)S(1)} %pad_maximum_fusion.a_ref, f32[4,16,512]{2,1,0:T(8,128)S(1)} %get-tuple-element.31.b0, ...), custom_call_target="tpu_custom_call" | custom-call | flops 3221225472 | bytes 12582912 | tf_op jit(solution)/shard_map/pallas_call | solution.py:107
  65.2 2.7 %collective-permute-start.24 = (f32[4,16,512]{2,1,0:T(8,128)S(1)}, f32[4,16,512]{2,1,0:T(8,128)S(1)}, u32[]{:S(2)}, u32[]{:S(2)}) collective-permute-start(f32[4,16,512]{2,1,0:T(8,128)S(1)} %collective-permute-done.22.b0), channel_id=1, source_target_pairs={{0,3},{1,0},{2,1},{3,2},{4,7},{5,4},{6,5},{7,6},{8,11},{9,8},{10,9... | collective-permute-start | bytes 393224 | tf_op jit(solution)/shard_map/ppermute | solution.py:152
  68.3 6.7 %shard_map.48 = (f32[8,16,256]{2,1,0:T(8,128)S(1)}, f32[8,16,256]{2,1,0:T(8,128)S(1)}) custom-call(s32[9]{0:T(128)S(1)} %pad_add_fusion.1.ids, f32[8,4,16,512]{3,2,1,0:T(8,128)S(1)} %copy-done, f32[4,4,16,512]{3,2,1,0:T(8,128)S(1)} %collective-permute-done.13.a_ref, f32[4,16,512]{2,1,0:T(8,128)S(1)} %collective-permute-done.14.b0, ...), custom_call_target="tpu_custom_call" | custom-call | flops 3221225472 | bytes 12582912 | tf_op jit(solution)/shard_map/pallas_call | solution.py:107
  75.1 7.0 %collective-permute-start.10 = (f32[8,16,256]{2,1,0:T(8,128)S(1)}, f32[8,16,256]{2,1,0:T(8,128)S(1)}, u32[]{:S(2)}, u32[]{:S(2)}) collective-permute-start(f32[8,16,256]{2,1,0:T(8,128)S(1)} %get-tuple-element.22), channel_id=1, source_target_pairs={{0,32},{32,0},{64,96},{96,64},{1,33},{33,1},{65,97},{97,65},{2,34}... | collective-permute-start | bytes 393224 | tf_op jit(solution)/shard_map/ppermute | solution.py:153
  82.1 2.7 %collective-permute-start.32 = (f32[4,16,512]{2,1,0:T(8,128)S(1)}, f32[4,16,512]{2,1,0:T(8,128)S(1)}, u32[]{:S(2)}, u32[]{:S(2)}) collective-permute-start(f32[4,16,512]{2,1,0:T(8,128)S(1)} %collective-permute-done.30.b0), channel_id=1, source_target_pairs={{0,3},{1,0},{2,1},{3,2},{4,7},{5,4},{6,5},{7,6},{8,11},{9,8},{10,9... | collective-permute-start | bytes 393224 | tf_op jit(solution)/shard_map/ppermute | solution.py:152
  85.5 6.7 %shard_map.49 = (f32[8,16,256]{2,1,0:T(8,128)S(1)}, f32[8,16,256]{2,1,0:T(8,128)S(1)}) custom-call(s32[9]{0:T(128)S(1)} %pad_add_fusion.1.ids, f32[8,4,16,512]{3,2,1,0:T(8,128)S(1)} %copy-done, f32[4,4,16,512]{3,2,1,0:T(8,128)S(1)} %collective-permute-done.21.a_ref, f32[4,16,512]{2,1,0:T(8,128)S(1)} %collective-permute-done.22.b0, ...), custom_call_target="tpu_custom_call" | custom-call | flops 3221225472 | bytes 12582912 | tf_op jit(solution)/shard_map/pallas_call | solution.py:107
  93.5 6.7 %shard_map.50 = (f32[8,16,256]{2,1,0:T(8,128)S(1)}, f32[8,16,256]{2,1,0:T(8,128)S(1)}) custom-call(s32[9]{0:T(128)S(1)} %pad_add_fusion.1.ids, f32[8,4,16,512]{3,2,1,0:T(8,128)S(1)} %copy-done, f32[4,4,16,512]{3,2,1,0:T(8,128)S(1)} %collective-permute-done.29.a_ref, f32[4,16,512]{2,1,0:T(8,128)S(1)} %collective-permute-done.30.b0, ...), custom_call_target="tpu_custom_call" | custom-call | flops 3221225472 | bytes 12582912 | tf_op jit(solution)/shard_map/pallas_call | solution.py:107
  100.7 1.5 %collective-permute-start.19 = (f32[8,16,256]{2,1,0:T(8,128)S(1)}, f32[8,16,256]{2,1,0:T(8,128)S(1)}, u32[]{:S(2)}, u32[]{:S(2)}) collective-permute-start(f32[8,16,256]{2,1,0:T(8,128)S(1)} %add.65), channel_id=1, source_target_pairs={{0,64},{32,96},{64,0},{96,32},{1,65},{33,97},{65,1},{97,33},{2,66}... | collective-permute-start | bytes 393224 | tf_op jit(solution)/shard_map/ppermute | solution.py:154
  102.4 1.5 %collective-permute-start.35 = (f32[8,16,256]{2,1,0:T(8,128)S(1)}, f32[8,16,256]{2,1,0:T(8,128)S(1)}, u32[]{:S(2)}, u32[]{:S(2)}) collective-permute-start(f32[8,16,256]{2,1,0:T(8,128)S(1)} %add.69), channel_id=1, source_target_pairs={{0,64},{32,96},{64,0},{96,32},{1,65},{33,97},{65,1},{97,33},{2,66}... | collective-permute-start | bytes 393224 | tf_op jit(solution)/shard_map/ppermute | solution.py:154
  103.9 1.5 %collective-permute-done.11 = f32[8,16,256]{2,1,0:T(8,128)S(1)} collective-permute-done((f32[8,16,256]{2,1,0:T(8,128)S(1)}, f32[8,16,256]{2,1,0:T(8,128)S(1)}, u32[]{:S(2)}, u32[]{:S(2)}) %collective-permute-start.11) | collective-permute-done | bytes 131104 | tf_op jit(solution)/shard_map/ppermute | solution.py:154
  105.5 1.9 %collective-permute-start.12 = (f32[8,16,256]{2,1,0:T(8,128)S(1)}, f32[8,16,256]{2,1,0:T(8,128)S(1)}, u32[]{:S(2)}, u32[]{:S(2)}) collective-permute-start(f32[8,16,256]{2,1,0:T(8,128)S(1)} %add.64.refs_0_), channel_id=1, source_target_pairs={{0,32},{32,0},{64,96},{96,64},{1,33},{33,1},{65,97},{97,65},{2,34}... | collective-permute-start | bytes 393224 | tf_op jit(solution)/shard_map/ppermute | solution.py:153
  108.3 1.9 %collective-permute-start.20 = (f32[8,16,256]{2,1,0:T(8,128)S(1)}, f32[8,16,256]{2,1,0:T(8,128)S(1)}, u32[]{:S(2)}, u32[]{:S(2)}) collective-permute-start(f32[8,16,256]{2,1,0:T(8,128)S(1)} %add.66.refs_2_), channel_id=1, source_target_pairs={{0,32},{32,0},{64,96},{96,64},{1,33},{33,1},{65,97},{97,65},{2,34}... | collective-permute-start | bytes 393224 | tf_op jit(solution)/shard_map/ppermute | solution.py:153
  111.1 1.9 %collective-permute-start.28 = (f32[8,16,256]{2,1,0:T(8,128)S(1)}, f32[8,16,256]{2,1,0:T(8,128)S(1)}, u32[]{:S(2)}, u32[]{:S(2)}) collective-permute-start(f32[8,16,256]{2,1,0:T(8,128)S(1)} %add.68.refs_4_), channel_id=1, source_target_pairs={{0,32},{32,0},{64,96},{96,64},{1,33},{33,1},{65,97},{97,65},{2,34}... | collective-permute-start | bytes 393224 | tf_op jit(solution)/shard_map/ppermute | solution.py:153
  117.1 2.3 %shard_map.51 = f32[16,4,16,256]{3,2,1,0:T(8,128)} custom-call(s32[5]{0:T(128)} %pad_add_fusion.where_ref, f32[8,16,256]{2,1,0:T(8,128)} %copy-done.3, f32[8,16,256]{2,1,0:T(8,128)} %copy-done.7, f32[8,16,256]{2,1,0:T(8,128)} %copy-done.4, f32[8,16,256]{2,1,0:T(8,128)} %copy-done.8, f32[8,16,256]{2,1,0:T(8,128)} %copy-done.5, f32[8,16,256]{2,1,0:T(8,128)} %copy-done.9, ...), custom_call_target="tpu_custom_call" | custom-call | tf_op jit(solution)/shard_map/pallas_call | solution.py:139
  (95 shorter events, 22.2 us)
Async XLA Ops:
  5.8 23.1 %collective-permute-start.3 = (f32[2,4,16,512]{3,2,1,0:T(8,128)S(1)}, f32[2,4,16,512]{3,2,1,0:T(8,128)S(1)}, u32[]{:S(2)}, u32[]{:S(2)}) collective-permute-start(f32[2,4,16,512]{3,2,1,0:T(8,128)S(1)} %add_select_fusion), channel_id=1, source_target_pairs={{0,4},{1,5},{2,6},{3,7},{8,12},{9,13},{10,14},{11,15},{16,20},{17,... | collective-permute-start | bytes 786440 | tf_op jit(solution)/shard_map/ppermute | solution.py:160
  34.1 10.9 %collective-permute-start.8 = (f32[4,16,512]{2,1,0:T(8,128)S(1)}, f32[4,16,512]{2,1,0:T(8,128)S(1)}, u32[]{:S(2)}, u32[]{:S(2)}) collective-permute-start(f32[4,16,512]{2,1,0:T(8,128)S(1)} %get-tuple-element.31.b0), channel_id=1, source_target_pairs={{0,3},{1,0},{2,1},{3,2},{4,7},{5,4},{6,5},{7,6},{8,11},{9,8},{10,9... | collective-permute-start | bytes 393224 | tf_op jit(solution)/shard_map/ppermute | solution.py:152
  36.8 8.6 %collective-permute-start.9 = (f32[4,16,512]{2,1,0:T(8,128)S(1)}, f32[4,16,512]{2,1,0:T(8,128)S(1)}, u32[]{:S(2)}, u32[]{:S(2)}) collective-permute-start(f32[4,16,512]{2,1,0:T(8,128)S(1)} %get-tuple-element.31.b0), channel_id=1, source_target_pairs={{0,2},{1,3},{2,0},{3,1},{4,6},{5,7},{6,4},{7,5},{8,10},{9,11},{10,... | collective-permute-start | bytes 393224 | tf_op jit(solution)/shard_map/ppermute | solution.py:152
  38.0 9.7 %collective-permute-start.14 = (f32[4,16,512]{2,1,0:T(8,128)S(1)}, f32[4,16,512]{2,1,0:T(8,128)S(1)}, u32[]{:S(2)}, u32[]{:S(2)}) collective-permute-start(f32[4,16,512]{2,1,0:T(8,128)S(1)} %get-tuple-element.31.b0), channel_id=1, source_target_pairs={{0,8},{1,9},{2,10},{3,11},{4,12},{5,13},{6,14},{7,15},{8,16},{9,17... | collective-permute-start | bytes 393224 | tf_op jit(solution)/shard_map/ppermute | solution.py:151
  39.3 8.5 %collective-permute-start.22 = (f32[4,16,512]{2,1,0:T(8,128)S(1)}, f32[4,16,512]{2,1,0:T(8,128)S(1)}, u32[]{:S(2)}, u32[]{:S(2)}) collective-permute-start(f32[4,16,512]{2,1,0:T(8,128)S(1)} %get-tuple-element.31.b0), channel_id=1, source_target_pairs={{0,24},{1,25},{2,26},{3,27},{4,28},{5,29},{6,30},{7,31},{8,0},{9,1... | collective-permute-start | bytes 393224 | tf_op jit(solution)/shard_map/ppermute | solution.py:151
  42.2 8.2 %collective-permute-start.30 = (f32[4,16,512]{2,1,0:T(8,128)S(1)}, f32[4,16,512]{2,1,0:T(8,128)S(1)}, u32[]{:S(2)}, u32[]{:S(2)}) collective-permute-start(f32[4,16,512]{2,1,0:T(8,128)S(1)} %get-tuple-element.31.b0), channel_id=1, source_target_pairs={{0,16},{1,17},{2,18},{3,19},{4,20},{5,21},{6,22},{7,23},{8,24},{9,... | collective-permute-start | bytes 393224 | tf_op jit(solution)/shard_map/ppermute | solution.py:151
  45.0 22.9 %collective-permute-start.13 = (f32[4,4,16,512]{3,2,1,0:T(8,128)S(1)}, f32[4,4,16,512]{3,2,1,0:T(8,128)S(1)}, u32[]{:S(2)}, u32[]{:S(2)}) collective-permute-start(f32[4,4,16,512]{3,2,1,0:T(8,128)S(1)} %pad_maximum_fusion.a_ref), channel_id=1, source_target_pairs={{0,8},{1,9},{2,10},{3,11},{4,12},{5,13},{6,14},{7,15},{8,16},{9,17... | collective-permute-start | bytes 1572872 | tf_op jit(solution)/shard_map/ppermute | solution.py:151
  45.4 39.4 %collective-permute-start.21 = (f32[4,4,16,512]{3,2,1,0:T(8,128)S(1)}, f32[4,4,16,512]{3,2,1,0:T(8,128)S(1)}, u32[]{:S(2)}, u32[]{:S(2)}) collective-permute-start(f32[4,4,16,512]{3,2,1,0:T(8,128)S(1)} %pad_maximum_fusion.a_ref), channel_id=1, source_target_pairs={{0,24},{1,25},{2,26},{3,27},{4,28},{5,29},{6,30},{7,31},{8,0},{9,1... | collective-permute-start | bytes 1572872 | tf_op jit(solution)/shard_map/ppermute | solution.py:151
  47.8 16.1 %collective-permute-start.15 = (f32[4,16,512]{2,1,0:T(8,128)S(1)}, f32[4,16,512]{2,1,0:T(8,128)S(1)}, u32[]{:S(2)}, u32[]{:S(2)}) collective-permute-start(f32[4,16,512]{2,1,0:T(8,128)S(1)} %collective-permute-done.14.b0), channel_id=1, source_target_pairs={{0,1},{1,2},{2,3},{3,0},{4,5},{5,6},{6,7},{7,4},{8,9},{9,10},{10,1... | collective-permute-start | bytes 393224 | tf_op jit(solution)/shard_map/ppermute | solution.py:152
  47.8 17.4 %collective-permute-start.16 = (f32[4,16,512]{2,1,0:T(8,128)S(1)}, f32[4,16,512]{2,1,0:T(8,128)S(1)}, u32[]{:S(2)}, u32[]{:S(2)}) collective-permute-start(f32[4,16,512]{2,1,0:T(8,128)S(1)} %collective-permute-done.14.b0), channel_id=1, source_target_pairs={{0,3},{1,0},{2,1},{3,2},{4,7},{5,4},{6,5},{7,6},{8,11},{9,8},{10,9... | collective-permute-start | bytes 393224 | tf_op jit(solution)/shard_map/ppermute | solution.py:152
  50.5 14.7 %collective-permute-start.17 = (f32[4,16,512]{2,1,0:T(8,128)S(1)}, f32[4,16,512]{2,1,0:T(8,128)S(1)}, u32[]{:S(2)}, u32[]{:S(2)}) collective-permute-start(f32[4,16,512]{2,1,0:T(8,128)S(1)} %collective-permute-done.14.b0), channel_id=1, source_target_pairs={{0,2},{1,3},{2,0},{3,1},{4,6},{5,7},{6,4},{7,5},{8,10},{9,11},{10,... | collective-permute-start | bytes 393224 | tf_op jit(solution)/shard_map/ppermute | solution.py:152
  63.9 29.6 %collective-permute-start.29 = (f32[4,4,16,512]{3,2,1,0:T(8,128)S(1)}, f32[4,4,16,512]{3,2,1,0:T(8,128)S(1)}, u32[]{:S(2)}, u32[]{:S(2)}) collective-permute-start(f32[4,4,16,512]{3,2,1,0:T(8,128)S(1)} %pad_maximum_fusion.a_ref), channel_id=1, source_target_pairs={{0,16},{1,17},{2,18},{3,19},{4,20},{5,21},{6,22},{7,23},{8,24},{9,... | collective-permute-start | bytes 1572872 | tf_op jit(solution)/shard_map/ppermute | solution.py:151
  65.2 9.9 %collective-permute-start.23 = (f32[4,16,512]{2,1,0:T(8,128)S(1)}, f32[4,16,512]{2,1,0:T(8,128)S(1)}, u32[]{:S(2)}, u32[]{:S(2)}) collective-permute-start(f32[4,16,512]{2,1,0:T(8,128)S(1)} %collective-permute-done.22.b0), channel_id=1, source_target_pairs={{0,1},{1,2},{2,3},{3,0},{4,5},{5,6},{6,7},{7,4},{8,9},{9,10},{10,1... | collective-permute-start | bytes 393224 | tf_op jit(solution)/shard_map/ppermute | solution.py:152
  65.2 16.9 %collective-permute-start.24 = (f32[4,16,512]{2,1,0:T(8,128)S(1)}, f32[4,16,512]{2,1,0:T(8,128)S(1)}, u32[]{:S(2)}, u32[]{:S(2)}) collective-permute-start(f32[4,16,512]{2,1,0:T(8,128)S(1)} %collective-permute-done.22.b0), channel_id=1, source_target_pairs={{0,3},{1,0},{2,1},{3,2},{4,7},{5,4},{6,5},{7,6},{8,11},{9,8},{10,9... | collective-permute-start | bytes 393224 | tf_op jit(solution)/shard_map/ppermute | solution.py:152
  67.8 14.3 %collective-permute-start.25 = (f32[4,16,512]{2,1,0:T(8,128)S(1)}, f32[4,16,512]{2,1,0:T(8,128)S(1)}, u32[]{:S(2)}, u32[]{:S(2)}) collective-permute-start(f32[4,16,512]{2,1,0:T(8,128)S(1)} %collective-permute-done.22.b0), channel_id=1, source_target_pairs={{0,2},{1,3},{2,0},{3,1},{4,6},{5,7},{6,4},{7,5},{8,10},{9,11},{10,... | collective-permute-start | bytes 393224 | tf_op jit(solution)/shard_map/ppermute | solution.py:152
  75.1 25.5 %collective-permute-start.10 = (f32[8,16,256]{2,1,0:T(8,128)S(1)}, f32[8,16,256]{2,1,0:T(8,128)S(1)}, u32[]{:S(2)}, u32[]{:S(2)}) collective-permute-start(f32[8,16,256]{2,1,0:T(8,128)S(1)} %get-tuple-element.22), channel_id=1, source_target_pairs={{0,32},{32,0},{64,96},{96,64},{1,33},{33,1},{65,97},{97,65},{2,34}... | collective-permute-start | bytes 393224 | tf_op jit(solution)/shard_map/ppermute | solution.py:153
  82.1 10.1 %collective-permute-start.31 = (f32[4,16,512]{2,1,0:T(8,128)S(1)}, f32[4,16,512]{2,1,0:T(8,128)S(1)}, u32[]{:S(2)}, u32[]{:S(2)}) collective-permute-start(f32[4,16,512]{2,1,0:T(8,128)S(1)} %collective-permute-done.30.b0), channel_id=1, source_target_pairs={{0,1},{1,2},{2,3},{3,0},{4,5},{5,6},{6,7},{7,4},{8,9},{9,10},{10,1... | collective-permute-start | bytes 393224 | tf_op jit(solution)/shard_map/ppermute | solution.py:152
  82.1 11.1 %collective-permute-start.32 = (f32[4,16,512]{2,1,0:T(8,128)S(1)}, f32[4,16,512]{2,1,0:T(8,128)S(1)}, u32[]{:S(2)}, u32[]{:S(2)}) collective-permute-start(f32[4,16,512]{2,1,0:T(8,128)S(1)} %collective-permute-done.30.b0), channel_id=1, source_target_pairs={{0,3},{1,0},{2,1},{3,2},{4,7},{5,4},{6,5},{7,6},{8,11},{9,8},{10,9... | collective-permute-start | bytes 393224 | tf_op jit(solution)/shard_map/ppermute | solution.py:152
  84.8 8.7 %collective-permute-start.33 = (f32[4,16,512]{2,1,0:T(8,128)S(1)}, f32[4,16,512]{2,1,0:T(8,128)S(1)}, u32[]{:S(2)}, u32[]{:S(2)}) collective-permute-start(f32[4,16,512]{2,1,0:T(8,128)S(1)} %collective-permute-done.30.b0), channel_id=1, source_target_pairs={{0,2},{1,3},{2,0},{3,1},{4,6},{5,7},{6,4},{7,5},{8,10},{9,11},{10,... | collective-permute-start | bytes 393224 | tf_op jit(solution)/shard_map/ppermute | solution.py:152
  92.2 8.4 %collective-permute-start.18 = (f32[8,16,256]{2,1,0:T(8,128)S(1)}, f32[8,16,256]{2,1,0:T(8,128)S(1)}, u32[]{:S(2)}, u32[]{:S(2)}) collective-permute-start(f32[8,16,256]{2,1,0:T(8,128)S(1)} %get-tuple-element.24), channel_id=1, source_target_pairs={{0,32},{32,0},{64,96},{96,64},{1,33},{33,1},{65,97},{97,65},{2,34}... | collective-permute-start | bytes 393224 | tf_op jit(solution)/shard_map/ppermute | solution.py:153
  93.2 9.0 %collective-permute-start.26 = (f32[8,16,256]{2,1,0:T(8,128)S(1)}, f32[8,16,256]{2,1,0:T(8,128)S(1)}, u32[]{:S(2)}, u32[]{:S(2)}) collective-permute-start(f32[8,16,256]{2,1,0:T(8,128)S(1)} %get-tuple-element.26), channel_id=1, source_target_pairs={{0,32},{32,0},{64,96},{96,64},{1,33},{33,1},{65,97},{97,65},{2,34}... | collective-permute-start | bytes 393224 | tf_op jit(solution)/shard_map/ppermute | solution.py:153
  102.2 8.8 %collective-permute-start.27 = (f32[8,16,256]{2,1,0:T(8,128)S(1)}, f32[8,16,256]{2,1,0:T(8,128)S(1)}, u32[]{:S(2)}, u32[]{:S(2)}) collective-permute-start(f32[8,16,256]{2,1,0:T(8,128)S(1)} %add.67), channel_id=1, source_target_pairs={{0,64},{32,96},{64,0},{96,32},{1,65},{33,97},{65,1},{97,33},{2,66}... | collective-permute-start | bytes 393224 | tf_op jit(solution)/shard_map/ppermute | solution.py:154
  102.4 11.5 %collective-permute-start.35 = (f32[8,16,256]{2,1,0:T(8,128)S(1)}, f32[8,16,256]{2,1,0:T(8,128)S(1)}, u32[]{:S(2)}, u32[]{:S(2)}) collective-permute-start(f32[8,16,256]{2,1,0:T(8,128)S(1)} %add.69), channel_id=1, source_target_pairs={{0,64},{32,96},{64,0},{96,32},{1,65},{33,97},{65,1},{97,33},{2,66}... | collective-permute-start | bytes 393224 | tf_op jit(solution)/shard_map/ppermute | solution.py:154
  105.5 10.2 %collective-permute-start.12 = (f32[8,16,256]{2,1,0:T(8,128)S(1)}, f32[8,16,256]{2,1,0:T(8,128)S(1)}, u32[]{:S(2)}, u32[]{:S(2)}) collective-permute-start(f32[8,16,256]{2,1,0:T(8,128)S(1)} %add.64.refs_0_), channel_id=1, source_target_pairs={{0,32},{32,0},{64,96},{96,64},{1,33},{33,1},{65,97},{97,65},{2,34}... | collective-permute-start | bytes 393224 | tf_op jit(solution)/shard_map/ppermute | solution.py:153
  (25 other events, 140.3 us)

commit v2 on v1

v2 whole, which is shorter than its diff:
```python
import functools
import math

import jax
import jax.numpy as jnp
import numpy as np
from jax import lax
from jax.experimental import pallas as pl
from jax.experimental.pallas import tpu as pltpu
from jax.sharding import PartitionSpec as P

LAGS = 256
BINS = 8192
HALF = BINS // 2
CH = 16
WINDOWS = 4
PARTS = 8
W = HALF // PARTS
VMEM = pl.BlockSpec(memory_space=pltpu.VMEM)
SHIFTS = (1, -1, 2)


def tables():
    lag = np.arange(LAGS) - LAGS // 2
    turns = (np.arange(HALF)[:, None] * lag[None, :]) % BINS
    angle = 2.0 * np.pi * turns / BINS
    cosine, sine = np.cos(angle), -np.sin(angle)
    cosine[0], sine[0] = lag % 2 == 0, lag % 2 != 0
    table = np.concatenate([cosine.reshape(PARTS, W, LAGS), sine.reshape(PARTS, W, LAGS)], axis=1)
    table = table / (math.sqrt(BINS) * WINDOWS)
    high = table.astype(jnp.bfloat16)
    low = (table - high.astype(np.float64)).astype(jnp.bfloat16)
    return high, low


def fold_kernel(x_ref, all_ref, *quarter_refs):
    lane = lax.broadcasted_iota(jnp.int32, (8, 128), 1)
    mirror = lax.rem(128 - lane, 128)
    for part in range(2):
        for rows in (slice(0, 8), slice(8, 16)):
            for tile in range(HALF // 128):
                piece, offset = divmod(tile * 128, W)
                ahead = x_ref[part, rows, tile * 128 : tile * 128 + 128]
                last = BINS - tile * 128
                back = jnp.take_along_axis(x_ref[part, rows, last - 128 : last], mirror, axis=1)
                edge = last if tile else HALF
                back = jnp.where(lane == 0, x_ref[part, rows, edge : edge + 128] if edge < BINS else 0.0, back)
                columns = slice(offset, offset + 128)
                for row, value in ((part, ahead), (2 + part, back)):
                    all_ref[piece, row, rows, columns] = value
                    if piece >= 2:
                        quarter_refs[piece // 2 - 1][piece % 2, row, rows, columns] = value


def fold(x):
    shape = lambda n: jax.ShapeDtypeStruct((n, 4, CH, W), jnp.float32)
    return pl.pallas_call(
        fold_kernel,
        out_shape=[shape(PARTS)] + [shape(2)] * 3,
        in_specs=[VMEM],
        out_specs=[VMEM] * 4,
        compiler_params=pltpu.CompilerParams(vmem_limit_bytes=12 * 2**20),
    )(x)


def add_parts(ids, x_ref, g_ref, high_ref, low_ref, total, lh, ll):
    lane = lax.broadcasted_iota(jnp.int32, (CH, 128), 1)
    dot = functools.partial(jnp.dot, preferred_element_type=jnp.float32)
    for place in range(4):
        block, bins = ids[place], ids[4 + place]
        first = jnp.logical_and(lane == 0, bins == 0)
        for part in range(2):
            y = [g_ref[place, part, k] for k in range(4)]
            for channel in range(CH):
                x = [x_ref[2 * bins + part, k, channel : channel + 1, :] for k in range(4)]
                ahead = x[0] * y[0] + x[1] * y[1]
                back = x[2] * y[2] + x[3] * y[3]
                even = ahead + back
                odd = (x[1] * y[0] - x[0] * y[1]) + (x[2] * y[3] - x[3] * y[2])
                if part == 0:
                    edge = jnp.where(first, ahead[:, :128] - back[:, :128], odd[:, :128])
                    odd = jnp.concatenate([edge, odd[:, 128:]], axis=1)
                rows = slice(CH * channel, CH * channel + CH)
                for half, value in enumerate((even, odd)):
                    columns = slice((2 * part + half) * W, (2 * part + half + 1) * W)
                    top = value.astype(jnp.bfloat16)
                    lh[rows, columns] = top
                    ll[rows, columns] = (value - top.astype(jnp.float32)).astype(jnp.bfloat16)
        top, rest = lh[...], ll[...]
        high = high_ref[pl.ds(2 * bins, 2)].reshape(4 * W, LAGS)
        low = low_ref[pl.ds(2 * bins, 2)].reshape(4 * W, LAGS)
        got = dot(top, high) + dot(rest, high) + dot(top, low)
        total[block] += got.reshape(CH, CH, LAGS)


def first_kernel(ids, x_ref, g_ref, high_ref, low_ref, total, lh, ll):
    total[...] = jnp.zeros_like(total)
    add_parts(ids, x_ref, g_ref, high_ref, low_ref, total, lh, ll)


def middle_kernel(ids, x_ref, g_ref, high_ref, low_ref, before, total, lh, ll):
    add_parts(ids, x_ref, g_ref, high_ref, low_ref, total, lh, ll)


def last_kernel(ids, x_ref, g_ref, high_ref, low_ref, before, total, keep0, keep1, send0, send1, lh, ll):
    add_parts(ids, x_ref, g_ref, high_ref, low_ref, total, lh, ll)
    core = ids[8]
    for half, (keep, send) in enumerate(((keep0, send0), (keep1, send1))):
        keep[...] = total[2 * core + half]
        send[...] = total[2 * (1 - core) + half]


def correlate(kernel, ids, x, g, high, low, *total):
    here = lambda value: pltpu.with_memory_space_constraint(value, pltpu.VMEM)
    sums = jax.ShapeDtypeStruct((4, CH, CH, LAGS), jnp.float32)
    one = jax.ShapeDtypeStruct((CH, CH, LAGS), jnp.float32)
    outs = [sums] + ([one] * 4 if kernel is last_kernel else [])
    args = [here(value) for value in (x, g, high, low, *total)]
    return pl.pallas_call(
        kernel,
        out_shape=outs,
        in_specs=[pl.BlockSpec(memory_space=pltpu.SMEM)] + [VMEM] * len(args),
        out_specs=[VMEM] * len(outs),
        scratch_shapes=[pltpu.VMEM((CH * CH, 4 * W), jnp.bfloat16)] * 2,
        input_output_aliases={5: 0} if total else {},
        compiler_params=pltpu.CompilerParams(vmem_limit_bytes=16 * 2**20),
        cost_estimate=pl.CostEstimate(
            flops=6 * CH * CH * 2 * HALF * LAGS, bytes_accessed=12 * 2**20, transcendentals=0
        ),
    )(ids, *args)


def place_kernel(core_ref, *refs):
    out_ref = refs[-1]
    core = core_ref[0]
    for half in range(2):
        mine, other = refs[2 * half : 2 * half + 2]
        out_ref[:, 2 * core + half] = mine[...]
        out_ref[:, 2 * (1 - core) + half] = other[...]


def place(core, pieces):
    return pl.pallas_call(
        place_kernel,
        out_shape=jax.ShapeDtypeStruct((CH, 4, CH, LAGS), jnp.float32),
        in_specs=[pl.BlockSpec(memory_space=pltpu.SMEM)] + [VMEM] * len(pieces),
        out_specs=VMEM,
        compiler_params=pltpu.CompilerParams(vmem_limit_bytes=8 * 2**20),
    )(core, *pieces)


def stage_kernel(high_ref, low_ref, high_out, low_out, sems):
    copies = [
        pltpu.make_async_copy(source, target, sems.at[at])
        for at, (source, target) in enumerate(((high_ref, high_out), (low_ref, low_out)))
    ]
    for copy in copies:
        copy.start()
    for copy in copies:
        copy.wait()


def stage(high, low):
    return pl.pallas_call(
        stage_kernel,
        out_shape=[pltpu.VMEM(high.shape, high.dtype), pltpu.VMEM(low.shape, low.dtype)],
        in_specs=[pl.BlockSpec(memory_space=pl.ANY)] * 2,
        out_specs=[VMEM] * 2,
        scratch_shapes=[pltpu.SemaphoreType.DMA((2,))],
        compiler_params=pltpu.CompilerParams(vmem_limit_bytes=2**20),
    )(high, low)


def shards(spectra):
    me = lax.axis_index("chan")
    at_x, at_h, at_z = me // 8, me // 4 % 2, me % 4
    core = lax.axis_index("win") % 2
    over_x = lambda c, d: (c + 8 * d) % 32
    over_z = lambda c, d: c // 4 * 4 + (c + d) % 4

    def send(value, d, even, odd):
        pairs = [(w * 32 + c, w * 32 + (odd if w % 2 else even)(c, d)) for w in range(4) for c in range(32)]
        return lax.ppermute(value, ("win", "chan"), pairs)

    other_core = lambda value: lax.ppermute(value, "win", [(w, w ^ 1) for w in range(4)])
    other_chip = lambda value: lax.ppermute(value, "win", [(w, w ^ 2) for w in range(4)])

    high, low = stage(*(jnp.asarray(t) for t in tables()))
    x, *quarters = fold(spectra[0])
    got = [lax.ppermute(quarters[z - 1], "chan", [(8 * s, 8 * s + z) for s in range(4)]) for z in (1, 2, 3)]
    mine = jnp.where(at_z == 0, x[0:2], got[0] + got[1] + got[2])
    mine, high, low = lax.optimization_barrier((mine, high, low))
    over = lax.ppermute(mine, "chan", [(8 * s + z, 8 * s + 4 + z) for s in range(4) for z in range(4)])
    mine = jnp.where(at_h == 0, mine, over)
    group = jnp.stack([mine] + [send(mine, d, over_z, over_x) for d in SHIFTS])
    groups = [group] + [send(group, d, over_x, over_z) for d in SHIFTS]

    shifts = (0,) + SHIFTS
    kernels = [first_kernel, middle_kernel, middle_kernel, last_kernel]
    total = ()
    for kernel, shift, value in zip(kernels, shifts, groups):
        blocks = [jnp.where(core == 0, at_x - shift, at_x - d) % 4 for d in shifts]
        bins = [jnp.where(core == 0, at_z - d, at_z - shift) % 4 for d in shifts]
        ids = jnp.stack(blocks + bins + [core]).astype(jnp.int32)
        total = correlate(kernel, ids, x, value, high, low, *total)
        total, pieces = total[:1], total[1:]
    placed = []
    for keep, give in zip(pieces[:2], pieces[2:]):
        pair = keep + other_core(give)
        both = pair + other_chip(pair)
        placed += [both, other_core(both)]
    return place(core[None].astype(jnp.int32), placed).reshape(CH, 4 * CH, LAGS)


def solution(mesh):
    return jax.shard_map(
        shards,
        mesh=mesh,
        in_specs=(P("win", None, "chan", None),),
        out_specs=P("chan", None, None),
        check_vma=False,
    )
```

time: 120 us -> 101 us (0.84)
  starting transfers between devices: 51.5 us -> 14.9 us
  waiting for transfers between devices: 27.1 us -> 43.5 us
  local copies, waits for them, and re-layouts: 6.67 us -> 14.3 us
  Pallas kernels: 31.8 us -> 26.7 us
    ppermute x21 -> x6, starting transfers between devices: 29.4 us -> 6.97 us  [send(): return lax.ppermute(value, ('win', 'chan'), pairs)]
    ppermute x21 -> x6, waiting for transfers between devices: 0.87 us -> 18.9 us  [send(): return lax.ppermute(value, ('win', 'chan'), pairs)]
    ppermute x8 -> x4, starting transfers between devices: 15.5 us -> 3.2 us  [shards(): lax.ppermute(value, 'win', [(w, w ^ 1) for w in range(4)])]
    ppermute x1, waiting for transfers between devices: 21.7 us -> 12.1 us  [shards(): lax.ppermute(mine, 'chan', [(8 * s + z, 8 * s + 4 + z) for s in range(4)...]
    unnamed x24 -> x14, local copies, waits for them, and re-layouts: 6.64 us -> 13.9 us
    ppermute x4 -> x2, waiting for transfers between devices: 4.15 us -> 10.2 us  [shards(): lax.ppermute(value, 'win', [(w, w ^ 2) for w in range(4)])]
    pallas_call x1, Pallas kernels: 2.66 us -> 0.22 us  [fold(): pl.pallas_call(fold_kernel, out_shape=[shape(PARTS)] + [shape(2)] * 3, in...]
    ppermute x8 -> x4, waiting for transfers between devices: 0.36 us -> 2.42 us  [shards(): lax.ppermute(value, 'win', [(w, w ^ 1) for w in range(4)])]
  transfers between devices with their start and end apart: 37 -> 16, of which waited for: 7 -> 10; matrix products, arithmetic and copies ran while one was open for 1% -> 0% of each run, Pallas kernels for 22% -> 19%
where the time goes in v2:
time: 101 us
  waiting for transfers between devices  43.5 us (43%)
  Pallas kernels  26.7 us (26%)
  starting transfers between devices  14.9 us (15%)
  local copies, waits for them, and re-layouts  14.3 us (14%)
  other arithmetic  1.35 us (1%)
    pallas_call x4, Pallas kernels, correlate(): pl.pallas_call(kernel, out_shape=outs, in_specs=[pl.BlockSpec(memory_spac...  24.9 us
    ppermute x6, waiting for transfers between devices, send(): return lax.ppermute(value, ('win', 'chan'), pairs)  18.9 us
    unnamed x14, local copies, waits for them, and re-layouts  13.9 us
    ppermute x1, waiting for transfers between devices, shards(): lax.ppermute(mine, 'chan', [(8 * s + z, 8 * s + 4 + z) for s in range(4)...  12.1 us
    ppermute x2, waiting for transfers between devices, shards(): lax.ppermute(value, 'win', [(w, w ^ 2) for w in range(4)])  10.2 us
    ppermute x6, starting transfers between devices, send(): return lax.ppermute(value, ('win', 'chan'), pairs)  6.97 us
    ppermute x4, starting transfers between devices, shards(): lax.ppermute(value, 'win', [(w, w ^ 1) for w in range(4)])  3.2 us
    ppermute x4, waiting for transfers between devices, shards(): lax.ppermute(value, 'win', [(w, w ^ 1) for w in range(4)])  2.42 us
  transfers between devices with their start and end apart: 16, of which 10 were waited for; matrix products, arithmetic and copies ran while one was open for 0% of the time, Pallas kernels for 19%

profile of v2, /device:TPU:25, one launch (start us, length us, event | category | flops | bytes accessed | tf_op | source)
XLA Modules:
  0.0 101.0 jit_solution(8359668875754635654)
XLA Ops:
  0.0 1.2 %copy-done.6 = f32[1,2,16,8192]{3,2,1,0:T(8,128)S(1)} copy-done((f32[1,2,16,8192]{3,2,1,0:T(8,128)S(1)}, f32[1,2,16,8192]{3,2,1,0:T(8,128)}, u32[]{:S(2)}) %copy-start.6) | copy-done | bytes 1048600
  3.5 2.2 %copy-done.4 = bf16[8,1024,256]{2,1,0:T(8,128)(2,1)S(1)} copy-done((bf16[8,1024,256]{2,1,0:T(8,128)(2,1)S(1)}, bf16[8,1024,256]{2,1,0:T(8,128)(2,1)}, u32[]{:S(2)}) %copy-start.4) | copy-done | bytes 4194328
  5.7 2.2 %copy-done.5 = bf16[8,1024,256]{2,1,0:T(8,128)(2,1)S(1)} copy-done((bf16[8,1024,256]{2,1,0:T(8,128)(2,1)S(1)}, bf16[8,1024,256]{2,1,0:T(8,128)(2,1)}, u32[]{:S(2)}) %copy-start.5) | copy-done | bytes 4194328
  8.5 1.9 %copy-done = bf16[8,1024,256]{2,1,0:T(8,128)(2,1)} copy-done((bf16[8,1024,256]{2,1,0:T(8,128)(2,1)}, bf16[8,1024,256]{2,1,0:T(8,128)(2,1)S(1)}, u32[]{:S(2)}) %copy-start) | copy-done | bytes 4194328
  10.4 2.0 %copy-done.2 = bf16[8,1024,256]{2,1,0:T(8,128)(2,1)} copy-done((bf16[8,1024,256]{2,1,0:T(8,128)(2,1)}, bf16[8,1024,256]{2,1,0:T(8,128)(2,1)S(1)}, u32[]{:S(2)}) %copy-start.2) | copy-done | bytes 4194328
  12.6 1.3 %collective-permute-start.3 = (f32[2,4,16,512]{3,2,1,0:T(8,128)S(1)}, f32[2,4,16,512]{3,2,1,0:T(8,128)S(1)}, u32[]{:S(2)}, u32[]{:S(2)}) collective-permute-start(f32[2,4,16,512]{3,2,1,0:T(8,128)S(1)} %add_select_fusion), channel_id=1, source_target_pairs={{0,4},{1,5},{2,6},{3,7},{8,12},{9,13},{10,14},{11,15},{16,20},{17,... | collective-permute-start | bytes 786440 | tf_op jit(solution)/shard_map/ppermute | solution.py:193
  13.9 12.1 %collective-permute-done.3 = f32[2,4,16,512]{3,2,1,0:T(8,128)S(1)} collective-permute-done((f32[2,4,16,512]{3,2,1,0:T(8,128)S(1)}, f32[2,4,16,512]{3,2,1,0:T(8,128)S(1)}, u32[]{:S(2)}, u32[]{:S(2)}) %collective-permute-start.3) | collective-permute-done | bytes 262176 | tf_op jit(solution)/shard_map/ppermute | solution.py:193
  26.0 2.8 %collective-permute-start.6 = (f32[2,4,16,512]{3,2,1,0:T(8,128)S(1)}, f32[2,4,16,512]{3,2,1,0:T(8,128)S(1)}, u32[]{:S(2)}, u32[]{:S(2)}) collective-permute-start(f32[2,4,16,512]{3,2,1,0:T(8,128)S(1)} %broadcast_select_fusion), channel_id=1, source_target_pairs={{0,2},{1,3},{2,0},{3,1},{4,6},{5,7},{6,4},{7,5},{8,10},{9,11},{10,... | collective-permute-start | bytes 786440 | tf_op jit(solution)/shard_map/ppermute | solution.py:183
  30.3 2.8 %collective-permute-done.6 = f32[2,4,16,512]{3,2,1,0:T(8,128)S(1)} collective-permute-done((f32[2,4,16,512]{3,2,1,0:T(8,128)S(1)}, f32[2,4,16,512]{3,2,1,0:T(8,128)S(1)}, u32[]{:S(2)}, u32[]{:S(2)}) %collective-permute-start.6) | collective-permute-done | bytes 262176 | tf_op jit(solution)/shard_map/ppermute | solution.py:183
  33.1 2.9 %collective-permute-done.5 = f32[2,4,16,512]{3,2,1,0:T(8,128)S(1)} collective-permute-done((f32[2,4,16,512]{3,2,1,0:T(8,128)S(1)}, f32[2,4,16,512]{3,2,1,0:T(8,128)S(1)}, u32[]{:S(2)}, u32[]{:S(2)}) %collective-permute-start.5) | collective-permute-done | bytes 262176 | tf_op jit(solution)/shard_map/ppermute | solution.py:183
  36.4 1.1 %pad_maximum_fusion.g_ref = f32[4,2,4,16,512]{4,3,2,1,0:T(8,128)} fusion(f32[1,2,4,16,512]{4,3,2,1,0:T(8,128)S(1)} %bitcast.41, f32[1,2,4,16,512]{4,3,2,1,0:T(8,128)S(1)} %bitcast.42, f32[1,2,4,16,512]{4,3,2,1,0:T(8,128)S(1)} %bitcast.43, f32[1,2,4,16,512]{4,3,2,1,0:T(8,128)S(1)} %bitcast.40), kind=kLoop, calls=%fused_computation | loop fusion | flops 786432 | bytes 2097152 | tf_op jit(solution)/shard_map/stack | solution.py:195
  37.5 2.7 %collective-permute-start.8 = (f32[4,2,4,16,512]{4,3,2,1,0:T(8,128)}, f32[4,2,4,16,512]{4,3,2,1,0:T(8,128)S(1)}, u32[]{:S(2)}, u32[]{:S(2)}) collective-permute-start(f32[4,2,4,16,512]{4,3,2,1,0:T(8,128)} %pad_maximum_fusion.g_ref), channel_id=1, source_target_pairs={{0,24},{1,25},{2,26},{3,27},{4,28},{5,29},{6,30},{7,31},{8,0},{9,1... | collective-permute-start | bytes 3145736 | tf_op jit(solution)/shard_map/ppermute | solution.py:183
  40.5 2.2 %copy-done.1 = bf16[8,1024,256]{2,1,0:T(8,128)(2,1)S(1)} copy-done((bf16[8,1024,256]{2,1,0:T(8,128)(2,1)S(1)}, bf16[8,1024,256]{2,1,0:T(8,128)(2,1)}, u32[]{:S(2)}) %copy-start.1) | copy-done | bytes 4194328
  42.7 2.2 %copy-done.3 = bf16[8,1024,256]{2,1,0:T(8,128)(2,1)S(1)} copy-done((bf16[8,1024,256]{2,1,0:T(8,128)(2,1)S(1)}, bf16[8,1024,256]{2,1,0:T(8,128)(2,1)}, u32[]{:S(2)}) %copy-start.3) | copy-done | bytes 4194328
  44.9 6.5 %shard_map.39.before = f32[4,16,16,256]{3,2,1,0:T(8,128)S(1)} custom-call(s32[9]{0:T(128)S(1)} %stack.167.ids, f32[8,4,16,512]{3,2,1,0:T(8,128)S(1)} %get-tuple-element.18.x_ref, f32[4,2,4,16,512]{4,3,2,1,0:T(8,128)} %pad_maximum_fusion.g_ref, bf16[8,1024,256]{2,1,0:T(8,128)(2,1)S(1)} %copy-done.1, bf16[8,1024,256]{2,1,0:T(8,128)(2,1)S(1)} %copy-done.3), custom_call_target="tpu_custom_call" | custom-call | flops 3221225472 | bytes 12582912 | tf_op jit(solution)/shard_map/pallas_call | solution.py:119
  51.5 12.7 %collective-permute-done.9.g_ref = f32[4,2,4,16,512]{4,3,2,1,0:T(8,128)S(1)} collective-permute-done((f32[4,2,4,16,512]{4,3,2,1,0:T(8,128)}, f32[4,2,4,16,512]{4,3,2,1,0:T(8,128)S(1)}, u32[]{:S(2)}, u32[]{:S(2)}) %collective-permute-start.9) | collective-permute-done | bytes 1048608 | tf_op jit(solution)/shard_map/ppermute | solution.py:183
  64.2 5.8 %shard_map.40.before = f32[4,16,16,256]{3,2,1,0:T(8,128)S(1)} custom-call(s32[9]{0:T(128)S(1)} %stack.158.ids, f32[8,4,16,512]{3,2,1,0:T(8,128)S(1)} %get-tuple-element.18.x_ref, f32[4,2,4,16,512]{4,3,2,1,0:T(8,128)S(1)} %collective-permute-done.9.g_ref, bf16[8,1024,256]{2,1,0:T(8,128)(2,1)S(1)} %copy-done.1, ...), custom_call_target="tpu_custom_call", output_to_operand_aliasing={{}: (5, {})} | custom-call | flops 3221225472 | bytes 12582912 | tf_op jit(solution)/shard_map/pallas_call | solution.py:119
  70.0 6.0 %shard_map.41.before = f32[4,16,16,256]{3,2,1,0:T(8,128)S(1)} custom-call(s32[9]{0:T(128)S(1)} %stack.149.ids, f32[8,4,16,512]{3,2,1,0:T(8,128)S(1)} %get-tuple-element.18.x_ref, f32[4,2,4,16,512]{4,3,2,1,0:T(8,128)S(1)} %collective-permute-done.8.g_ref, bf16[8,1024,256]{2,1,0:T(8,128)(2,1)S(1)} %copy-done.1, ...), custom_call_target="tpu_custom_call", output_to_operand_aliasing={{}: (5, {})} | custom-call | flops 3221225472 | bytes 12582912 | tf_op jit(solution)/shard_map/pallas_call | solution.py:119
  76.1 6.5 %shard_map.42 = (f32[4,16,16,256]{3,2,1,0:T(8,128)S(1)}, f32[16,16,256]{2,1,0:T(8,128)S(1)}, f32[16,16,256]{2,1,0:T(8,128)S(1)}, f32[16,16,256]{2,1,0:T(8,128)S(1)}, f32[16,16,256]{2,1,0:T(8,128)S(1)}) custom-call(s32[9]{0:T(128)S(1)} %stack.135.ids, f32[8,4,16,512]{3,2,1,0:T(8,128)S(1)} %get-tuple-element.18.x_ref, ...), custom_call_target="tpu_custom_call", output_to_operand_aliasing={{0}: (5, {})} | custom-call | flops 3221225472 | bytes 12582912 | tf_op jit(solution)/shard_map/pallas_call | solution.py:119
  84.7 1.3 %collective-permute-start.14 = (f32[16,16,256]{2,1,0:T(8,128)S(1)}, f32[16,16,256]{2,1,0:T(8,128)S(1)}, u32[]{:S(2)}, u32[]{:S(2)}) collective-permute-start(f32[16,16,256]{2,1,0:T(8,128)S(1)} %add.171), channel_id=1, source_target_pairs={{0,64},{32,96},{64,0},{96,32},{1,65},{33,97},{65,1},{97,33},{2,66}... | collective-permute-start | bytes 786440 | tf_op jit(solution)/shard_map/ppermute | solution.py:186
  85.9 6.2 %collective-permute-done.11 = f32[16,16,256]{2,1,0:T(8,128)S(1)} collective-permute-done((f32[16,16,256]{2,1,0:T(8,128)S(1)}, f32[16,16,256]{2,1,0:T(8,128)S(1)}, u32[]{:S(2)}, u32[]{:S(2)}) %collective-permute-start.11) | collective-permute-done | bytes 262176 | tf_op jit(solution)/shard_map/ppermute | solution.py:186
  92.2 1.6 %collective-permute-start.12 = (f32[16,16,256]{2,1,0:T(8,128)S(1)}, f32[16,16,256]{2,1,0:T(8,128)S(1)}, u32[]{:S(2)}, u32[]{:S(2)}) collective-permute-start(f32[16,16,256]{2,1,0:T(8,128)S(1)} %add.170.refs_0_), channel_id=1, source_target_pairs={{0,32},{32,0},{64,96},{96,64},{1,33},{33,1},{65,97},{97,65},{2,34}... | collective-permute-start | bytes 786440 | tf_op jit(solution)/shard_map/ppermute | solution.py:185
  93.8 4.0 %collective-permute-done.14 = f32[16,16,256]{2,1,0:T(8,128)S(1)} collective-permute-done((f32[16,16,256]{2,1,0:T(8,128)S(1)}, f32[16,16,256]{2,1,0:T(8,128)S(1)}, u32[]{:S(2)}, u32[]{:S(2)}) %collective-permute-start.14) | collective-permute-done | bytes 262176 | tf_op jit(solution)/shard_map/ppermute | solution.py:186
  98.8 1.2 %collective-permute-done.15.refs_3_ = f32[16,16,256]{2,1,0:T(8,128)S(1)} collective-permute-done((f32[16,16,256]{2,1,0:T(8,128)S(1)}, f32[16,16,256]{2,1,0:T(8,128)S(1)}, u32[]{:S(2)}, u32[]{:S(2)}) %collective-permute-start.15) | collective-permute-done | bytes 262176 | tf_op jit(solution)/shard_map/ppermute | solution.py:185
  (40 shorter events, 9.3 us)
Async XLA Ops:
  0.0 1.2 %copy-start.6 = (f32[1,2,16,8192]{3,2,1,0:T(8,128)S(1)}, f32[1,2,16,8192]{3,2,1,0:T(8,128)}, u32[]{:S(2)}) copy-start(f32[1,2,16,8192]{3,2,1,0:T(8,128)} %param.3) | copy-start | bytes 3145732
  1.5 11.0 %collective-permute-start = (f32[2,4,16,512]{3,2,1,0:T(8,128)S(1)}, f32[2,4,16,512]{3,2,1,0:T(8,128)S(1)}, u32[]{:S(2)}, u32[]{:S(2)}) collective-permute-start(f32[2,4,16,512]{3,2,1,0:T(8,128)S(1)} %get-tuple-element.19), channel_id=1, source_target_pairs={{0,1},{8,9},{16,17},{24,25},{32,33},{40,41},{48,49},{56,57},{64,65... | collective-permute-start | bytes 786440 | tf_op jit(solution)/shard_map/ppermute | solution.py:190
  2.1 10.3 %collective-permute-start.1 = (f32[2,4,16,512]{3,2,1,0:T(8,128)S(1)}, f32[2,4,16,512]{3,2,1,0:T(8,128)S(1)}, u32[]{:S(2)}, u32[]{:S(2)}) collective-permute-start(f32[2,4,16,512]{3,2,1,0:T(8,128)S(1)} %get-tuple-element.20), channel_id=1, source_target_pairs={{0,2},{8,10},{16,18},{24,26},{32,34},{40,42},{48,50},{56,58},{64,6... | collective-permute-start | bytes 786440 | tf_op jit(solution)/shard_map/ppermute | solution.py:190
  2.8 9.6 %collective-permute-start.2 = (f32[2,4,16,512]{3,2,1,0:T(8,128)S(1)}, f32[2,4,16,512]{3,2,1,0:T(8,128)S(1)}, u32[]{:S(2)}, u32[]{:S(2)}) collective-permute-start(f32[2,4,16,512]{3,2,1,0:T(8,128)S(1)} %get-tuple-element.21), channel_id=1, source_target_pairs={{0,3},{8,11},{16,19},{24,27},{32,35},{40,43},{48,51},{56,59},{64,6... | collective-permute-start | bytes 786440 | tf_op jit(solution)/shard_map/ppermute | solution.py:190
  3.5 2.2 %copy-start.4 = (bf16[8,1024,256]{2,1,0:T(8,128)(2,1)S(1)}, bf16[8,1024,256]{2,1,0:T(8,128)(2,1)}, u32[]{:S(2)}) copy-start(bf16[8,1024,256]{2,1,0:T(8,128)(2,1)} %constant.200.clone.low_ref) | copy-start | bytes 12582916
  5.7 2.2 %copy-start.5 = (bf16[8,1024,256]{2,1,0:T(8,128)(2,1)S(1)}, bf16[8,1024,256]{2,1,0:T(8,128)(2,1)}, u32[]{:S(2)}) copy-start(bf16[8,1024,256]{2,1,0:T(8,128)(2,1)} %constant.199.clone.high_ref) | copy-start | bytes 12582916
  8.5 1.9 %copy-start = (bf16[8,1024,256]{2,1,0:T(8,128)(2,1)}, bf16[8,1024,256]{2,1,0:T(8,128)(2,1)S(1)}, u32[]{:S(2)}) copy-start(bf16[8,1024,256]{2,1,0:T(8,128)(2,1)S(1)} %get-tuple-element.25.high_ref) | copy-start | bytes 12582916
  10.4 2.0 %copy-start.2 = (bf16[8,1024,256]{2,1,0:T(8,128)(2,1)}, bf16[8,1024,256]{2,1,0:T(8,128)(2,1)S(1)}, u32[]{:S(2)}) copy-start(bf16[8,1024,256]{2,1,0:T(8,128)(2,1)S(1)} %get-tuple-element.26.low_ref) | copy-start | bytes 12582916
  12.6 13.4 %collective-permute-start.3 = (f32[2,4,16,512]{3,2,1,0:T(8,128)S(1)}, f32[2,4,16,512]{3,2,1,0:T(8,128)S(1)}, u32[]{:S(2)}, u32[]{:S(2)}) collective-permute-start(f32[2,4,16,512]{3,2,1,0:T(8,128)S(1)} %add_select_fusion), channel_id=1, source_target_pairs={{0,4},{1,5},{2,6},{3,7},{8,12},{9,13},{10,14},{11,15},{16,20},{17,... | collective-permute-start | bytes 786440 | tf_op jit(solution)/shard_map/ppermute | solution.py:193
  26.0 7.1 %collective-permute-start.6 = (f32[2,4,16,512]{3,2,1,0:T(8,128)S(1)}, f32[2,4,16,512]{3,2,1,0:T(8,128)S(1)}, u32[]{:S(2)}, u32[]{:S(2)}) collective-permute-start(f32[2,4,16,512]{3,2,1,0:T(8,128)S(1)} %broadcast_select_fusion), channel_id=1, source_target_pairs={{0,2},{1,3},{2,0},{3,1},{4,6},{5,7},{6,4},{7,5},{8,10},{9,11},{10,... | collective-permute-start | bytes 786440 | tf_op jit(solution)/shard_map/ppermute | solution.py:183
  28.8 7.2 %collective-permute-start.5 = (f32[2,4,16,512]{3,2,1,0:T(8,128)S(1)}, f32[2,4,16,512]{3,2,1,0:T(8,128)S(1)}, u32[]{:S(2)}, u32[]{:S(2)}) collective-permute-start(f32[2,4,16,512]{3,2,1,0:T(8,128)S(1)} %broadcast_select_fusion), channel_id=1, source_target_pairs={{0,3},{1,0},{2,1},{3,2},{4,7},{5,4},{6,5},{7,6},{8,11},{9,8},{10,9... | collective-permute-start | bytes 786440 | tf_op jit(solution)/shard_map/ppermute | solution.py:183
  29.7 6.7 %collective-permute-start.4 = (f32[2,4,16,512]{3,2,1,0:T(8,128)S(1)}, f32[2,4,16,512]{3,2,1,0:T(8,128)S(1)}, u32[]{:S(2)}, u32[]{:S(2)}) collective-permute-start(f32[2,4,16,512]{3,2,1,0:T(8,128)S(1)} %broadcast_select_fusion), channel_id=1, source_target_pairs={{0,1},{1,2},{2,3},{3,0},{4,5},{5,6},{6,7},{7,4},{8,9},{9,10},{10,1... | collective-permute-start | bytes 786440 | tf_op jit(solution)/shard_map/ppermute | solution.py:183
  37.5 26.7 %collective-permute-start.9 = (f32[4,2,4,16,512]{4,3,2,1,0:T(8,128)}, f32[4,2,4,16,512]{4,3,2,1,0:T(8,128)S(1)}, u32[]{:S(2)}, u32[]{:S(2)}) collective-permute-start(f32[4,2,4,16,512]{4,3,2,1,0:T(8,128)} %pad_maximum_fusion.g_ref), channel_id=1, source_target_pairs={{0,8},{1,9},{2,10},{3,11},{4,12},{5,13},{6,14},{7,15},{8,16},{9,17... | collective-permute-start | bytes 3145736 | tf_op jit(solution)/shard_map/ppermute | solution.py:183
  37.5 32.5 %collective-permute-start.8 = (f32[4,2,4,16,512]{4,3,2,1,0:T(8,128)}, f32[4,2,4,16,512]{4,3,2,1,0:T(8,128)S(1)}, u32[]{:S(2)}, u32[]{:S(2)}) collective-permute-start(f32[4,2,4,16,512]{4,3,2,1,0:T(8,128)} %pad_maximum_fusion.g_ref), channel_id=1, source_target_pairs={{0,24},{1,25},{2,26},{3,27},{4,28},{5,29},{6,30},{7,31},{8,0},{9,1... | collective-permute-start | bytes 3145736 | tf_op jit(solution)/shard_map/ppermute | solution.py:183
  40.2 35.9 %collective-permute-start.7 = (f32[4,2,4,16,512]{4,3,2,1,0:T(8,128)}, f32[4,2,4,16,512]{4,3,2,1,0:T(8,128)}, u32[]{:S(2)}, u32[]{:S(2)}) collective-permute-start(f32[4,2,4,16,512]{4,3,2,1,0:T(8,128)} %pad_maximum_fusion.g_ref), channel_id=1, source_target_pairs={{0,16},{1,17},{2,18},{3,19},{4,20},{5,21},{6,22},{7,23},{8,24},{9,... | collective-permute-start | bytes 3145736 | tf_op jit(solution)/shard_map/ppermute | solution.py:183
  40.5 2.2 %copy-start.1 = (bf16[8,1024,256]{2,1,0:T(8,128)(2,1)S(1)}, bf16[8,1024,256]{2,1,0:T(8,128)(2,1)}, u32[]{:S(2)}) copy-start(bf16[8,1024,256]{2,1,0:T(8,128)(2,1)} %copy-done) | copy-start | bytes 12582916
  42.7 2.2 %copy-start.3 = (bf16[8,1024,256]{2,1,0:T(8,128)(2,1)S(1)}, bf16[8,1024,256]{2,1,0:T(8,128)(2,1)}, u32[]{:S(2)}) copy-start(bf16[8,1024,256]{2,1,0:T(8,128)(2,1)} %copy-done.2) | copy-start | bytes 12582916
  82.6 1.6 %collective-permute-start.10 = (f32[16,16,256]{2,1,0:T(8,128)S(1)}, f32[16,16,256]{2,1,0:T(8,128)S(1)}, u32[]{:S(2)}, u32[]{:S(2)}) collective-permute-start(f32[16,16,256]{2,1,0:T(8,128)S(1)} %get-tuple-element.28), channel_id=1, source_target_pairs={{0,32},{32,0},{64,96},{96,64},{1,33},{33,1},{65,97},{97,65},{2,34}... | collective-permute-start | bytes 786440 | tf_op jit(solution)/shard_map/ppermute | solution.py:185
  82.7 1.9 %collective-permute-start.13 = (f32[16,16,256]{2,1,0:T(8,128)S(1)}, f32[16,16,256]{2,1,0:T(8,128)S(1)}, u32[]{:S(2)}, u32[]{:S(2)}) collective-permute-start(f32[16,16,256]{2,1,0:T(8,128)S(1)} %get-tuple-element.30), channel_id=1, source_target_pairs={{0,32},{32,0},{64,96},{96,64},{1,33},{33,1},{65,97},{97,65},{2,34}... | collective-permute-start | bytes 786440 | tf_op jit(solution)/shard_map/ppermute | solution.py:185
  84.3 7.8 %collective-permute-start.11 = (f32[16,16,256]{2,1,0:T(8,128)S(1)}, f32[16,16,256]{2,1,0:T(8,128)S(1)}, u32[]{:S(2)}, u32[]{:S(2)}) collective-permute-start(f32[16,16,256]{2,1,0:T(8,128)S(1)} %add.169), channel_id=1, source_target_pairs={{0,64},{32,96},{64,0},{96,32},{1,65},{33,97},{65,1},{97,33},{2,66}... | collective-permute-start | bytes 786440 | tf_op jit(solution)/shard_map/ppermute | solution.py:186
  84.7 13.1 %collective-permute-start.14 = (f32[16,16,256]{2,1,0:T(8,128)S(1)}, f32[16,16,256]{2,1,0:T(8,128)S(1)}, u32[]{:S(2)}, u32[]{:S(2)}) collective-permute-start(f32[16,16,256]{2,1,0:T(8,128)S(1)} %add.171), channel_id=1, source_target_pairs={{0,64},{32,96},{64,0},{96,32},{1,65},{33,97},{65,1},{97,33},{2,66}... | collective-permute-start | bytes 786440 | tf_op jit(solution)/shard_map/ppermute | solution.py:186
  92.2 6.7 %collective-permute-start.12 = (f32[16,16,256]{2,1,0:T(8,128)S(1)}, f32[16,16,256]{2,1,0:T(8,128)S(1)}, u32[]{:S(2)}, u32[]{:S(2)}) collective-permute-start(f32[16,16,256]{2,1,0:T(8,128)S(1)} %add.170.refs_0_), channel_id=1, source_target_pairs={{0,32},{32,0},{64,96},{96,64},{1,33},{33,1},{65,97},{97,65},{2,34}... | collective-permute-start | bytes 786440 | tf_op jit(solution)/shard_map/ppermute | solution.py:185
  97.8 2.2 %collective-permute-start.15 = (f32[16,16,256]{2,1,0:T(8,128)S(1)}, f32[16,16,256]{2,1,0:T(8,128)S(1)}, u32[]{:S(2)}, u32[]{:S(2)}) collective-permute-start(f32[16,16,256]{2,1,0:T(8,128)S(1)} %add.172.refs_2_), channel_id=1, source_target_pairs={{0,32},{32,0},{64,96},{96,64},{1,33},{33,1},{65,97},{97,65},{2,34}... | collective-permute-start | bytes 786440 | tf_op jit(solution)/shard_map/ppermute | solution.py:185

commit v3 on v2

v3 whole, which is shorter than its diff:
```python
import functools
import math

import jax
import jax.numpy as jnp
import numpy as np
from jax import lax
from jax.experimental import pallas as pl
from jax.experimental.pallas import tpu as pltpu
from jax.sharding import PartitionSpec as P

LAGS = 256
BINS = 8192
HALF = BINS // 2
CH = 16
WINDOWS = 4
PARTS = 8
W = HALF // PARTS
VMEM = pl.BlockSpec(memory_space=pltpu.VMEM)
HALVES = ((1, 3), (0, 2))


def tables():
    lag = np.arange(LAGS) - LAGS // 2
    turns = (np.arange(HALF)[:, None] * lag[None, :]) % BINS
    angle = 2.0 * np.pi * turns / BINS
    cosine, sine = np.cos(angle), -np.sin(angle)
    cosine[0], sine[0] = lag % 2 == 0, lag % 2 != 0
    table = np.concatenate([cosine.reshape(PARTS, W, LAGS), sine.reshape(PARTS, W, LAGS)], axis=1)
    table = table / (math.sqrt(BINS) * WINDOWS)
    high = table.astype(jnp.bfloat16)
    low = (table - high.astype(np.float64)).astype(jnp.bfloat16)
    return high, low


def fold_kernel(x_ref, all_ref, *quarter_refs):
    lane = lax.broadcasted_iota(jnp.int32, (8, 128), 1)
    mirror = lax.rem(128 - lane, 128)
    for part in range(2):
        for rows in (slice(0, 8), slice(8, 16)):
            for tile in range(HALF // 128):
                piece, offset = divmod(tile * 128, W)
                ahead = x_ref[part, rows, tile * 128 : tile * 128 + 128]
                last = BINS - tile * 128
                back = jnp.take_along_axis(x_ref[part, rows, last - 128 : last], mirror, axis=1)
                edge = last if tile else HALF
                back = jnp.where(lane == 0, x_ref[part, rows, edge : edge + 128] if edge < BINS else 0.0, back)
                columns = slice(offset, offset + 128)
                for row, value in ((part, ahead), (2 + part, back)):
                    all_ref[piece, row, rows, columns] = value
                    if piece >= 2:
                        quarter_refs[piece // 2 - 1][piece % 2, row, rows, columns] = value


def fold(x):
    shape = lambda n: jax.ShapeDtypeStruct((n, 4, CH, W), jnp.float32)
    return pl.pallas_call(
        fold_kernel,
        out_shape=[shape(PARTS)] + [shape(2)] * 3,
        in_specs=[VMEM],
        out_specs=[VMEM] * 4,
        compiler_params=pltpu.CompilerParams(vmem_limit_bytes=12 * 2**20),
    )(x)


def position():
    chan = lax.axis_index("chan")
    return chan // 8, chan % 4, lax.axis_index("win") % 2


def add_parts(sources, x_ref, high_ref, low_ref, total, lh, ll):
    at_x, at_z, core = position()
    lane = lax.broadcasted_iota(jnp.int32, (CH, 128), 1)
    dot = functools.partial(jnp.dot, preferred_element_type=jnp.float32)
    for g_ref, far, nears in sources:
        for place, near in enumerate(nears):
            block = (at_x + 4 - jnp.where(core == 0, far, near)) % 4
            bins = (at_z + 4 - jnp.where(core == 0, near, far)) % 4
            first = jnp.logical_and(lane == 0, bins == 0)
            for part in range(2):
                y = [g_ref[place, part, k] for k in range(4)]
                for channel in range(CH):
                    x = [x_ref[2 * bins + part, k, channel : channel + 1, :] for k in range(4)]
                    ahead = x[0] * y[0] + x[1] * y[1]
                    back = x[2] * y[2] + x[3] * y[3]
                    even = ahead + back
                    odd = (x[1] * y[0] - x[0] * y[1]) + (x[2] * y[3] - x[3] * y[2])
                    if part == 0:
                        edge = jnp.where(first, ahead[:, :128] - back[:, :128], odd[:, :128])
                        odd = jnp.concatenate([edge, odd[:, 128:]], axis=1)
                    rows = slice(CH * channel, CH * channel + CH)
                    for half, value in enumerate((even, odd)):
                        columns = slice((2 * part + half) * W, (2 * part + half + 1) * W)
                        top = value.astype(jnp.bfloat16)
                        lh[rows, columns] = top
                        ll[rows, columns] = (value - top.astype(jnp.float32)).astype(jnp.bfloat16)
            top = lh[...]
            high = high_ref[pl.ds(2 * bins, 2)].reshape(4 * W, LAGS)
            low = low_ref[pl.ds(2 * bins, 2)].reshape(4 * W, LAGS)
            both = dot(jnp.concatenate([top, ll[...]], axis=0), high)
            got = both[: CH * CH] + both[CH * CH :] + dot(top, low)
            total[block] += got.reshape(CH, CH, LAGS)


def correlate_kernel(steps, started, finished, x_ref, high_ref, low_ref, *refs):
    n = len(steps)
    total = refs[n + started]
    if not started:
        total[...] = jnp.zeros_like(total)
    sources = [(ref, far, nears) for ref, (far, nears) in zip(refs[:n], steps)]
    add_parts(sources, x_ref, high_ref, low_ref, total, *refs[-2:])
    if finished is not None:
        at_x, _, core = position()
        keep, send = refs[n + started + 1 : n + started + 3]
        here, there = finished
        keep[...] = total[(at_x + jnp.where(core == 0, here, there)) % 4]
        send[...] = total[(at_x + jnp.where(core == 0, there, here)) % 4]


def correlate(steps, values, tables, total=None, finished=None):
    here = lambda value: pltpu.with_memory_space_constraint(value, pltpu.VMEM)
    started = total is not None
    args = [here(value) for value in (*tables, *values, *([total] if started else []))]
    sums = jax.ShapeDtypeStruct((4, CH, CH, LAGS), jnp.float32)
    one = jax.ShapeDtypeStruct((CH, CH, LAGS), jnp.float32)
    outs = [sums] + ([one] * 2 if finished is not None else [])
    pairs = 2 * len(steps)
    return pl.pallas_call(
        functools.partial(correlate_kernel, steps, started, finished),
        out_shape=outs,
        in_specs=[VMEM] * len(args),
        out_specs=[VMEM] * len(outs),
        scratch_shapes=[pltpu.VMEM((CH * CH, 4 * W), jnp.bfloat16)] * 2,
        input_output_aliases={len(args) - 1: 0} if started else {},
        compiler_params=pltpu.CompilerParams(vmem_limit_bytes=16 * 2**20),
        cost_estimate=pl.CostEstimate(
            flops=6 * CH * CH * 4 * W * LAGS * pairs, bytes_accessed=3 * 2**20 * pairs, transcendentals=0
        ),
    )(*args)


def place_kernel(*refs):
    out_ref = refs[-1]
    at_x, _, core = position()
    for pair, (here, there) in enumerate(HALVES):
        mine, other = refs[2 * pair : 2 * pair + 2]
        out_ref[:, (at_x + jnp.where(core == 0, here, there)) % 4] = mine[...]
        out_ref[:, (at_x + jnp.where(core == 0, there, here)) % 4] = other[...]


def place(pieces):
    return pl.pallas_call(
        place_kernel,
        out_shape=jax.ShapeDtypeStruct((CH, 4, CH, LAGS), jnp.float32),
        in_specs=[VMEM] * len(pieces),
        out_specs=VMEM,
        compiler_params=pltpu.CompilerParams(vmem_limit_bytes=8 * 2**20),
    )(*pieces)


def stage_kernel(high_ref, low_ref, high_out, low_out, sems):
    copies = [
        pltpu.make_async_copy(source, target, sems.at[at])
        for at, (source, target) in enumerate(((high_ref, high_out), (low_ref, low_out)))
    ]
    for copy in copies:
        copy.start()
    for copy in copies:
        copy.wait()


def stage(high, low):
    return pl.pallas_call(
        stage_kernel,
        out_shape=[pltpu.VMEM(high.shape, high.dtype), pltpu.VMEM(low.shape, low.dtype)],
        in_specs=[pl.BlockSpec(memory_space=pl.ANY)] * 2,
        out_specs=[VMEM] * 2,
        scratch_shapes=[pltpu.SemaphoreType.DMA((2,))],
        compiler_params=pltpu.CompilerParams(vmem_limit_bytes=2**20),
    )(high, low)


def shards(spectra):
    me = lax.axis_index("chan")
    at_start, at_near = me % 4 == 0, me // 4 % 2 == 0
    spectra, at_start, at_near = lax.optimization_barrier((spectra, at_start, at_near))
    over_x = lambda c, d: (c + 8 * d) % 32
    over_z = lambda c, d: c // 4 * 4 + (c + d) % 4

    def send(value, d, even, odd):
        pairs = [(w * 32 + c, w * 32 + (odd if w % 2 else even)(c, d)) for w in range(4) for c in range(32)]
        return lax.ppermute(value, ("win", "chan"), pairs)

    other_core = lambda value: lax.ppermute(value, "win", [(w, w ^ 1) for w in range(4)])
    other_chip = lambda value: lax.ppermute(value, "win", [(w, w ^ 2) for w in range(4)])

    high, low = stage(*(jnp.asarray(t) for t in tables()))
    x, *quarters = fold(spectra[0])
    got = [lax.ppermute(quarters[z - 1], "chan", [(8 * s, 8 * s + z) for s in range(4)]) for z in (1, 2, 3)]
    mine = jnp.where(at_start, x[0:2], got[0] + got[1] + got[2])
    mine, high, low = lax.optimization_barrier((mine, high, low))
    over = lax.ppermute(mine, "chan", [(8 * s + z, 8 * s + 4 + z) for s in range(4) for z in range(4)])
    mine = jnp.where(at_near, mine, over)
    came = {d: send(mine, d, over_z, over_x) for d in (1, -1, 2)}
    first = jnp.stack([came[1], came[-1]])
    second = jnp.stack([mine, came[2]])
    firsts, seconds = {0: first}, {0: second}
    for group, value in ((firsts, first), (seconds, second)):
        for d in (1, -1):
            group[d] = send(value, d, over_x, over_z)
    firsts[2] = send(firsts[1], 1, over_x, over_z)
    seconds[2] = send(seconds[-1], -1, over_x, over_z)

    near, ends = (1, -1), (0, 2)
    tabled = (x, high, low)
    total = correlate([(0, near), (0, ends)], [firsts[0], seconds[0]], tabled)[0]
    total = correlate([(1, near), (-1, near)], [firsts[1], firsts[-1]], tabled, total)[0]
    total = correlate([(1, ends), (-1, ends)], [seconds[1], seconds[-1]], tabled, total)[0]
    total, *pieces = correlate([(2, near)], [firsts[2]], tabled, total, HALVES[0])
    total, *others = correlate([(2, ends)], [seconds[2]], tabled, total, HALVES[1])
    placed = []
    for keep, give in (pieces, others):
        pair = keep + other_core(give)
        both = pair + other_chip(pair)
        placed += [both, other_core(both)]
    return place(placed).reshape(CH, 4 * CH, LAGS)


def solution(mesh):
    return jax.shard_map(
        shards,
        mesh=mesh,
        in_specs=(P("win", None, "chan", None),),
        out_specs=P("chan", None, None),
        check_vma=False,
    )
```

time: 101 us -> 86.1 us (0.85)
  waiting for transfers between devices: 43.5 us -> 33.5 us
  starting transfers between devices: 14.9 us -> 24.7 us
  local copies, waits for them, and re-layouts: 14.3 us -> 5.6 us
  Pallas kernels: 26.7 us -> 21.1 us
    ppermute x6 -> x9, waiting for transfers between devices: 18.9 us -> 8.57 us  [send(): return lax.ppermute(value, ('win', 'chan'), pairs)]
    unnamed x14 -> x6, local copies, waits for them, and re-layouts: 13.9 us -> 5.6 us
    pallas_call x4 -> x5, Pallas kernels: 24.9 us -> 19.2 us  [correlate(): pl.pallas_call(functools.partial(correlate_kernel, steps, started, finish...]
    ppermute x4, starting transfers between devices: 3.2 us -> 8.83 us  [shards(): lax.ppermute(value, 'win', [(w, w ^ 1) for w in range(4)])]
    ppermute x6 -> x9, starting transfers between devices: 6.97 us -> 11.1 us  [send(): return lax.ppermute(value, ('win', 'chan'), pairs)]
  transfers between devices with their start and end apart: 16 -> 19, of which waited for: 10 -> 9; matrix products, arithmetic and copies ran while one was open for 0% -> 0% of each run, Pallas kernels for 19% -> 20%
where the time goes in v3:
time: 86.1 us; the launch traced here: 85.5 us
  waiting for transfers between devices  33.5 us (39%)
  starting transfers between devices  24.7 us (29%)
  Pallas kernels  21.1 us (25%)
  local copies, waits for them, and re-layouts  5.6 us (7%)
    pallas_call x5, Pallas kernels, correlate(): pl.pallas_call(functools.partial(correlate_kernel, steps, started, finish...  19.2 us
    ppermute x1, waiting for transfers between devices, shards(): lax.ppermute(mine, 'chan', [(8 * s + z, 8 * s + 4 + z) for s in range(4)...  13.1 us
    ppermute x9, starting transfers between devices, send(): return lax.ppermute(value, ('win', 'chan'), pairs)  11.1 us
    ppermute x2, waiting for transfers between devices, shards(): lax.ppermute(value, 'win', [(w, w ^ 2) for w in range(4)])  9.42 us
    ppermute x4, starting transfers between devices, shards(): lax.ppermute(value, 'win', [(w, w ^ 1) for w in range(4)])  8.83 us
    ppermute x9, waiting for transfers between devices, send(): return lax.ppermute(value, ('win', 'chan'), pairs)  8.57 us
    unnamed x6, local copies, waits for them, and re-layouts  5.6 us
    ppermute x4, waiting for transfers between devices, shards(): lax.ppermute(value, 'win', [(w, w ^ 1) for w in range(4)])  2.47 us
  transfers between devices with their start and end apart: 19, of which 9 were waited for; matrix products, arithmetic and copies ran while one was open for 0% of the time, Pallas kernels for 20%

profile of v3, /device:TPU:25, one launch (start us, length us, event | category | flops | bytes accessed | tf_op | source)
XLA Modules:
  0.0 85.5 jit_solution(3841401702823780353)
XLA Ops:
  3.5 2.2 %copy-done = bf16[8,1024,256]{2,1,0:T(8,128)(2,1)S(1)} copy-done((bf16[8,1024,256]{2,1,0:T(8,128)(2,1)S(1)}, bf16[8,1024,256]{2,1,0:T(8,128)(2,1)}, u32[]{:S(2)}) %copy-start) | copy-done | bytes 4194328
  5.7 2.2 %copy-done.1 = bf16[8,1024,256]{2,1,0:T(8,128)(2,1)S(1)} copy-done((bf16[8,1024,256]{2,1,0:T(8,128)(2,1)S(1)}, bf16[8,1024,256]{2,1,0:T(8,128)(2,1)}, u32[]{:S(2)}) %copy-start.1) | copy-done | bytes 4194328
  8.6 1.3 %collective-permute-start.3 = (f32[2,4,16,512]{3,2,1,0:T(8,128)S(1)}, f32[2,4,16,512]{3,2,1,0:T(8,128)S(1)}, u32[]{:S(2)}, u32[]{:S(2)}) collective-permute-start(f32[2,4,16,512]{3,2,1,0:T(8,128)S(1)} %add_select_fusion), channel_id=1, source_target_pairs={{0,4},{1,5},{2,6},{3,7},{8,12},{9,13},{10,14},{11,15},{16,20},{17,... | collective-permute-start | bytes 786440 | tf_op jit(solution)/shard_map/ppermute | solution.py:202
  9.9 13.1 %collective-permute-done.3 = f32[2,4,16,512]{3,2,1,0:T(8,128)S(1)} collective-permute-done((f32[2,4,16,512]{3,2,1,0:T(8,128)S(1)}, f32[2,4,16,512]{3,2,1,0:T(8,128)S(1)}, u32[]{:S(2)}, u32[]{:S(2)}) %collective-permute-start.3) | collective-permute-done | bytes 262176 | tf_op jit(solution)/shard_map/ppermute | solution.py:202
  23.0 1.3 %collective-permute-start.4 = (f32[2,4,16,512]{3,2,1,0:T(8,128)S(1)}, f32[2,4,16,512]{3,2,1,0:T(8,128)S(1)}, u32[]{:S(2)}, u32[]{:S(2)}) collective-permute-start(f32[2,4,16,512]{3,2,1,0:T(8,128)S(1)} %broadcast_select_fusion), channel_id=1, source_target_pairs={{0,1},{1,2},{2,3},{3,0},{4,5},{5,6},{6,7},{7,4},{8,9},{9,10},{10,1... | collective-permute-start | bytes 786440 | tf_op jit(solution)/shard_map/ppermute | solution.py:192
  24.3 1.5 %collective-permute-start.5 = (f32[2,4,16,512]{3,2,1,0:T(8,128)S(1)}, f32[2,4,16,512]{3,2,1,0:T(8,128)S(1)}, u32[]{:S(2)}, u32[]{:S(2)}) collective-permute-start(f32[2,4,16,512]{3,2,1,0:T(8,128)S(1)} %broadcast_select_fusion), channel_id=1, source_target_pairs={{0,3},{1,0},{2,1},{3,2},{4,7},{5,4},{6,5},{7,6},{8,11},{9,8},{10,9... | collective-permute-start | bytes 786440 | tf_op jit(solution)/shard_map/ppermute | solution.py:192
  25.8 1.5 %collective-permute-start.8 = (f32[2,4,16,512]{3,2,1,0:T(8,128)S(1)}, f32[2,4,16,512]{3,2,1,0:T(8,128)S(1)}, u32[]{:S(2)}, u32[]{:S(2)}) collective-permute-start(f32[2,4,16,512]{3,2,1,0:T(8,128)S(1)} %broadcast_select_fusion), channel_id=1, source_target_pairs={{0,2},{1,3},{2,0},{3,1},{4,6},{5,7},{6,4},{7,5},{8,10},{9,11},{10,... | collective-permute-start | bytes 786440 | tf_op jit(solution)/shard_map/ppermute | solution.py:192
  27.3 2.5 %collective-permute-done.4 = f32[2,4,16,512]{3,2,1,0:T(8,128)S(1)} collective-permute-done((f32[2,4,16,512]{3,2,1,0:T(8,128)S(1)}, f32[2,4,16,512]{3,2,1,0:T(8,128)S(1)}, u32[]{:S(2)}, u32[]{:S(2)}) %collective-permute-start.4) | collective-permute-done | bytes 262176 | tf_op jit(solution)/shard_map/ppermute | solution.py:192
  30.0 3.7 %collective-permute-done.8 = f32[2,4,16,512]{3,2,1,0:T(8,128)S(1)} collective-permute-done((f32[2,4,16,512]{3,2,1,0:T(8,128)S(1)}, f32[2,4,16,512]{3,2,1,0:T(8,128)S(1)}, u32[]{:S(2)}, u32[]{:S(2)}) %collective-permute-start.8) | collective-permute-done | bytes 262176 | tf_op jit(solution)/shard_map/ppermute | solution.py:192
  33.7 1.5 %collective-permute-start.10 = (f32[2,2,4,16,512]{4,3,2,1,0:T(8,128)S(1)}, f32[2,2,4,16,512]{4,3,2,1,0:T(8,128)S(1)}, u32[]{:S(2)}, u32[]{:S(2)}) collective-permute-start(f32[2,2,4,16,512]{4,3,2,1,0:T(8,128)S(1)} %pad_maximum_fusion.1.refs_1_), channel_id=1, source_target_pairs={{0,24},{1,25},{2,26},{3,27},{4,28},{5,29},{6,30},{7,31},{8,0},{9,1... | collective-permute-start | bytes 1572872 | tf_op jit(solution)/shard_map/ppermute | solution.py:192
  35.2 2.2 %collective-permute-start.11 = (f32[2,2,4,16,512]{4,3,2,1,0:T(8,128)S(1)}, f32[2,2,4,16,512]{4,3,2,1,0:T(8,128)S(1)}, u32[]{:S(2)}, u32[]{:S(2)}) collective-permute-start(f32[2,2,4,16,512]{4,3,2,1,0:T(8,128)S(1)} %pad_maximum_fusion.refs_0_), channel_id=1, source_target_pairs={{0,24},{1,25},{2,26},{3,27},{4,28},{5,29},{6,30},{7,31},{8,0},{9,1... | collective-permute-start | bytes 1572872 | tf_op jit(solution)/shard_map/ppermute | solution.py:192
  37.4 4.8 %shard_map.39.refs_2_ = f32[4,16,16,256]{3,2,1,0:T(8,128)S(1)} custom-call(f32[8,4,16,512]{3,2,1,0:T(8,128)S(1)} %get-tuple-element.23.x_ref, bf16[8,1024,256]{2,1,0:T(8,128)(2,1)S(1)} %get-tuple-element.30.high_ref, bf16[8,1024,256]{2,1,0:T(8,128)(2,1)S(1)} %get-tuple-element.31.low_ref, f32[2,2,4,16,512]{4,3,2,1,0:T(8,128)S(1)} %pad_maximum_fusion.refs_0_, ...), custom_call_target="tpu_custom_call" | custom-call | flops 3221225472 | bytes 12582912 | tf_op jit(solution)/shard_map/pallas_call | solution.py:128
  42.4 2.9 %collective-permute-start.15 = (f32[2,2,4,16,512]{4,3,2,1,0:T(8,128)S(1)}, f32[2,2,4,16,512]{4,3,2,1,0:T(8,128)S(1)}, u32[]{:S(2)}, u32[]{:S(2)}) collective-permute-start(f32[2,2,4,16,512]{4,3,2,1,0:T(8,128)S(1)} %collective-permute-done.10.refs_1_), channel_id=1, source_target_pairs={{0,24},{1,25},{2,26},{3,27},{4,28},{5,29},{6,30},{7,31},{8,0},{9,1... | collective-permute-start | bytes 1572872 | tf_op jit(solution)/shard_map/ppermute | solution.py:192
  45.3 2.4 %collective-permute-done.11.refs_1_ = f32[2,2,4,16,512]{4,3,2,1,0:T(8,128)S(1)} collective-permute-done((f32[2,2,4,16,512]{4,3,2,1,0:T(8,128)S(1)}, f32[2,2,4,16,512]{4,3,2,1,0:T(8,128)S(1)}, u32[]{:S(2)}, u32[]{:S(2)}) %collective-permute-start.11) | collective-permute-done | bytes 524320 | tf_op jit(solution)/shard_map/ppermute | solution.py:192
  47.7 4.5 %shard_map.40.refs_2_ = f32[4,16,16,256]{3,2,1,0:T(8,128)S(1)} custom-call(f32[8,4,16,512]{3,2,1,0:T(8,128)S(1)} %get-tuple-element.23.x_ref, bf16[8,1024,256]{2,1,0:T(8,128)(2,1)S(1)} %get-tuple-element.30.high_ref, bf16[8,1024,256]{2,1,0:T(8,128)(2,1)S(1)} %get-tuple-element.31.low_ref, ...), custom_call_target="tpu_custom_call", output_to_operand_aliasing={{}: (5, {})} | custom-call | flops 3221225472 | bytes 12582912 | tf_op jit(solution)/shard_map/pallas_call | solution.py:128
  52.2 4.8 %shard_map.41.refs_1_ = f32[4,16,16,256]{3,2,1,0:T(8,128)S(1)} custom-call(f32[8,4,16,512]{3,2,1,0:T(8,128)S(1)} %get-tuple-element.23.x_ref, bf16[8,1024,256]{2,1,0:T(8,128)(2,1)S(1)} %get-tuple-element.30.high_ref, bf16[8,1024,256]{2,1,0:T(8,128)(2,1)S(1)} %get-tuple-element.31.low_ref, ...), custom_call_target="tpu_custom_call", output_to_operand_aliasing={{}: (5, {})} | custom-call | flops 3221225472 | bytes 12582912 | tf_op jit(solution)/shard_map/pallas_call | solution.py:128
  57.0 2.5 %shard_map.42 = (f32[4,16,16,256]{3,2,1,0:T(8,128)S(1)}, f32[16,16,256]{2,1,0:T(8,128)S(1)}, f32[16,16,256]{2,1,0:T(8,128)S(1)}) custom-call(f32[8,4,16,512]{3,2,1,0:T(8,128)S(1)} %get-tuple-element.23.x_ref, bf16[8,1024,256]{2,1,0:T(8,128)(2,1)S(1)} %get-tuple-element.30.high_ref, ...), custom_call_target="tpu_custom_call", output_to_operand_aliasing={{0}: (4, {})} | custom-call | flops 1610612736 | bytes 6291456 | tf_op jit(solution)/shard_map/pallas_call | solution.py:128
  59.6 2.6 %shard_map.43 = (f32[4,16,16,256]{3,2,1,0:T(8,128)S(1)}, f32[16,16,256]{2,1,0:T(8,128)S(1)}, f32[16,16,256]{2,1,0:T(8,128)S(1)}) custom-call(f32[8,4,16,512]{3,2,1,0:T(8,128)S(1)} %get-tuple-element.23.x_ref, bf16[8,1024,256]{2,1,0:T(8,128)(2,1)S(1)} %get-tuple-element.30.high_ref, ...), custom_call_target="tpu_custom_call", output_to_operand_aliasing={{0}: (4, {})} | custom-call | flops 1610612736 | bytes 6291456 | tf_op jit(solution)/shard_map/pallas_call | solution.py:128
  62.2 5.4 %collective-permute-start.16 = (f32[16,16,256]{2,1,0:T(8,128)S(1)}, f32[16,16,256]{2,1,0:T(8,128)S(1)}, u32[]{:S(2)}, u32[]{:S(2)}) collective-permute-start(f32[16,16,256]{2,1,0:T(8,128)S(1)} %get-tuple-element.38), channel_id=1, source_target_pairs={{0,32},{32,0},{64,96},{96,64},{1,33},{33,1},{65,97},{97,65},{2,34}... | collective-permute-start | bytes 786440 | tf_op jit(solution)/shard_map/ppermute | solution.py:194
  69.1 1.3 %collective-permute-start.13 = (f32[16,16,256]{2,1,0:T(8,128)S(1)}, f32[16,16,256]{2,1,0:T(8,128)S(1)}, u32[]{:S(2)}, u32[]{:S(2)}) collective-permute-start(f32[16,16,256]{2,1,0:T(8,128)S(1)} %add.30), channel_id=1, source_target_pairs={{0,64},{32,96},{64,0},{96,32},{1,65},{33,97},{65,1},{97,33},{2,66}... | collective-permute-start | bytes 786440 | tf_op jit(solution)/shard_map/ppermute | solution.py:195
  70.4 5.9 %collective-permute-done.17 = f32[16,16,256]{2,1,0:T(8,128)S(1)} collective-permute-done((f32[16,16,256]{2,1,0:T(8,128)S(1)}, f32[16,16,256]{2,1,0:T(8,128)S(1)}, u32[]{:S(2)}, u32[]{:S(2)}) %collective-permute-start.17) | collective-permute-done | bytes 262176 | tf_op jit(solution)/shard_map/ppermute | solution.py:195
  76.4 2.1 %collective-permute-start.18 = (f32[16,16,256]{2,1,0:T(8,128)S(1)}, f32[16,16,256]{2,1,0:T(8,128)S(1)}, u32[]{:S(2)}, u32[]{:S(2)}) collective-permute-start(f32[16,16,256]{2,1,0:T(8,128)S(1)} %add.33.refs_2_), channel_id=1, source_target_pairs={{0,32},{32,0},{64,96},{96,64},{1,33},{33,1},{65,97},{97,65},{2,34}... | collective-permute-start | bytes 786440 | tf_op jit(solution)/shard_map/ppermute | solution.py:194
  78.5 3.5 %collective-permute-done.13 = f32[16,16,256]{2,1,0:T(8,128)S(1)} collective-permute-done((f32[16,16,256]{2,1,0:T(8,128)S(1)}, f32[16,16,256]{2,1,0:T(8,128)S(1)}, u32[]{:S(2)}, u32[]{:S(2)}) %collective-permute-start.13) | collective-permute-done | bytes 262176 | tf_op jit(solution)/shard_map/ppermute | solution.py:195
  82.0 1.3 %collective-permute-start.14 = (f32[16,16,256]{2,1,0:T(8,128)S(1)}, f32[16,16,256]{2,1,0:T(8,128)S(1)}, u32[]{:S(2)}, u32[]{:S(2)}) collective-permute-start(f32[16,16,256]{2,1,0:T(8,128)S(1)} %add.31.refs_0_), channel_id=1, source_target_pairs={{0,32},{32,0},{64,96},{96,64},{1,33},{33,1},{65,97},{97,65},{2,34}... | collective-permute-start | bytes 786440 | tf_op jit(solution)/shard_map/ppermute | solution.py:194
  (36 shorter events, 8.3 us)
Async XLA Ops:
  0.0 1.2 %copy-start.2 = (f32[1,2,16,8192]{3,2,1,0:T(8,128)S(1)}, f32[1,2,16,8192]{3,2,1,0:T(8,128)}, u32[]{:S(2)}) copy-start(f32[1,2,16,8192]{3,2,1,0:T(8,128)} %param.3) | copy-start | bytes 3145732
  1.5 7.0 %collective-permute-start = (f32[2,4,16,512]{3,2,1,0:T(8,128)S(1)}, f32[2,4,16,512]{3,2,1,0:T(8,128)S(1)}, u32[]{:S(2)}, u32[]{:S(2)}) collective-permute-start(f32[2,4,16,512]{3,2,1,0:T(8,128)S(1)} %get-tuple-element.25), channel_id=1, source_target_pairs={{0,1},{8,9},{16,17},{24,25},{32,33},{40,41},{48,49},{56,57},{64,65... | collective-permute-start | bytes 786440 | tf_op jit(solution)/shard_map/ppermute | solution.py:199
  2.1 6.3 %collective-permute-start.1 = (f32[2,4,16,512]{3,2,1,0:T(8,128)S(1)}, f32[2,4,16,512]{3,2,1,0:T(8,128)S(1)}, u32[]{:S(2)}, u32[]{:S(2)}) collective-permute-start(f32[2,4,16,512]{3,2,1,0:T(8,128)S(1)} %get-tuple-element.26), channel_id=1, source_target_pairs={{0,2},{8,10},{16,18},{24,26},{32,34},{40,42},{48,50},{56,58},{64,6... | collective-permute-start | bytes 786440 | tf_op jit(solution)/shard_map/ppermute | solution.py:199
  2.8 5.7 %collective-permute-start.2 = (f32[2,4,16,512]{3,2,1,0:T(8,128)S(1)}, f32[2,4,16,512]{3,2,1,0:T(8,128)S(1)}, u32[]{:S(2)}, u32[]{:S(2)}) collective-permute-start(f32[2,4,16,512]{3,2,1,0:T(8,128)S(1)} %get-tuple-element.27), channel_id=1, source_target_pairs={{0,3},{8,11},{16,19},{24,27},{32,35},{40,43},{48,51},{56,59},{64,6... | collective-permute-start | bytes 786440 | tf_op jit(solution)/shard_map/ppermute | solution.py:199
  3.5 2.2 %copy-start = (bf16[8,1024,256]{2,1,0:T(8,128)(2,1)S(1)}, bf16[8,1024,256]{2,1,0:T(8,128)(2,1)}, u32[]{:S(2)}) copy-start(bf16[8,1024,256]{2,1,0:T(8,128)(2,1)} %constant.43.clone.high_ref) | copy-start | bytes 12582916
  5.7 2.2 %copy-start.1 = (bf16[8,1024,256]{2,1,0:T(8,128)(2,1)S(1)}, bf16[8,1024,256]{2,1,0:T(8,128)(2,1)}, u32[]{:S(2)}) copy-start(bf16[8,1024,256]{2,1,0:T(8,128)(2,1)} %constant.44.clone.low_ref) | copy-start | bytes 12582916
  8.6 14.4 %collective-permute-start.3 = (f32[2,4,16,512]{3,2,1,0:T(8,128)S(1)}, f32[2,4,16,512]{3,2,1,0:T(8,128)S(1)}, u32[]{:S(2)}, u32[]{:S(2)}) collective-permute-start(f32[2,4,16,512]{3,2,1,0:T(8,128)S(1)} %add_select_fusion), channel_id=1, source_target_pairs={{0,4},{1,5},{2,6},{3,7},{8,12},{9,13},{10,14},{11,15},{16,20},{17,... | collective-permute-start | bytes 786440 | tf_op jit(solution)/shard_map/ppermute | solution.py:202
  23.0 6.8 %collective-permute-start.4 = (f32[2,4,16,512]{3,2,1,0:T(8,128)S(1)}, f32[2,4,16,512]{3,2,1,0:T(8,128)S(1)}, u32[]{:S(2)}, u32[]{:S(2)}) collective-permute-start(f32[2,4,16,512]{3,2,1,0:T(8,128)S(1)} %broadcast_select_fusion), channel_id=1, source_target_pairs={{0,1},{1,2},{2,3},{3,0},{4,5},{5,6},{6,7},{7,4},{8,9},{9,10},{10,1... | collective-permute-start | bytes 786440 | tf_op jit(solution)/shard_map/ppermute | solution.py:192
  24.3 5.5 %collective-permute-start.5 = (f32[2,4,16,512]{3,2,1,0:T(8,128)S(1)}, f32[2,4,16,512]{3,2,1,0:T(8,128)S(1)}, u32[]{:S(2)}, u32[]{:S(2)}) collective-permute-start(f32[2,4,16,512]{3,2,1,0:T(8,128)S(1)} %broadcast_select_fusion), channel_id=1, source_target_pairs={{0,3},{1,0},{2,1},{3,2},{4,7},{5,4},{6,5},{7,6},{8,11},{9,8},{10,9... | collective-permute-start | bytes 786440 | tf_op jit(solution)/shard_map/ppermute | solution.py:192
  25.8 7.8 %collective-permute-start.8 = (f32[2,4,16,512]{3,2,1,0:T(8,128)S(1)}, f32[2,4,16,512]{3,2,1,0:T(8,128)S(1)}, u32[]{:S(2)}, u32[]{:S(2)}) collective-permute-start(f32[2,4,16,512]{3,2,1,0:T(8,128)S(1)} %broadcast_select_fusion), channel_id=1, source_target_pairs={{0,2},{1,3},{2,0},{3,1},{4,6},{5,7},{6,4},{7,5},{8,10},{9,11},{10,... | collective-permute-start | bytes 786440 | tf_op jit(solution)/shard_map/ppermute | solution.py:192
  29.9 12.4 %collective-permute-start.6 = (f32[2,2,4,16,512]{4,3,2,1,0:T(8,128)S(1)}, f32[2,2,4,16,512]{4,3,2,1,0:T(8,128)S(1)}, u32[]{:S(2)}, u32[]{:S(2)}) collective-permute-start(f32[2,2,4,16,512]{4,3,2,1,0:T(8,128)S(1)} %pad_maximum_fusion.refs_0_), channel_id=1, source_target_pairs={{0,8},{1,9},{2,10},{3,11},{4,12},{5,13},{6,14},{7,15},{8,16},{9,17... | collective-permute-start | bytes 1572872 | tf_op jit(solution)/shard_map/ppermute | solution.py:192
  33.7 8.7 %collective-permute-start.10 = (f32[2,2,4,16,512]{4,3,2,1,0:T(8,128)S(1)}, f32[2,2,4,16,512]{4,3,2,1,0:T(8,128)S(1)}, u32[]{:S(2)}, u32[]{:S(2)}) collective-permute-start(f32[2,2,4,16,512]{4,3,2,1,0:T(8,128)S(1)} %pad_maximum_fusion.1.refs_1_), channel_id=1, source_target_pairs={{0,24},{1,25},{2,26},{3,27},{4,28},{5,29},{6,30},{7,31},{8,0},{9,1... | collective-permute-start | bytes 1572872 | tf_op jit(solution)/shard_map/ppermute | solution.py:192
  35.2 12.5 %collective-permute-start.11 = (f32[2,2,4,16,512]{4,3,2,1,0:T(8,128)S(1)}, f32[2,2,4,16,512]{4,3,2,1,0:T(8,128)S(1)}, u32[]{:S(2)}, u32[]{:S(2)}) collective-permute-start(f32[2,2,4,16,512]{4,3,2,1,0:T(8,128)S(1)} %pad_maximum_fusion.refs_0_), channel_id=1, source_target_pairs={{0,24},{1,25},{2,26},{3,27},{4,28},{5,29},{6,30},{7,31},{8,0},{9,1... | collective-permute-start | bytes 1572872 | tf_op jit(solution)/shard_map/ppermute | solution.py:192
  37.4 14.8 %collective-permute-start.9 = (f32[2,2,4,16,512]{4,3,2,1,0:T(8,128)S(1)}, f32[2,2,4,16,512]{4,3,2,1,0:T(8,128)S(1)}, u32[]{:S(2)}, u32[]{:S(2)}) collective-permute-start(f32[2,2,4,16,512]{4,3,2,1,0:T(8,128)S(1)} %pad_maximum_fusion.1.refs_1_), channel_id=1, source_target_pairs={{0,8},{1,9},{2,10},{3,11},{4,12},{5,13},{6,14},{7,15},{8,16},{9,17... | collective-permute-start | bytes 1572872 | tf_op jit(solution)/shard_map/ppermute | solution.py:192
  42.3 14.7 %collective-permute-start.7 = (f32[2,2,4,16,512]{4,3,2,1,0:T(8,128)S(1)}, f32[2,2,4,16,512]{4,3,2,1,0:T(8,128)S(1)}, u32[]{:S(2)}, u32[]{:S(2)}) collective-permute-start(f32[2,2,4,16,512]{4,3,2,1,0:T(8,128)S(1)} %collective-permute-done.6.refs_0_), channel_id=1, source_target_pairs={{0,8},{1,9},{2,10},{3,11},{4,12},{5,13},{6,14},{7,15},{8,16},{9,17... | collective-permute-start | bytes 1572872 | tf_op jit(solution)/shard_map/ppermute | solution.py:192
  42.4 17.2 %collective-permute-start.15 = (f32[2,2,4,16,512]{4,3,2,1,0:T(8,128)S(1)}, f32[2,2,4,16,512]{4,3,2,1,0:T(8,128)S(1)}, u32[]{:S(2)}, u32[]{:S(2)}) collective-permute-start(f32[2,2,4,16,512]{4,3,2,1,0:T(8,128)S(1)} %collective-permute-done.10.refs_1_), channel_id=1, source_target_pairs={{0,24},{1,25},{2,26},{3,27},{4,28},{5,29},{6,30},{7,31},{8,0},{9,1... | collective-permute-start | bytes 1572872 | tf_op jit(solution)/shard_map/ppermute | solution.py:192
  62.2 6.5 %collective-permute-start.16 = (f32[16,16,256]{2,1,0:T(8,128)S(1)}, f32[16,16,256]{2,1,0:T(8,128)S(1)}, u32[]{:S(2)}, u32[]{:S(2)}) collective-permute-start(f32[16,16,256]{2,1,0:T(8,128)S(1)} %get-tuple-element.38), channel_id=1, source_target_pairs={{0,32},{32,0},{64,96},{96,64},{1,33},{33,1},{65,97},{97,65},{2,34}... | collective-permute-start | bytes 786440 | tf_op jit(solution)/shard_map/ppermute | solution.py:194
  67.5 1.5 %collective-permute-start.12 = (f32[16,16,256]{2,1,0:T(8,128)S(1)}, f32[16,16,256]{2,1,0:T(8,128)S(1)}, u32[]{:S(2)}, u32[]{:S(2)}) collective-permute-start(f32[16,16,256]{2,1,0:T(8,128)S(1)} %get-tuple-element.35), channel_id=1, source_target_pairs={{0,32},{32,0},{64,96},{96,64},{1,33},{33,1},{65,97},{97,65},{2,34}... | collective-permute-start | bytes 786440 | tf_op jit(solution)/shard_map/ppermute | solution.py:194
  68.7 7.6 %collective-permute-start.17 = (f32[16,16,256]{2,1,0:T(8,128)S(1)}, f32[16,16,256]{2,1,0:T(8,128)S(1)}, u32[]{:S(2)}, u32[]{:S(2)}) collective-permute-start(f32[16,16,256]{2,1,0:T(8,128)S(1)} %add.32), channel_id=1, source_target_pairs={{0,64},{32,96},{64,0},{96,32},{1,65},{33,97},{65,1},{97,33},{2,66}... | collective-permute-start | bytes 786440 | tf_op jit(solution)/shard_map/ppermute | solution.py:195
  69.1 12.8 %collective-permute-start.13 = (f32[16,16,256]{2,1,0:T(8,128)S(1)}, f32[16,16,256]{2,1,0:T(8,128)S(1)}, u32[]{:S(2)}, u32[]{:S(2)}) collective-permute-start(f32[16,16,256]{2,1,0:T(8,128)S(1)} %add.30), channel_id=1, source_target_pairs={{0,64},{32,96},{64,0},{96,32},{1,65},{33,97},{65,1},{97,33},{2,66}... | collective-permute-start | bytes 786440 | tf_op jit(solution)/shard_map/ppermute | solution.py:195
  76.4 6.9 %collective-permute-start.18 = (f32[16,16,256]{2,1,0:T(8,128)S(1)}, f32[16,16,256]{2,1,0:T(8,128)S(1)}, u32[]{:S(2)}, u32[]{:S(2)}) collective-permute-start(f32[16,16,256]{2,1,0:T(8,128)S(1)} %add.33.refs_2_), channel_id=1, source_target_pairs={{0,32},{32,0},{64,96},{96,64},{1,33},{33,1},{65,97},{97,65},{2,34}... | collective-permute-start | bytes 786440 | tf_op jit(solution)/shard_map/ppermute | solution.py:194
  82.0 2.4 %collective-permute-start.14 = (f32[16,16,256]{2,1,0:T(8,128)S(1)}, f32[16,16,256]{2,1,0:T(8,128)S(1)}, u32[]{:S(2)}, u32[]{:S(2)}) collective-permute-start(f32[16,16,256]{2,1,0:T(8,128)S(1)} %add.31.refs_0_), channel_id=1, source_target_pairs={{0,32},{32,0},{64,96},{96,64},{1,33},{33,1},{65,97},{97,65},{2,34}... | collective-permute-start | bytes 786440 | tf_op jit(solution)/shard_map/ppermute | solution.py:194

commit v4 on v3

--- a/solution.py
+++ b/solution.py
@@ -120,11 +120,12 @@
 def correlate(steps, values, tables, total=None, finished=None):
     here = lambda value: pltpu.with_memory_space_constraint(value, pltpu.VMEM)
     started = total is not None
+    values = [value.reshape(-1, 2, 4, CH, W) for value in values]
     args = [here(value) for value in (*tables, *values, *([total] if started else []))]
     sums = jax.ShapeDtypeStruct((4, CH, CH, LAGS), jnp.float32)
     one = jax.ShapeDtypeStruct((CH, CH, LAGS), jnp.float32)
     outs = [sums] + ([one] * 2 if finished is not None else [])
-    pairs = 2 * len(steps)
+    pairs = sum(len(nears) for _, nears in steps)
     return pl.pallas_call(
         functools.partial(correlate_kernel, steps, started, finished),
         out_shape=outs,
@@ -214,15 +215,18 @@
     near, ends = (1, -1), (0, 2)
     tabled = (x, high, low)
     total = correlate([(0, near), (0, ends)], [firsts[0], seconds[0]], tabled)[0]
-    total = correlate([(1, near), (-1, near)], [firsts[1], firsts[-1]], tabled, total)[0]
-    total = correlate([(1, ends), (-1, ends)], [seconds[1], seconds[-1]], tabled, total)[0]
-    total, *pieces = correlate([(2, near)], [firsts[2]], tabled, total, HALVES[0])
-    total, *others = correlate([(2, ends)], [seconds[2]], tabled, total, HALVES[1])
-    placed = []
-    for keep, give in (pieces, others):
-        pair = keep + other_core(give)
-        both = pair + other_chip(pair)
-        placed += [both, other_core(both)]
+    total = correlate([(1, near), (-1, ends)], [firsts[1], seconds[-1]], tabled, total)[0]
+    total = correlate([(-1, near), (1, ends)], [firsts[-1], seconds[1]], tabled, total)[0]
+    total, keep, give = correlate([(2, near)], [firsts[2]], tabled, total, HALVES[0])
+    pair = keep + other_core(give)
+    total = correlate([(2, (0,))], [seconds[2][0]], tabled, total)[0]
+    total, pair = lax.optimization_barrier((total, pair))
+    both = pair + other_chip(pair)
+    placed = [both, other_core(both)]
+    _, keep, give = correlate([(2, (2,))], [seconds[2][1]], tabled, total, HALVES[1])
+    pair = keep + other_core(give)
+    both = pair + other_chip(pair)
+    placed += [both, other_core(both)]
     return place(placed).reshape(CH, 4 * CH, LAGS)
 
 

time: 86.1 us -> 82.1 us (0.954)
  waiting for transfers between devices: 33.5 us -> 31.6 us
  starting transfers between devices: 24.7 us -> 23.2 us
    ppermute x9, waiting for transfers between devices: 8.57 us -> 6.19 us  [send(): return lax.ppermute(value, ('win', 'chan'), pairs)]
    ppermute x2, starting transfers between devices: 1.38 us -> 0.3 us  [shards(): lax.ppermute(value, 'win', [(w, w ^ 2) for w in range(4)])]
    pallas_call x5 -> x6, Pallas kernels: 19.2 us -> 18.8 us  [correlate(): pl.pallas_call(functools.partial(correlate_kernel, steps, started, finish...]
  transfers between devices with their start and end apart: 19 -> 19, of which waited for: 9 -> 7; matrix products, arithmetic and copies ran while one was open for 0% -> 0% of each run, Pallas kernels for 20% -> 22%
where the time goes in v4:
time: 82.1 us; the launch traced here: 81.6 us
  waiting for transfers between devices  31.6 us (38%)
  starting transfers between devices  23.2 us (28%)
  Pallas kernels  20.6 us (25%)
  local copies, waits for them, and re-layouts  5.64 us (7%)
    pallas_call x6, Pallas kernels, correlate(): pl.pallas_call(functools.partial(correlate_kernel, steps, started, finish...  18.8 us
    ppermute x1, waiting for transfers between devices, shards(): lax.ppermute(mine, 'chan', [(8 * s + z, 8 * s + 4 + z) for s in range(4)...  13.1 us
    ppermute x9, starting transfers between devices, send(): return lax.ppermute(value, ('win', 'chan'), pairs)  11.1 us
    ppermute x2, waiting for transfers between devices, shards(): lax.ppermute(value, 'win', [(w, w ^ 2) for w in range(4)])  9.9 us
    ppermute x4, starting transfers between devices, shards(): lax.ppermute(value, 'win', [(w, w ^ 1) for w in range(4)])  8.43 us
    ppermute x9, waiting for transfers between devices, send(): return lax.ppermute(value, ('win', 'chan'), pairs)  6.19 us
    unnamed x6, local copies, waits for them, and re-layouts  5.6 us
    ppermute x4, waiting for transfers between devices, shards(): lax.ppermute(value, 'win', [(w, w ^ 1) for w in range(4)])  2.42 us
  transfers between devices with their start and end apart: 19, of which 7 were waited for; matrix products, arithmetic and copies ran while one was open for 0% of the time, Pallas kernels for 22%

profile of v4, /device:TPU:25, one launch (start us, length us, event | category | flops | bytes accessed | tf_op | source)
XLA Modules:
  0.0 81.6 jit_solution(17696698722113527382)
XLA Ops:
  0.0 1.2 %copy-done.2 = f32[1,2,16,8192]{3,2,1,0:T(8,128)S(1)} copy-done((f32[1,2,16,8192]{3,2,1,0:T(8,128)S(1)}, f32[1,2,16,8192]{3,2,1,0:T(8,128)}, u32[]{:S(2)}) %copy-start.2) | copy-done | bytes 1048600
  3.5 2.2 %copy-done = bf16[8,1024,256]{2,1,0:T(8,128)(2,1)S(1)} copy-done((bf16[8,1024,256]{2,1,0:T(8,128)(2,1)S(1)}, bf16[8,1024,256]{2,1,0:T(8,128)(2,1)}, u32[]{:S(2)}) %copy-start) | copy-done | bytes 4194328
  5.7 2.2 %copy-done.1 = bf16[8,1024,256]{2,1,0:T(8,128)(2,1)S(1)} copy-done((bf16[8,1024,256]{2,1,0:T(8,128)(2,1)S(1)}, bf16[8,1024,256]{2,1,0:T(8,128)(2,1)}, u32[]{:S(2)}) %copy-start.1) | copy-done | bytes 4194328
  8.6 1.3 %collective-permute-start.3 = (f32[2,4,16,512]{3,2,1,0:T(8,128)S(1)}, f32[2,4,16,512]{3,2,1,0:T(8,128)S(1)}, u32[]{:S(2)}, u32[]{:S(2)}) collective-permute-start(f32[2,4,16,512]{3,2,1,0:T(8,128)S(1)} %add_select_fusion), channel_id=1, source_target_pairs={{0,4},{1,5},{2,6},{3,7},{8,12},{9,13},{10,14},{11,15},{16,20},{17,... | collective-permute-start | bytes 786440 | tf_op jit(solution)/shard_map/ppermute | solution.py:203
  9.9 13.1 %collective-permute-done.3 = f32[2,4,16,512]{3,2,1,0:T(8,128)S(1)} collective-permute-done((f32[2,4,16,512]{3,2,1,0:T(8,128)S(1)}, f32[2,4,16,512]{3,2,1,0:T(8,128)S(1)}, u32[]{:S(2)}, u32[]{:S(2)}) %collective-permute-start.3) | collective-permute-done | bytes 262176 | tf_op jit(solution)/shard_map/ppermute | solution.py:203
  23.0 1.3 %collective-permute-start.7 = (f32[2,4,16,512]{3,2,1,0:T(8,128)S(1)}, f32[2,4,16,512]{3,2,1,0:T(8,128)S(1)}, u32[]{:S(2)}, u32[]{:S(2)}) collective-permute-start(f32[2,4,16,512]{3,2,1,0:T(8,128)S(1)} %broadcast_select_fusion), channel_id=1, source_target_pairs={{0,1},{1,2},{2,3},{3,0},{4,5},{5,6},{6,7},{7,4},{8,9},{9,10},{10,1... | collective-permute-start | bytes 786440 | tf_op jit(solution)/shard_map/ppermute | solution.py:193
  24.3 1.5 %collective-permute-start.8 = (f32[2,4,16,512]{3,2,1,0:T(8,128)S(1)}, f32[2,4,16,512]{3,2,1,0:T(8,128)S(1)}, u32[]{:S(2)}, u32[]{:S(2)}) collective-permute-start(f32[2,4,16,512]{3,2,1,0:T(8,128)S(1)} %broadcast_select_fusion), channel_id=1, source_target_pairs={{0,3},{1,0},{2,1},{3,2},{4,7},{5,4},{6,5},{7,6},{8,11},{9,8},{10,9... | collective-permute-start | bytes 786440 | tf_op jit(solution)/shard_map/ppermute | solution.py:193
  25.8 1.5 %collective-permute-start.4 = (f32[2,4,16,512]{3,2,1,0:T(8,128)S(1)}, f32[2,4,16,512]{3,2,1,0:T(8,128)S(1)}, u32[]{:S(2)}, u32[]{:S(2)}) collective-permute-start(f32[2,4,16,512]{3,2,1,0:T(8,128)S(1)} %broadcast_select_fusion), channel_id=1, source_target_pairs={{0,2},{1,3},{2,0},{3,1},{4,6},{5,7},{6,4},{7,5},{8,10},{9,11},{10,... | collective-permute-start | bytes 786440 | tf_op jit(solution)/shard_map/ppermute | solution.py:193
  27.3 2.5 %collective-permute-done.7 = f32[2,4,16,512]{3,2,1,0:T(8,128)S(1)} collective-permute-done((f32[2,4,16,512]{3,2,1,0:T(8,128)S(1)}, f32[2,4,16,512]{3,2,1,0:T(8,128)S(1)}, u32[]{:S(2)}, u32[]{:S(2)}) %collective-permute-start.7) | collective-permute-done | bytes 262176 | tf_op jit(solution)/shard_map/ppermute | solution.py:193
  30.0 3.7 %collective-permute-done.4 = f32[2,4,16,512]{3,2,1,0:T(8,128)S(1)} collective-permute-done((f32[2,4,16,512]{3,2,1,0:T(8,128)S(1)}, f32[2,4,16,512]{3,2,1,0:T(8,128)S(1)}, u32[]{:S(2)}, u32[]{:S(2)}) %collective-permute-start.4) | collective-permute-done | bytes 262176 | tf_op jit(solution)/shard_map/ppermute | solution.py:193
  33.7 1.5 %collective-permute-start.5 = (f32[2,2,4,16,512]{4,3,2,1,0:T(8,128)S(1)}, f32[2,2,4,16,512]{4,3,2,1,0:T(8,128)S(1)}, u32[]{:S(2)}, u32[]{:S(2)}) collective-permute-start(f32[2,2,4,16,512]{4,3,2,1,0:T(8,128)S(1)} %pad_maximum_fusion.refs_1_), channel_id=1, source_target_pairs={{0,24},{1,25},{2,26},{3,27},{4,28},{5,29},{6,30},{7,31},{8,0},{9,1... | collective-permute-start | bytes 1572872 | tf_op jit(solution)/shard_map/ppermute | solution.py:193
  35.2 2.2 %collective-permute-start.11 = (f32[2,2,4,16,512]{4,3,2,1,0:T(8,128)S(1)}, f32[2,2,4,16,512]{4,3,2,1,0:T(8,128)S(1)}, u32[]{:S(2)}, u32[]{:S(2)}) collective-permute-start(f32[2,2,4,16,512]{4,3,2,1,0:T(8,128)S(1)} %pad_maximum_fusion.1.refs_0_), channel_id=1, source_target_pairs={{0,24},{1,25},{2,26},{3,27},{4,28},{5,29},{6,30},{7,31},{8,0},{9,1... | collective-permute-start | bytes 1572872 | tf_op jit(solution)/shard_map/ppermute | solution.py:193
  37.4 4.8 %shard_map.39.refs_2_ = f32[4,16,16,256]{3,2,1,0:T(8,128)S(1)} custom-call(f32[8,4,16,512]{3,2,1,0:T(8,128)S(1)} %get-tuple-element.25.x_ref, bf16[8,1024,256]{2,1,0:T(8,128)(2,1)S(1)} %get-tuple-element.32.high_ref, bf16[8,1024,256]{2,1,0:T(8,128)(2,1)S(1)} %get-tuple-element.33.low_ref, f32[2,2,4,16,512]{4,3,2,1,0:T(8,128)S(1)} %pad_maximum_fusion.1.refs_0_, ...), custom_call_target="tpu_custom_call" | custom-call | flops 3221225472 | bytes 12582912 | tf_op jit(solution)/shard_map/pallas_call | solution.py:129
  42.4 2.9 %collective-permute-start.6 = (f32[2,2,4,16,512]{4,3,2,1,0:T(8,128)S(1)}, f32[2,2,4,16,512]{4,3,2,1,0:T(8,128)S(1)}, u32[]{:S(2)}, u32[]{:S(2)}) collective-permute-start(f32[2,2,4,16,512]{4,3,2,1,0:T(8,128)S(1)} %collective-permute-done.5.refs_1_), channel_id=1, source_target_pairs={{0,24},{1,25},{2,26},{3,27},{4,28},{5,29},{6,30},{7,31},{8,0},{9,1... | collective-permute-start | bytes 1572872 | tf_op jit(solution)/shard_map/ppermute | solution.py:193
  45.3 4.5 %shard_map.40.refs_2_ = f32[4,16,16,256]{3,2,1,0:T(8,128)S(1)} custom-call(f32[8,4,16,512]{3,2,1,0:T(8,128)S(1)} %get-tuple-element.25.x_ref, bf16[8,1024,256]{2,1,0:T(8,128)(2,1)S(1)} %get-tuple-element.32.high_ref, bf16[8,1024,256]{2,1,0:T(8,128)(2,1)S(1)} %get-tuple-element.33.low_ref, ...), custom_call_target="tpu_custom_call", output_to_operand_aliasing={{}: (5, {})} | custom-call | flops 3221225472 | bytes 12582912 | tf_op jit(solution)/shard_map/pallas_call | solution.py:129
  49.8 4.5 %shard_map.41.refs_1_ = f32[4,16,16,256]{3,2,1,0:T(8,128)S(1)} custom-call(f32[8,4,16,512]{3,2,1,0:T(8,128)S(1)} %get-tuple-element.25.x_ref, bf16[8,1024,256]{2,1,0:T(8,128)(2,1)S(1)} %get-tuple-element.32.high_ref, bf16[8,1024,256]{2,1,0:T(8,128)(2,1)S(1)} %get-tuple-element.33.low_ref, ...), custom_call_target="tpu_custom_call", output_to_operand_aliasing={{}: (5, {})} | custom-call | flops 3221225472 | bytes 12582912 | tf_op jit(solution)/shard_map/pallas_call | solution.py:129
  54.3 2.5 %shard_map.42 = (f32[4,16,16,256]{3,2,1,0:T(8,128)S(1)}, f32[16,16,256]{2,1,0:T(8,128)S(1)}, f32[16,16,256]{2,1,0:T(8,128)S(1)}) custom-call(f32[8,4,16,512]{3,2,1,0:T(8,128)S(1)} %get-tuple-element.25.x_ref, bf16[8,1024,256]{2,1,0:T(8,128)(2,1)S(1)} %get-tuple-element.32.high_ref, ...), custom_call_target="tpu_custom_call", output_to_operand_aliasing={{0}: (4, {})} | custom-call | flops 1610612736 | bytes 6291456 | tf_op jit(solution)/shard_map/pallas_call | solution.py:129
  56.9 5.2 %collective-permute-start.13 = (f32[16,16,256]{2,1,0:T(8,128)S(1)}, f32[16,16,256]{2,1,0:T(8,128)S(1)}, u32[]{:S(2)}, u32[]{:S(2)}) collective-permute-start(f32[16,16,256]{2,1,0:T(8,128)S(1)} %get-tuple-element.38), channel_id=1, source_target_pairs={{0,32},{32,0},{64,96},{96,64},{1,33},{33,1},{65,97},{97,65},{2,34}... | collective-permute-start | bytes 786440 | tf_op jit(solution)/shard_map/ppermute | solution.py:195
  62.1 1.2 %shard_map.43.refs_1_ = f32[4,16,16,256]{3,2,1,0:T(8,128)S(1)} custom-call(f32[8,4,16,512]{3,2,1,0:T(8,128)S(1)} %get-tuple-element.25.x_ref, bf16[8,1024,256]{2,1,0:T(8,128)(2,1)S(1)} %get-tuple-element.32.high_ref, bf16[8,1024,256]{2,1,0:T(8,128)(2,1)S(1)} %get-tuple-element.33.low_ref, ...), custom_call_target="tpu_custom_call", output_to_operand_aliasing={{}: (4, {})} | custom-call | flops 805306368 | bytes 3145728 | tf_op jit(solution)/shard_map/pallas_call | solution.py:129
  63.4 1.2 %shard_map.44 = (f32[4,16,16,256]{3,2,1,0:T(8,128)S(1)}, f32[16,16,256]{2,1,0:T(8,128)S(1)}, f32[16,16,256]{2,1,0:T(8,128)S(1)}) custom-call(f32[8,4,16,512]{3,2,1,0:T(8,128)S(1)} %get-tuple-element.25.x_ref, bf16[8,1024,256]{2,1,0:T(8,128)(2,1)S(1)} %get-tuple-element.32.high_ref, ...), custom_call_target="tpu_custom_call", output_to_operand_aliasing={{0}: (4, {})} | custom-call | flops 805306368 | bytes 3145728 | tf_op jit(solution)/shard_map/pallas_call | solution.py:129
  65.0 1.3 %collective-permute-done.16 = f32[16,16,256]{2,1,0:T(8,128)S(1)} collective-permute-done((f32[16,16,256]{2,1,0:T(8,128)S(1)}, f32[16,16,256]{2,1,0:T(8,128)S(1)}, u32[]{:S(2)}, u32[]{:S(2)}) %collective-permute-start.16) | collective-permute-done | bytes 262176 | tf_op jit(solution)/shard_map/ppermute | solution.py:195
  66.5 6.1 %collective-permute-done.14 = f32[16,16,256]{2,1,0:T(8,128)S(1)} collective-permute-done((f32[16,16,256]{2,1,0:T(8,128)S(1)}, f32[16,16,256]{2,1,0:T(8,128)S(1)}, u32[]{:S(2)}, u32[]{:S(2)}) %collective-permute-start.14) | collective-permute-done | bytes 262176 | tf_op jit(solution)/shard_map/ppermute | solution.py:196
  72.7 1.8 %collective-permute-start.15 = (f32[16,16,256]{2,1,0:T(8,128)S(1)}, f32[16,16,256]{2,1,0:T(8,128)S(1)}, u32[]{:S(2)}, u32[]{:S(2)}) collective-permute-start(f32[16,16,256]{2,1,0:T(8,128)S(1)} %add.31.refs_0_), channel_id=1, source_target_pairs={{0,32},{32,0},{64,96},{96,64},{1,33},{33,1},{65,97},{97,65},{2,34}... | collective-permute-start | bytes 786440 | tf_op jit(solution)/shard_map/ppermute | solution.py:195
  74.4 3.8 %collective-permute-done.17 = f32[16,16,256]{2,1,0:T(8,128)S(1)} collective-permute-done((f32[16,16,256]{2,1,0:T(8,128)S(1)}, f32[16,16,256]{2,1,0:T(8,128)S(1)}, u32[]{:S(2)}, u32[]{:S(2)}) %collective-permute-start.17) | collective-permute-done | bytes 262176 | tf_op jit(solution)/shard_map/ppermute | solution.py:196
  (38 shorter events, 7.4 us)
Async XLA Ops:
  0.0 1.2 %copy-start.2 = (f32[1,2,16,8192]{3,2,1,0:T(8,128)S(1)}, f32[1,2,16,8192]{3,2,1,0:T(8,128)}, u32[]{:S(2)}) copy-start(f32[1,2,16,8192]{3,2,1,0:T(8,128)} %param.3) | copy-start | bytes 3145732
  1.5 7.0 %collective-permute-start = (f32[2,4,16,512]{3,2,1,0:T(8,128)S(1)}, f32[2,4,16,512]{3,2,1,0:T(8,128)S(1)}, u32[]{:S(2)}, u32[]{:S(2)}) collective-permute-start(f32[2,4,16,512]{3,2,1,0:T(8,128)S(1)} %get-tuple-element.27), channel_id=1, source_target_pairs={{0,1},{8,9},{16,17},{24,25},{32,33},{40,41},{48,49},{56,57},{64,65... | collective-permute-start | bytes 786440 | tf_op jit(solution)/shard_map/ppermute | solution.py:200
  2.1 6.3 %collective-permute-start.1 = (f32[2,4,16,512]{3,2,1,0:T(8,128)S(1)}, f32[2,4,16,512]{3,2,1,0:T(8,128)S(1)}, u32[]{:S(2)}, u32[]{:S(2)}) collective-permute-start(f32[2,4,16,512]{3,2,1,0:T(8,128)S(1)} %get-tuple-element.28), channel_id=1, source_target_pairs={{0,2},{8,10},{16,18},{24,26},{32,34},{40,42},{48,50},{56,58},{64,6... | collective-permute-start | bytes 786440 | tf_op jit(solution)/shard_map/ppermute | solution.py:200
  2.8 5.7 %collective-permute-start.2 = (f32[2,4,16,512]{3,2,1,0:T(8,128)S(1)}, f32[2,4,16,512]{3,2,1,0:T(8,128)S(1)}, u32[]{:S(2)}, u32[]{:S(2)}) collective-permute-start(f32[2,4,16,512]{3,2,1,0:T(8,128)S(1)} %get-tuple-element.29), channel_id=1, source_target_pairs={{0,3},{8,11},{16,19},{24,27},{32,35},{40,43},{48,51},{56,59},{64,6... | collective-permute-start | bytes 786440 | tf_op jit(solution)/shard_map/ppermute | solution.py:200
  3.5 2.2 %copy-start = (bf16[8,1024,256]{2,1,0:T(8,128)(2,1)S(1)}, bf16[8,1024,256]{2,1,0:T(8,128)(2,1)}, u32[]{:S(2)}) copy-start(bf16[8,1024,256]{2,1,0:T(8,128)(2,1)} %constant.43.clone.high_ref) | copy-start | bytes 12582916
  5.7 2.2 %copy-start.1 = (bf16[8,1024,256]{2,1,0:T(8,128)(2,1)S(1)}, bf16[8,1024,256]{2,1,0:T(8,128)(2,1)}, u32[]{:S(2)}) copy-start(bf16[8,1024,256]{2,1,0:T(8,128)(2,1)} %constant.44.clone.low_ref) | copy-start | bytes 12582916
  8.6 14.4 %collective-permute-start.3 = (f32[2,4,16,512]{3,2,1,0:T(8,128)S(1)}, f32[2,4,16,512]{3,2,1,0:T(8,128)S(1)}, u32[]{:S(2)}, u32[]{:S(2)}) collective-permute-start(f32[2,4,16,512]{3,2,1,0:T(8,128)S(1)} %add_select_fusion), channel_id=1, source_target_pairs={{0,4},{1,5},{2,6},{3,7},{8,12},{9,13},{10,14},{11,15},{16,20},{17,... | collective-permute-start | bytes 786440 | tf_op jit(solution)/shard_map/ppermute | solution.py:203
  23.0 6.8 %collective-permute-start.7 = (f32[2,4,16,512]{3,2,1,0:T(8,128)S(1)}, f32[2,4,16,512]{3,2,1,0:T(8,128)S(1)}, u32[]{:S(2)}, u32[]{:S(2)}) collective-permute-start(f32[2,4,16,512]{3,2,1,0:T(8,128)S(1)} %broadcast_select_fusion), channel_id=1, source_target_pairs={{0,1},{1,2},{2,3},{3,0},{4,5},{5,6},{6,7},{7,4},{8,9},{9,10},{10,1... | collective-permute-start | bytes 786440 | tf_op jit(solution)/shard_map/ppermute | solution.py:193
  24.3 5.5 %collective-permute-start.8 = (f32[2,4,16,512]{3,2,1,0:T(8,128)S(1)}, f32[2,4,16,512]{3,2,1,0:T(8,128)S(1)}, u32[]{:S(2)}, u32[]{:S(2)}) collective-permute-start(f32[2,4,16,512]{3,2,1,0:T(8,128)S(1)} %broadcast_select_fusion), channel_id=1, source_target_pairs={{0,3},{1,0},{2,1},{3,2},{4,7},{5,4},{6,5},{7,6},{8,11},{9,8},{10,9... | collective-permute-start | bytes 786440 | tf_op jit(solution)/shard_map/ppermute | solution.py:193
  25.8 7.8 %collective-permute-start.4 = (f32[2,4,16,512]{3,2,1,0:T(8,128)S(1)}, f32[2,4,16,512]{3,2,1,0:T(8,128)S(1)}, u32[]{:S(2)}, u32[]{:S(2)}) collective-permute-start(f32[2,4,16,512]{3,2,1,0:T(8,128)S(1)} %broadcast_select_fusion), channel_id=1, source_target_pairs={{0,2},{1,3},{2,0},{3,1},{4,6},{5,7},{6,4},{7,5},{8,10},{9,11},{10,... | collective-permute-start | bytes 786440 | tf_op jit(solution)/shard_map/ppermute | solution.py:193
  29.9 12.4 %collective-permute-start.9 = (f32[2,2,4,16,512]{4,3,2,1,0:T(8,128)S(1)}, f32[2,2,4,16,512]{4,3,2,1,0:T(8,128)S(1)}, u32[]{:S(2)}, u32[]{:S(2)}) collective-permute-start(f32[2,2,4,16,512]{4,3,2,1,0:T(8,128)S(1)} %pad_maximum_fusion.1.refs_0_), channel_id=1, source_target_pairs={{0,8},{1,9},{2,10},{3,11},{4,12},{5,13},{6,14},{7,15},{8,16},{9,17... | collective-permute-start | bytes 1572872 | tf_op jit(solution)/shard_map/ppermute | solution.py:193
  33.7 8.7 %collective-permute-start.5 = (f32[2,2,4,16,512]{4,3,2,1,0:T(8,128)S(1)}, f32[2,2,4,16,512]{4,3,2,1,0:T(8,128)S(1)}, u32[]{:S(2)}, u32[]{:S(2)}) collective-permute-start(f32[2,2,4,16,512]{4,3,2,1,0:T(8,128)S(1)} %pad_maximum_fusion.refs_1_), channel_id=1, source_target_pairs={{0,24},{1,25},{2,26},{3,27},{4,28},{5,29},{6,30},{7,31},{8,0},{9,1... | collective-permute-start | bytes 1572872 | tf_op jit(solution)/shard_map/ppermute | solution.py:193
  35.2 14.6 %collective-permute-start.11 = (f32[2,2,4,16,512]{4,3,2,1,0:T(8,128)S(1)}, f32[2,2,4,16,512]{4,3,2,1,0:T(8,128)S(1)}, u32[]{:S(2)}, u32[]{:S(2)}) collective-permute-start(f32[2,2,4,16,512]{4,3,2,1,0:T(8,128)S(1)} %pad_maximum_fusion.1.refs_0_), channel_id=1, source_target_pairs={{0,24},{1,25},{2,26},{3,27},{4,28},{5,29},{6,30},{7,31},{8,0},{9,1... | collective-permute-start | bytes 1572872 | tf_op jit(solution)/shard_map/ppermute | solution.py:193
  37.4 12.4 %collective-permute-start.12 = (f32[2,2,4,16,512]{4,3,2,1,0:T(8,128)S(1)}, f32[2,2,4,16,512]{4,3,2,1,0:T(8,128)S(1)}, u32[]{:S(2)}, u32[]{:S(2)}) collective-permute-start(f32[2,2,4,16,512]{4,3,2,1,0:T(8,128)S(1)} %pad_maximum_fusion.refs_1_), channel_id=1, source_target_pairs={{0,8},{1,9},{2,10},{3,11},{4,12},{5,13},{6,14},{7,15},{8,16},{9,17... | collective-permute-start | bytes 1572872 | tf_op jit(solution)/shard_map/ppermute | solution.py:193
  42.3 12.0 %collective-permute-start.10 = (f32[2,2,4,16,512]{4,3,2,1,0:T(8,128)S(1)}, f32[2,2,4,16,512]{4,3,2,1,0:T(8,128)S(1)}, u32[]{:S(2)}, u32[]{:S(2)}) collective-permute-start(f32[2,2,4,16,512]{4,3,2,1,0:T(8,128)S(1)} %collective-permute-done.9.refs_0_), channel_id=1, source_target_pairs={{0,8},{1,9},{2,10},{3,11},{4,12},{5,13},{6,14},{7,15},{8,16},{9,17... | collective-permute-start | bytes 1572872 | tf_op jit(solution)/shard_map/ppermute | solution.py:193
  42.4 19.7 %collective-permute-start.6 = (f32[2,2,4,16,512]{4,3,2,1,0:T(8,128)S(1)}, f32[2,2,4,16,512]{4,3,2,1,0:T(8,128)S(1)}, u32[]{:S(2)}, u32[]{:S(2)}) collective-permute-start(f32[2,2,4,16,512]{4,3,2,1,0:T(8,128)S(1)} %collective-permute-done.5.refs_1_), channel_id=1, source_target_pairs={{0,24},{1,25},{2,26},{3,27},{4,28},{5,29},{6,30},{7,31},{8,0},{9,1... | collective-permute-start | bytes 1572872 | tf_op jit(solution)/shard_map/ppermute | solution.py:193
  56.9 6.4 %collective-permute-start.13 = (f32[16,16,256]{2,1,0:T(8,128)S(1)}, f32[16,16,256]{2,1,0:T(8,128)S(1)}, u32[]{:S(2)}, u32[]{:S(2)}) collective-permute-start(f32[16,16,256]{2,1,0:T(8,128)S(1)} %get-tuple-element.38), channel_id=1, source_target_pairs={{0,32},{32,0},{64,96},{96,64},{1,33},{33,1},{65,97},{97,65},{2,34}... | collective-permute-start | bytes 786440 | tf_op jit(solution)/shard_map/ppermute | solution.py:195
  64.6 1.6 %collective-permute-start.16 = (f32[16,16,256]{2,1,0:T(8,128)S(1)}, f32[16,16,256]{2,1,0:T(8,128)S(1)}, u32[]{:S(2)}, u32[]{:S(2)}) collective-permute-start(f32[16,16,256]{2,1,0:T(8,128)S(1)} %get-tuple-element.42), channel_id=1, source_target_pairs={{0,32},{32,0},{64,96},{96,64},{1,33},{33,1},{65,97},{97,65},{2,34}... | collective-permute-start | bytes 786440 | tf_op jit(solution)/shard_map/ppermute | solution.py:195
  64.9 7.7 %collective-permute-start.14 = (f32[16,16,256]{2,1,0:T(8,128)S(1)}, f32[16,16,256]{2,1,0:T(8,128)S(1)}, u32[]{:S(2)}, u32[]{:S(2)}) collective-permute-start(f32[16,16,256]{2,1,0:T(8,128)S(1)} %add.30), channel_id=1, source_target_pairs={{0,64},{32,96},{64,0},{96,32},{1,65},{33,97},{65,1},{97,33},{2,66}... | collective-permute-start | bytes 786440 | tf_op jit(solution)/shard_map/ppermute | solution.py:196
  66.2 12.0 %collective-permute-start.17 = (f32[16,16,256]{2,1,0:T(8,128)S(1)}, f32[16,16,256]{2,1,0:T(8,128)S(1)}, u32[]{:S(2)}, u32[]{:S(2)}) collective-permute-start(f32[16,16,256]{2,1,0:T(8,128)S(1)} %add.32), channel_id=1, source_target_pairs={{0,64},{32,96},{64,0},{96,32},{1,65},{33,97},{65,1},{97,33},{2,66}... | collective-permute-start | bytes 786440 | tf_op jit(solution)/shard_map/ppermute | solution.py:196
  72.7 6.7 %collective-permute-start.15 = (f32[16,16,256]{2,1,0:T(8,128)S(1)}, f32[16,16,256]{2,1,0:T(8,128)S(1)}, u32[]{:S(2)}, u32[]{:S(2)}) collective-permute-start(f32[16,16,256]{2,1,0:T(8,128)S(1)} %add.31.refs_0_), channel_id=1, source_target_pairs={{0,32},{32,0},{64,96},{96,64},{1,33},{33,1},{65,97},{97,65},{2,34}... | collective-permute-start | bytes 786440 | tf_op jit(solution)/shard_map/ppermute | solution.py:195
  78.3 2.3 %collective-permute-start.18 = (f32[16,16,256]{2,1,0:T(8,128)S(1)}, f32[16,16,256]{2,1,0:T(8,128)S(1)}, u32[]{:S(2)}, u32[]{:S(2)}) collective-permute-start(f32[16,16,256]{2,1,0:T(8,128)S(1)} %add.33.refs_2_), channel_id=1, source_target_pairs={{0,32},{32,0},{64,96},{96,64},{1,33},{33,1},{65,97},{97,65},{2,34}... | collective-permute-start | bytes 786440 | tf_op jit(solution)/shard_map/ppermute | solution.py:195

commit v5 on v4

--- a/solution.py
+++ b/solution.py
@@ -17,7 +17,7 @@
 PARTS = 8
 W = HALF // PARTS
 VMEM = pl.BlockSpec(memory_space=pltpu.VMEM)
-HALVES = ((1, 3), (0, 2))
+GROUPS = ((0, 1, 3), (2,))
 
 
 def tables():
@@ -72,34 +72,41 @@
     at_x, at_z, core = position()
     lane = lax.broadcasted_iota(jnp.int32, (CH, 128), 1)
     dot = functools.partial(jnp.dot, preferred_element_type=jnp.float32)
-    for g_ref, far, nears in sources:
-        for place, near in enumerate(nears):
-            block = (at_x + 4 - jnp.where(core == 0, far, near)) % 4
-            bins = (at_z + 4 - jnp.where(core == 0, near, far)) % 4
-            first = jnp.logical_and(lane == 0, bins == 0)
-            for part in range(2):
-                y = [g_ref[place, part, k] for k in range(4)]
-                for channel in range(CH):
-                    x = [x_ref[2 * bins + part, k, channel : channel + 1, :] for k in range(4)]
-                    ahead = x[0] * y[0] + x[1] * y[1]
-                    back = x[2] * y[2] + x[3] * y[3]
-                    even = ahead + back
-                    odd = (x[1] * y[0] - x[0] * y[1]) + (x[2] * y[3] - x[3] * y[2])
-                    if part == 0:
-                        edge = jnp.where(first, ahead[:, :128] - back[:, :128], odd[:, :128])
-                        odd = jnp.concatenate([edge, odd[:, 128:]], axis=1)
-                    rows = slice(CH * channel, CH * channel + CH)
-                    for half, value in enumerate((even, odd)):
-                        columns = slice((2 * part + half) * W, (2 * part + half + 1) * W)
-                        top = value.astype(jnp.bfloat16)
-                        lh[rows, columns] = top
-                        ll[rows, columns] = (value - top.astype(jnp.float32)).astype(jnp.bfloat16)
-            top = lh[...]
-            high = high_ref[pl.ds(2 * bins, 2)].reshape(4 * W, LAGS)
-            low = low_ref[pl.ds(2 * bins, 2)].reshape(4 * W, LAGS)
-            both = dot(jnp.concatenate([top, ll[...]], axis=0), high)
-            got = both[: CH * CH] + both[CH * CH :] + dot(top, low)
-            total[block] += got.reshape(CH, CH, LAGS)
+    for g_ref, far, nears, only in sources:
+
+        def add(g_ref=g_ref, far=far, nears=nears):
+            for place, near in enumerate(nears):
+                block = (at_x + 4 - jnp.where(core == 0, far, near)) % 4
+                bins = (at_z + 4 - jnp.where(core == 0, near, far)) % 4
+                first = jnp.logical_and(lane == 0, bins == 0)
+                for part in range(2):
+                    y = [g_ref[place, part, k] for k in range(4)]
+                    for channel in range(CH):
+                        x = [x_ref[2 * bins + part, k, channel : channel + 1, :] for k in range(4)]
+                        ahead = x[0] * y[0] + x[1] * y[1]
+                        back = x[2] * y[2] + x[3] * y[3]
+                        even = ahead + back
+                        odd = (x[1] * y[0] - x[0] * y[1]) + (x[2] * y[3] - x[3] * y[2])
+                        if part == 0:
+                            edge = jnp.where(first, ahead[:, :128] - back[:, :128], odd[:, :128])
+                            odd = jnp.concatenate([edge, odd[:, 128:]], axis=1)
+                        rows = slice(CH * channel, CH * channel + CH)
+                        for half, value in enumerate((even, odd)):
+                            columns = slice((2 * part + half) * W, (2 * part + half + 1) * W)
+                            top = value.astype(jnp.bfloat16)
+                            lh[rows, columns] = top
+                            ll[rows, columns] = (value - top.astype(jnp.float32)).astype(jnp.bfloat16)
+                top = lh[...]
+                high = high_ref[pl.ds(2 * bins, 2)].reshape(4 * W, LAGS)
+                low = low_ref[pl.ds(2 * bins, 2)].reshape(4 * W, LAGS)
+                both = dot(jnp.concatenate([top, ll[...]], axis=0), high)
+                got = both[: CH * CH] + both[CH * CH :] + dot(top, low)
+                total[block] += got.reshape(CH, CH, LAGS)
+
+        if only is None:
+            add()
+        else:
+            pl.when(core == only)(add)
 
 
 def correlate_kernel(steps, started, finished, x_ref, high_ref, low_ref, *refs):
@@ -107,14 +114,14 @@
     total = refs[n + started]
     if not started:
         total[...] = jnp.zeros_like(total)
-    sources = [(ref, far, nears) for ref, (far, nears) in zip(refs[:n], steps)]
+    sources = [(ref, far, nears, *(only or [None])) for ref, (far, nears, *only) in zip(refs[:n], steps)]
     add_parts(sources, x_ref, high_ref, low_ref, total, *refs[-2:])
     if finished is not None:
         at_x, _, core = position()
         keep, send = refs[n + started + 1 : n + started + 3]
-        here, there = finished
-        keep[...] = total[(at_x + jnp.where(core == 0, here, there)) % 4]
-        send[...] = total[(at_x + jnp.where(core == 0, there, here)) % 4]
+        for place, block in enumerate(finished):
+            keep[place] = total[(at_x + block) % 4, pl.ds(8 * core, 8)]
+            send[place] = total[(at_x + block) % 4, pl.ds(8 * (1 - core), 8)]
 
 
 def correlate(steps, values, tables, total=None, finished=None):
@@ -123,9 +130,9 @@
     values = [value.reshape(-1, 2, 4, CH, W) for value in values]
     args = [here(value) for value in (*tables, *values, *([total] if started else []))]
     sums = jax.ShapeDtypeStruct((4, CH, CH, LAGS), jnp.float32)
-    one = jax.ShapeDtypeStruct((CH, CH, LAGS), jnp.float32)
-    outs = [sums] + ([one] * 2 if finished is not None else [])
-    pairs = sum(len(nears) for _, nears in steps)
+    half = lambda blocks: jax.ShapeDtypeStruct((len(blocks), 8, CH, LAGS), jnp.float32)
+    outs = [sums] + ([half(finished)] * 2 if finished is not None else [])
+    pairs = sum(len(step[1]) for step in steps)
     return pl.pallas_call(
         functools.partial(correlate_kernel, steps, started, finished),
         out_shape=outs,
@@ -143,10 +150,11 @@
 def place_kernel(*refs):
     out_ref = refs[-1]
     at_x, _, core = position()
-    for pair, (here, there) in enumerate(HALVES):
+    for pair, blocks in enumerate(GROUPS):
         mine, other = refs[2 * pair : 2 * pair + 2]
-        out_ref[:, (at_x + jnp.where(core == 0, here, there)) % 4] = mine[...]
-        out_ref[:, (at_x + jnp.where(core == 0, there, here)) % 4] = other[...]
+        for place, block in enumerate(blocks):
+            out_ref[pl.ds(8 * core, 8), (at_x + block) % 4] = mine[place]
+            out_ref[pl.ds(8 * (1 - core), 8), (at_x + block) % 4] = other[place]
 
 
 def place(pieces):
@@ -217,16 +225,19 @@
     total = correlate([(0, near), (0, ends)], [firsts[0], seconds[0]], tabled)[0]
     total = correlate([(1, near), (-1, ends)], [firsts[1], seconds[-1]], tabled, total)[0]
     total = correlate([(-1, near), (1, ends)], [firsts[-1], seconds[1]], tabled, total)[0]
-    total, keep, give = correlate([(2, near)], [firsts[2]], tabled, total, HALVES[0])
+    values = [firsts[2], seconds[2][0]]
+    total, keep, give = correlate([(2, near, 1), (2, (0,), 1)], values, tabled, total, GROUPS[0])
     pair = keep + other_core(give)
-    total = correlate([(2, (0,))], [seconds[2][0]], tabled, total)[0]
+    total = correlate([(2, near, 0)], [firsts[2]], tabled, total)[0]
     total, pair = lax.optimization_barrier((total, pair))
-    both = pair + other_chip(pair)
-    placed = [both, other_core(both)]
-    _, keep, give = correlate([(2, (2,))], [seconds[2][1]], tabled, total, HALVES[1])
-    pair = keep + other_core(give)
-    both = pair + other_chip(pair)
-    placed += [both, other_core(both)]
+    far_pair = other_chip(pair)
+    values = [seconds[2][0], seconds[2][1]]
+    _, keep, give = correlate([(2, (0,), 0), (2, (2,))], values, tabled, total, GROUPS[1])
+    last = keep + other_core(give)
+    far_last = other_chip(last)
+    far_pair, far_last = lax.optimization_barrier((far_pair, far_last))
+    both, both_last = pair + far_pair, last + far_last
+    placed = [both, other_core(both), both_last, other_core(both_last)]
     return place(placed).reshape(CH, 4 * CH, LAGS)
 
 

time: 82.1 us -> 80.1 us (0.976)
  waiting for transfers between devices: 31.6 us -> 26.8 us
  starting transfers between devices: 23.2 us -> 26.4 us
    ppermute x2, waiting for transfers between devices: 9.9 us -> 6.83 us  [shards(): lax.ppermute(value, 'win', [(w, w ^ 2) for w in range(4)])]
    ppermute x9, waiting for transfers between devices: 6.19 us -> 3.15 us  [send(): return lax.ppermute(value, ('win', 'chan'), pairs)]
    ppermute x9, starting transfers between devices: 11.1 us -> 13.7 us  [send(): return lax.ppermute(value, ('win', 'chan'), pairs)]
    ppermute x2, starting transfers between devices: 0.3 us -> 1.87 us  [shards(): lax.ppermute(value, 'win', [(w, w ^ 2) for w in range(4)])]
    ppermute x4, waiting for transfers between devices: 2.42 us -> 3.75 us  [shards(): lax.ppermute(value, 'win', [(w, w ^ 1) for w in range(4)])]
    ppermute x4, starting transfers between devices: 8.43 us -> 7.55 us  [shards(): lax.ppermute(value, 'win', [(w, w ^ 1) for w in range(4)])]
  transfers between devices with their start and end apart: 19 -> 19, of which waited for: 7 -> 9; matrix products, arithmetic and copies ran while one was open for 0% -> 0% of each run, Pallas kernels for 22% -> 20%
where the time goes in v5:
time: 80.1 us; the launch traced here: 79.8 us
  waiting for transfers between devices  26.8 us (33%)
  starting transfers between devices  26.4 us (33%)
  Pallas kernels  20.4 us (25%)
  local copies, waits for them, and re-layouts  5.64 us (7%)
    pallas_call x6, Pallas kernels, correlate(): pl.pallas_call(functools.partial(correlate_kernel, steps, started, finish...  18.5 us
    ppermute x9, starting transfers between devices, send(): return lax.ppermute(value, ('win', 'chan'), pairs)  13.7 us
    ppermute x1, waiting for transfers between devices, shards(): lax.ppermute(mine, 'chan', [(8 * s + z, 8 * s + 4 + z) for s in range(4)...  13.1 us
    ppermute x4, starting transfers between devices, shards(): lax.ppermute(value, 'win', [(w, w ^ 1) for w in range(4)])  7.55 us
    ppermute x2, waiting for transfers between devices, shards(): lax.ppermute(value, 'win', [(w, w ^ 2) for w in range(4)])  6.83 us
    unnamed x6, local copies, waits for them, and re-layouts  5.6 us
    ppermute x4, waiting for transfers between devices, shards(): lax.ppermute(value, 'win', [(w, w ^ 1) for w in range(4)])  3.75 us
    ppermute x9, waiting for transfers between devices, send(): return lax.ppermute(value, ('win', 'chan'), pairs)  3.15 us
  transfers between devices with their start and end apart: 19, of which 9 were waited for; matrix products, arithmetic and copies ran while one was open for 0% of the time, Pallas kernels for 20%

profile of v5, /device:TPU:25, one launch (start us, length us, event | category | flops | bytes accessed | tf_op | source)
XLA Modules:
  0.0 79.8 jit_solution(1742969393747442805)
XLA Ops:
  0.0 1.2 %copy-done.2 = f32[1,2,16,8192]{3,2,1,0:T(8,128)S(1)} copy-done((f32[1,2,16,8192]{3,2,1,0:T(8,128)S(1)}, f32[1,2,16,8192]{3,2,1,0:T(8,128)}, u32[]{:S(2)}) %copy-start.2) | copy-done | bytes 1048600
  3.5 2.2 %copy-done = bf16[8,1024,256]{2,1,0:T(8,128)(2,1)S(1)} copy-done((bf16[8,1024,256]{2,1,0:T(8,128)(2,1)S(1)}, bf16[8,1024,256]{2,1,0:T(8,128)(2,1)}, u32[]{:S(2)}) %copy-start) | copy-done | bytes 4194328
  5.7 2.2 %copy-done.1 = bf16[8,1024,256]{2,1,0:T(8,128)(2,1)S(1)} copy-done((bf16[8,1024,256]{2,1,0:T(8,128)(2,1)S(1)}, bf16[8,1024,256]{2,1,0:T(8,128)(2,1)}, u32[]{:S(2)}) %copy-start.1) | copy-done | bytes 4194328
  8.6 1.3 %collective-permute-start.3 = (f32[2,4,16,512]{3,2,1,0:T(8,128)S(1)}, f32[2,4,16,512]{3,2,1,0:T(8,128)S(1)}, u32[]{:S(2)}, u32[]{:S(2)}) collective-permute-start(f32[2,4,16,512]{3,2,1,0:T(8,128)S(1)} %add_select_fusion), channel_id=1, source_target_pairs={{0,4},{1,5},{2,6},{3,7},{8,12},{9,13},{10,14},{11,15},{16,20},{17,... | collective-permute-start | bytes 786440 | tf_op jit(solution)/shard_map/ppermute | solution.py:211
  9.9 13.1 %collective-permute-done.3 = f32[2,4,16,512]{3,2,1,0:T(8,128)S(1)} collective-permute-done((f32[2,4,16,512]{3,2,1,0:T(8,128)S(1)}, f32[2,4,16,512]{3,2,1,0:T(8,128)S(1)}, u32[]{:S(2)}, u32[]{:S(2)}) %collective-permute-start.3) | collective-permute-done | bytes 262176 | tf_op jit(solution)/shard_map/ppermute | solution.py:211
  23.0 2.8 %collective-permute-start.8 = (f32[2,4,16,512]{3,2,1,0:T(8,128)S(1)}, f32[2,4,16,512]{3,2,1,0:T(8,128)S(1)}, u32[]{:S(2)}, u32[]{:S(2)}) collective-permute-start(f32[2,4,16,512]{3,2,1,0:T(8,128)S(1)} %broadcast_select_fusion), channel_id=1, source_target_pairs={{0,2},{1,3},{2,0},{3,1},{4,6},{5,7},{6,4},{7,5},{8,10},{9,11},{10,... | collective-permute-start | bytes 786440 | tf_op jit(solution)/shard_map/ppermute | solution.py:201
  26.2 2.4 %collective-permute-start.5 = (f32[2,4,16,512]{3,2,1,0:T(8,128)S(1)}, f32[2,4,16,512]{3,2,1,0:T(8,128)S(1)}, u32[]{:S(2)}, u32[]{:S(2)}) collective-permute-start(f32[2,4,16,512]{3,2,1,0:T(8,128)S(1)} %broadcast_select_fusion), channel_id=1, source_target_pairs={{0,3},{1,0},{2,1},{3,2},{4,7},{5,4},{6,5},{7,6},{8,11},{9,8},{10,9... | collective-permute-start | bytes 786440 | tf_op jit(solution)/shard_map/ppermute | solution.py:201
  28.5 1.3 %collective-permute-done.8 = f32[2,4,16,512]{3,2,1,0:T(8,128)S(1)} collective-permute-done((f32[2,4,16,512]{3,2,1,0:T(8,128)S(1)}, f32[2,4,16,512]{3,2,1,0:T(8,128)S(1)}, u32[]{:S(2)}, u32[]{:S(2)}) %collective-permute-start.8) | collective-permute-done | bytes 262176 | tf_op jit(solution)/shard_map/ppermute | solution.py:201
  29.9 2.1 %collective-permute-start.9 = (f32[2,2,4,16,512]{4,3,2,1,0:T(8,128)S(1)}, f32[2,2,4,16,512]{4,3,2,1,0:T(8,128)S(1)}, u32[]{:S(2)}, u32[]{:S(2)}) collective-permute-start(f32[2,2,4,16,512]{4,3,2,1,0:T(8,128)S(1)} %pad_maximum_fusion.1.refs_1_), channel_id=1, source_target_pairs={{0,24},{1,25},{2,26},{3,27},{4,28},{5,29},{6,30},{7,31},{8,0},{9,1... | collective-permute-start | bytes 1572872 | tf_op jit(solution)/shard_map/ppermute | solution.py:201
  33.2 3.4 %collective-permute-start.12 = (f32[2,2,4,16,512]{4,3,2,1,0:T(8,128)S(1)}, f32[2,2,4,16,512]{4,3,2,1,0:T(8,128)S(1)}, u32[]{:S(2)}, u32[]{:S(2)}) collective-permute-start(f32[2,2,4,16,512]{4,3,2,1,0:T(8,128)S(1)} %pad_maximum_fusion.1.refs_1_), channel_id=1, source_target_pairs={{0,8},{1,9},{2,10},{3,11},{4,12},{5,13},{6,14},{7,15},{8,16},{9,17... | collective-permute-start | bytes 1572872 | tf_op jit(solution)/shard_map/ppermute | solution.py:201
  36.5 4.8 %shard_map.39.refs_2_ = f32[4,16,16,256]{3,2,1,0:T(8,128)S(1)} custom-call(f32[8,4,16,512]{3,2,1,0:T(8,128)S(1)} %get-tuple-element.27.x_ref, bf16[8,1024,256]{2,1,0:T(8,128)(2,1)S(1)} %get-tuple-element.34.high_ref, bf16[8,1024,256]{2,1,0:T(8,128)(2,1)S(1)} %get-tuple-element.35.low_ref, f32[2,2,4,16,512]{4,3,2,1,0:T(8,128)S(1)} %pad_maximum_fusion.refs_0_, ...), custom_call_target="tpu_custom_call" | custom-call | flops 3221225472 | bytes 12582912 | tf_op jit(solution)/shard_map/pallas_call | solution.py:136
  41.4 2.7 %collective-permute-start.10 = (f32[2,2,4,16,512]{4,3,2,1,0:T(8,128)S(1)}, f32[2,2,4,16,512]{4,3,2,1,0:T(8,128)S(1)}, u32[]{:S(2)}, u32[]{:S(2)}) collective-permute-start(f32[2,2,4,16,512]{4,3,2,1,0:T(8,128)S(1)} %collective-permute-done.9.refs_1_), channel_id=1, source_target_pairs={{0,24},{1,25},{2,26},{3,27},{4,28},{5,29},{6,30},{7,31},{8,0},{9,1... | collective-permute-start | bytes 1572872 | tf_op jit(solution)/shard_map/ppermute | solution.py:201
  44.1 4.5 %shard_map.40.refs_2_ = f32[4,16,16,256]{3,2,1,0:T(8,128)S(1)} custom-call(f32[8,4,16,512]{3,2,1,0:T(8,128)S(1)} %get-tuple-element.27.x_ref, bf16[8,1024,256]{2,1,0:T(8,128)(2,1)S(1)} %get-tuple-element.34.high_ref, bf16[8,1024,256]{2,1,0:T(8,128)(2,1)S(1)} %get-tuple-element.35.low_ref, ...), custom_call_target="tpu_custom_call", output_to_operand_aliasing={{}: (5, {})} | custom-call | flops 3221225472 | bytes 12582912 | tf_op jit(solution)/shard_map/pallas_call | solution.py:136
  48.6 4.5 %shard_map.41.refs_2_ = f32[4,16,16,256]{3,2,1,0:T(8,128)S(1)} custom-call(f32[8,4,16,512]{3,2,1,0:T(8,128)S(1)} %get-tuple-element.27.x_ref, bf16[8,1024,256]{2,1,0:T(8,128)(2,1)S(1)} %get-tuple-element.34.high_ref, bf16[8,1024,256]{2,1,0:T(8,128)(2,1)S(1)} %get-tuple-element.35.low_ref, ...), custom_call_target="tpu_custom_call", output_to_operand_aliasing={{}: (5, {})} | custom-call | flops 3221225472 | bytes 12582912 | tf_op jit(solution)/shard_map/pallas_call | solution.py:136
  53.9 3.5 %shard_map.42 = (f32[4,16,16,256]{3,2,1,0:T(8,128)S(1)}, f32[3,8,16,256]{3,2,1,0:T(8,128)S(1)}, f32[3,8,16,256]{3,2,1,0:T(8,128)S(1)}) custom-call(f32[8,4,16,512]{3,2,1,0:T(8,128)S(1)} %get-tuple-element.27.x_ref, bf16[8,1024,256]{2,1,0:T(8,128)(2,1)S(1)} %get-tuple-element.34.high_ref, ...), custom_call_target="tpu_custom_call", output_to_operand_aliasing={{0}: (5, {})} | custom-call | flops 2415919104 | bytes 9437184 | tf_op jit(solution)/shard_map/pallas_call | solution.py:136
  57.4 3.8 %collective-permute-start.13 = (f32[3,8,16,256]{3,2,1,0:T(8,128)S(1)}, f32[3,8,16,256]{3,2,1,0:T(8,128)S(1)}, u32[]{:S(2)}, u32[]{:S(2)}) collective-permute-start(f32[3,8,16,256]{3,2,1,0:T(8,128)S(1)} %get-tuple-element.40), channel_id=1, source_target_pairs={{0,32},{32,0},{64,96},{96,64},{1,33},{33,1},{65,97},{97,65},{2,34}... | collective-permute-start | bytes 1179656 | tf_op jit(solution)/shard_map/ppermute | solution.py:203
  61.3 1.3 %collective-permute-done.13 = f32[3,8,16,256]{3,2,1,0:T(8,128)S(1)} collective-permute-done((f32[3,8,16,256]{3,2,1,0:T(8,128)S(1)}, f32[3,8,16,256]{3,2,1,0:T(8,128)S(1)}, u32[]{:S(2)}, u32[]{:S(2)}) %collective-permute-start.13) | collective-permute-done | bytes 393248 | tf_op jit(solution)/shard_map/ppermute | solution.py:203
  62.8 1.2 %shard_map.44 = (f32[4,16,16,256]{3,2,1,0:T(8,128)S(1)}, f32[1,8,16,256]{3,2,1,0:T(8,128)S(1)}, f32[1,8,16,256]{3,2,1,0:T(8,128)S(1)}) custom-call(f32[8,4,16,512]{3,2,1,0:T(8,128)S(1)} %get-tuple-element.27.x_ref, bf16[8,1024,256]{2,1,0:T(8,128)(2,1)S(1)} %get-tuple-element.34.high_ref, ...), custom_call_target="tpu_custom_call", output_to_operand_aliasing={{0}: (5, {})} | custom-call | flops 1610612736 | bytes 6291456 | tf_op jit(solution)/shard_map/pallas_call | solution.py:136
  64.0 1.9 %collective-permute-start.15 = (f32[1,8,16,256]{3,2,1,0:T(8,128)S(1)}, f32[1,8,16,256]{3,2,1,0:T(8,128)S(1)}, u32[]{:S(2)}, u32[]{:S(2)}) collective-permute-start(f32[1,8,16,256]{3,2,1,0:T(8,128)S(1)} %get-tuple-element.44), channel_id=1, source_target_pairs={{0,32},{32,0},{64,96},{96,64},{1,33},{33,1},{65,97},{97,65},{2,34}... | collective-permute-start | bytes 393224 | tf_op jit(solution)/shard_map/ppermute | solution.py:203
  66.9 1.8 %collective-permute-start.16 = (f32[1,8,16,256]{3,2,1,0:T(8,128)S(1)}, f32[1,8,16,256]{3,2,1,0:T(8,128)S(1)}, u32[]{:S(2)}, u32[]{:S(2)}) collective-permute-start(f32[1,8,16,256]{3,2,1,0:T(8,128)S(1)} %add.31), channel_id=1, source_target_pairs={{0,64},{32,96},{64,0},{96,32},{1,65},{33,97},{65,1},{97,33},{2,66}... | collective-permute-start | bytes 393224 | tf_op jit(solution)/shard_map/ppermute | solution.py:204
  68.7 6.8 %collective-permute-done.16 = f32[1,8,16,256]{3,2,1,0:T(8,128)S(1)} collective-permute-done((f32[1,8,16,256]{3,2,1,0:T(8,128)S(1)}, f32[1,8,16,256]{3,2,1,0:T(8,128)S(1)}, u32[]{:S(2)}, u32[]{:S(2)}) %collective-permute-start.16) | collective-permute-done | bytes 131104 | tf_op jit(solution)/shard_map/ppermute | solution.py:204
  75.6 1.7 %collective-permute-start.17 = (f32[3,8,16,256]{3,2,1,0:T(8,128)S(1)}, f32[3,8,16,256]{3,2,1,0:T(8,128)S(1)}, u32[]{:S(2)}, u32[]{:S(2)}) collective-permute-start(f32[3,8,16,256]{3,2,1,0:T(8,128)S(1)} %add.32.refs_0_), channel_id=1, source_target_pairs={{0,32},{32,0},{64,96},{96,64},{1,33},{33,1},{65,97},{97,65},{2,34}... | collective-permute-start | bytes 1179656 | tf_op jit(solution)/shard_map/ppermute | solution.py:203
  77.4 1.4 %collective-permute-done.18.refs_3_ = f32[1,8,16,256]{3,2,1,0:T(8,128)S(1)} collective-permute-done((f32[1,8,16,256]{3,2,1,0:T(8,128)S(1)}, f32[1,8,16,256]{3,2,1,0:T(8,128)S(1)}, u32[]{:S(2)}, u32[]{:S(2)}) %collective-permute-start.18) | collective-permute-done | bytes 131104 | tf_op jit(solution)/shard_map/ppermute | solution.py:203
  78.8 1.1 %shard_map.45 = f32[16,4,16,256]{3,2,1,0:T(8,128)} custom-call(f32[3,8,16,256]{3,2,1,0:T(8,128)S(1)} %add.32.refs_0_, f32[3,8,16,256]{3,2,1,0:T(8,128)S(1)} %collective-permute-done.17.refs_1_, f32[1,8,16,256]{3,2,1,0:T(8,128)S(1)} %add.33.refs_2_, f32[1,8,16,256]{3,2,1,0:T(8,128)S(1)} %collective-permute-done.18.refs_3_), custom_call_target="tpu_custom_call" | custom-call | tf_op jit(solution)/shard_map/pallas_call | solution.py:161
  (38 shorter events, 6.6 us)
Async XLA Ops:
  0.0 1.2 %copy-start.2 = (f32[1,2,16,8192]{3,2,1,0:T(8,128)S(1)}, f32[1,2,16,8192]{3,2,1,0:T(8,128)}, u32[]{:S(2)}) copy-start(f32[1,2,16,8192]{3,2,1,0:T(8,128)} %param.3) | copy-start | bytes 3145732
  1.5 7.0 %collective-permute-start = (f32[2,4,16,512]{3,2,1,0:T(8,128)S(1)}, f32[2,4,16,512]{3,2,1,0:T(8,128)S(1)}, u32[]{:S(2)}, u32[]{:S(2)}) collective-permute-start(f32[2,4,16,512]{3,2,1,0:T(8,128)S(1)} %get-tuple-element.29), channel_id=1, source_target_pairs={{0,1},{8,9},{16,17},{24,25},{32,33},{40,41},{48,49},{56,57},{64,65... | collective-permute-start | bytes 786440 | tf_op jit(solution)/shard_map/ppermute | solution.py:208
  2.1 6.3 %collective-permute-start.1 = (f32[2,4,16,512]{3,2,1,0:T(8,128)S(1)}, f32[2,4,16,512]{3,2,1,0:T(8,128)S(1)}, u32[]{:S(2)}, u32[]{:S(2)}) collective-permute-start(f32[2,4,16,512]{3,2,1,0:T(8,128)S(1)} %get-tuple-element.30), channel_id=1, source_target_pairs={{0,2},{8,10},{16,18},{24,26},{32,34},{40,42},{48,50},{56,58},{64,6... | collective-permute-start | bytes 786440 | tf_op jit(solution)/shard_map/ppermute | solution.py:208
  2.8 5.7 %collective-permute-start.2 = (f32[2,4,16,512]{3,2,1,0:T(8,128)S(1)}, f32[2,4,16,512]{3,2,1,0:T(8,128)S(1)}, u32[]{:S(2)}, u32[]{:S(2)}) collective-permute-start(f32[2,4,16,512]{3,2,1,0:T(8,128)S(1)} %get-tuple-element.31), channel_id=1, source_target_pairs={{0,3},{8,11},{16,19},{24,27},{32,35},{40,43},{48,51},{56,59},{64,6... | collective-permute-start | bytes 786440 | tf_op jit(solution)/shard_map/ppermute | solution.py:208
  3.5 2.2 %copy-start = (bf16[8,1024,256]{2,1,0:T(8,128)(2,1)S(1)}, bf16[8,1024,256]{2,1,0:T(8,128)(2,1)}, u32[]{:S(2)}) copy-start(bf16[8,1024,256]{2,1,0:T(8,128)(2,1)} %constant.43.clone.high_ref) | copy-start | bytes 12582916
  5.7 2.2 %copy-start.1 = (bf16[8,1024,256]{2,1,0:T(8,128)(2,1)S(1)}, bf16[8,1024,256]{2,1,0:T(8,128)(2,1)}, u32[]{:S(2)}) copy-start(bf16[8,1024,256]{2,1,0:T(8,128)(2,1)} %constant.44.clone.low_ref) | copy-start | bytes 12582916
  8.6 14.4 %collective-permute-start.3 = (f32[2,4,16,512]{3,2,1,0:T(8,128)S(1)}, f32[2,4,16,512]{3,2,1,0:T(8,128)S(1)}, u32[]{:S(2)}, u32[]{:S(2)}) collective-permute-start(f32[2,4,16,512]{3,2,1,0:T(8,128)S(1)} %add_select_fusion), channel_id=1, source_target_pairs={{0,4},{1,5},{2,6},{3,7},{8,12},{9,13},{10,14},{11,15},{16,20},{17,... | collective-permute-start | bytes 786440 | tf_op jit(solution)/shard_map/ppermute | solution.py:211
  23.0 6.8 %collective-permute-start.8 = (f32[2,4,16,512]{3,2,1,0:T(8,128)S(1)}, f32[2,4,16,512]{3,2,1,0:T(8,128)S(1)}, u32[]{:S(2)}, u32[]{:S(2)}) collective-permute-start(f32[2,4,16,512]{3,2,1,0:T(8,128)S(1)} %broadcast_select_fusion), channel_id=1, source_target_pairs={{0,2},{1,3},{2,0},{3,1},{4,6},{5,7},{6,4},{7,5},{8,10},{9,11},{10,... | collective-permute-start | bytes 786440 | tf_op jit(solution)/shard_map/ppermute | solution.py:201
  25.9 7.1 %collective-permute-start.4 = (f32[2,4,16,512]{3,2,1,0:T(8,128)S(1)}, f32[2,4,16,512]{3,2,1,0:T(8,128)S(1)}, u32[]{:S(2)}, u32[]{:S(2)}) collective-permute-start(f32[2,4,16,512]{3,2,1,0:T(8,128)S(1)} %broadcast_select_fusion), channel_id=1, source_target_pairs={{0,1},{1,2},{2,3},{3,0},{4,5},{5,6},{6,7},{7,4},{8,9},{9,10},{10,1... | collective-permute-start | bytes 786440 | tf_op jit(solution)/shard_map/ppermute | solution.py:201
  26.2 6.9 %collective-permute-start.5 = (f32[2,4,16,512]{3,2,1,0:T(8,128)S(1)}, f32[2,4,16,512]{3,2,1,0:T(8,128)S(1)}, u32[]{:S(2)}, u32[]{:S(2)}) collective-permute-start(f32[2,4,16,512]{3,2,1,0:T(8,128)S(1)} %broadcast_select_fusion), channel_id=1, source_target_pairs={{0,3},{1,0},{2,1},{3,2},{4,7},{5,4},{6,5},{7,6},{8,11},{9,8},{10,9... | collective-permute-start | bytes 786440 | tf_op jit(solution)/shard_map/ppermute | solution.py:201
  29.9 11.4 %collective-permute-start.9 = (f32[2,2,4,16,512]{4,3,2,1,0:T(8,128)S(1)}, f32[2,2,4,16,512]{4,3,2,1,0:T(8,128)S(1)}, u32[]{:S(2)}, u32[]{:S(2)}) collective-permute-start(f32[2,2,4,16,512]{4,3,2,1,0:T(8,128)S(1)} %pad_maximum_fusion.1.refs_1_), channel_id=1, source_target_pairs={{0,24},{1,25},{2,26},{3,27},{4,28},{5,29},{6,30},{7,31},{8,0},{9,1... | collective-permute-start | bytes 1572872 | tf_op jit(solution)/shard_map/ppermute | solution.py:201
  33.1 11.0 %collective-permute-start.6 = (f32[2,2,4,16,512]{4,3,2,1,0:T(8,128)S(1)}, f32[2,2,4,16,512]{4,3,2,1,0:T(8,128)S(1)}, u32[]{:S(2)}, u32[]{:S(2)}) collective-permute-start(f32[2,2,4,16,512]{4,3,2,1,0:T(8,128)S(1)} %pad_maximum_fusion.refs_0_), channel_id=1, source_target_pairs={{0,8},{1,9},{2,10},{3,11},{4,12},{5,13},{6,14},{7,15},{8,16},{9,17... | collective-permute-start | bytes 1572872 | tf_op jit(solution)/shard_map/ppermute | solution.py:201
  33.2 15.4 %collective-permute-start.12 = (f32[2,2,4,16,512]{4,3,2,1,0:T(8,128)S(1)}, f32[2,2,4,16,512]{4,3,2,1,0:T(8,128)S(1)}, u32[]{:S(2)}, u32[]{:S(2)}) collective-permute-start(f32[2,2,4,16,512]{4,3,2,1,0:T(8,128)S(1)} %pad_maximum_fusion.1.refs_1_), channel_id=1, source_target_pairs={{0,8},{1,9},{2,10},{3,11},{4,12},{5,13},{6,14},{7,15},{8,16},{9,17... | collective-permute-start | bytes 1572872 | tf_op jit(solution)/shard_map/ppermute | solution.py:201
  36.5 12.0 %collective-permute-start.11 = (f32[2,2,4,16,512]{4,3,2,1,0:T(8,128)S(1)}, f32[2,2,4,16,512]{4,3,2,1,0:T(8,128)S(1)}, u32[]{:S(2)}, u32[]{:S(2)}) collective-permute-start(f32[2,2,4,16,512]{4,3,2,1,0:T(8,128)S(1)} %pad_maximum_fusion.refs_0_), channel_id=1, source_target_pairs={{0,24},{1,25},{2,26},{3,27},{4,28},{5,29},{6,30},{7,31},{8,0},{9,1... | collective-permute-start | bytes 1572872 | tf_op jit(solution)/shard_map/ppermute | solution.py:201
  41.4 11.7 %collective-permute-start.10 = (f32[2,2,4,16,512]{4,3,2,1,0:T(8,128)S(1)}, f32[2,2,4,16,512]{4,3,2,1,0:T(8,128)S(1)}, u32[]{:S(2)}, u32[]{:S(2)}) collective-permute-start(f32[2,2,4,16,512]{4,3,2,1,0:T(8,128)S(1)} %collective-permute-done.9.refs_1_), channel_id=1, source_target_pairs={{0,24},{1,25},{2,26},{3,27},{4,28},{5,29},{6,30},{7,31},{8,0},{9,1... | collective-permute-start | bytes 1572872 | tf_op jit(solution)/shard_map/ppermute | solution.py:201
  44.1 9.9 %collective-permute-start.7 = (f32[2,2,4,16,512]{4,3,2,1,0:T(8,128)S(1)}, f32[2,2,4,16,512]{4,3,2,1,0:T(8,128)S(1)}, u32[]{:S(2)}, u32[]{:S(2)}) collective-permute-start(f32[2,2,4,16,512]{4,3,2,1,0:T(8,128)S(1)} %collective-permute-done.6.refs_0_), channel_id=1, source_target_pairs={{0,8},{1,9},{2,10},{3,11},{4,12},{5,13},{6,14},{7,15},{8,16},{9,17... | collective-permute-start | bytes 1572872 | tf_op jit(solution)/shard_map/ppermute | solution.py:201
  57.4 5.2 %collective-permute-start.13 = (f32[3,8,16,256]{3,2,1,0:T(8,128)S(1)}, f32[3,8,16,256]{3,2,1,0:T(8,128)S(1)}, u32[]{:S(2)}, u32[]{:S(2)}) collective-permute-start(f32[3,8,16,256]{3,2,1,0:T(8,128)S(1)} %get-tuple-element.40), channel_id=1, source_target_pairs={{0,32},{32,0},{64,96},{96,64},{1,33},{33,1},{65,97},{97,65},{2,34}... | collective-permute-start | bytes 1179656 | tf_op jit(solution)/shard_map/ppermute | solution.py:203
  62.7 12.8 %collective-permute-start.14 = (f32[3,8,16,256]{3,2,1,0:T(8,128)S(1)}, f32[3,8,16,256]{3,2,1,0:T(8,128)S(1)}, u32[]{:S(2)}, u32[]{:S(2)}) collective-permute-start(f32[3,8,16,256]{3,2,1,0:T(8,128)S(1)} %add.30), channel_id=1, source_target_pairs={{0,64},{32,96},{64,0},{96,32},{1,65},{33,97},{65,1},{97,33},{2,66}... | collective-permute-start | bytes 1179656 | tf_op jit(solution)/shard_map/ppermute | solution.py:204
  64.0 2.9 %collective-permute-start.15 = (f32[1,8,16,256]{3,2,1,0:T(8,128)S(1)}, f32[1,8,16,256]{3,2,1,0:T(8,128)S(1)}, u32[]{:S(2)}, u32[]{:S(2)}) collective-permute-start(f32[1,8,16,256]{3,2,1,0:T(8,128)S(1)} %get-tuple-element.44), channel_id=1, source_target_pairs={{0,32},{32,0},{64,96},{96,64},{1,33},{33,1},{65,97},{97,65},{2,34}... | collective-permute-start | bytes 393224 | tf_op jit(solution)/shard_map/ppermute | solution.py:203
  66.9 8.6 %collective-permute-start.16 = (f32[1,8,16,256]{3,2,1,0:T(8,128)S(1)}, f32[1,8,16,256]{3,2,1,0:T(8,128)S(1)}, u32[]{:S(2)}, u32[]{:S(2)}) collective-permute-start(f32[1,8,16,256]{3,2,1,0:T(8,128)S(1)} %add.31), channel_id=1, source_target_pairs={{0,64},{32,96},{64,0},{96,32},{1,65},{33,97},{65,1},{97,33},{2,66}... | collective-permute-start | bytes 393224 | tf_op jit(solution)/shard_map/ppermute | solution.py:204
  75.6 3.2 %collective-permute-start.17 = (f32[3,8,16,256]{3,2,1,0:T(8,128)S(1)}, f32[3,8,16,256]{3,2,1,0:T(8,128)S(1)}, u32[]{:S(2)}, u32[]{:S(2)}) collective-permute-start(f32[3,8,16,256]{3,2,1,0:T(8,128)S(1)} %add.32.refs_0_), channel_id=1, source_target_pairs={{0,32},{32,0},{64,96},{96,64},{1,33},{33,1},{65,97},{97,65},{2,34}... | collective-permute-start | bytes 1179656 | tf_op jit(solution)/shard_map/ppermute | solution.py:203
  77.3 1.5 %collective-permute-start.18 = (f32[1,8,16,256]{3,2,1,0:T(8,128)S(1)}, f32[1,8,16,256]{3,2,1,0:T(8,128)S(1)}, u32[]{:S(2)}, u32[]{:S(2)}) collective-permute-start(f32[1,8,16,256]{3,2,1,0:T(8,128)S(1)} %add.33.refs_2_), channel_id=1, source_target_pairs={{0,32},{32,0},{64,96},{96,64},{1,33},{33,1},{65,97},{97,65},{2,34}... | collective-permute-start | bytes 393224 | tf_op jit(solution)/shard_map/ppermute | solution.py:203

commit v6 on v5

--- a/solution.py
+++ b/solution.py
@@ -76,6 +76,7 @@
 
         def add(g_ref=g_ref, far=far, nears=nears):
             for place, near in enumerate(nears):
+                near = jnp.where(jnp.where(core == 0, at_z, at_x) % 2 == 0, -near, near)
                 block = (at_x + 4 - jnp.where(core == 0, far, near)) % 4
                 bins = (at_z + 4 - jnp.where(core == 0, near, far)) % 4
                 first = jnp.logical_and(lane == 0, bins == 0)
@@ -210,7 +211,11 @@
     mine, high, low = lax.optimization_barrier((mine, high, low))
     over = lax.ppermute(mine, "chan", [(8 * s + z, 8 * s + 4 + z) for s in range(4) for z in range(4)])
     mine = jnp.where(at_near, mine, over)
-    came = {d: send(mine, d, over_z, over_x) for d in (1, -1, 2)}
+    swap = lambda at, d: at + d if at % 2 == 0 else at - d
+    swap_x = lambda c, d: swap(c // 8, d) % 4 * 8 + c % 8
+    swap_z = lambda c, d: c // 4 * 4 + swap(c % 4, d) % 4
+    came = {2: send(mine, 2, over_z, over_x)}
+    came.update({d: send(mine, d, swap_z, swap_x) for d in (1, -1)})
     first = jnp.stack([came[1], came[-1]])
     second = jnp.stack([mine, came[2]])
     firsts, seconds = {0: first}, {0: second}

time: 80.1 us -> 79.2 us (0.989)
  starting transfers between devices: 26.4 us -> 22.6 us
  waiting for transfers between devices: 26.8 us -> 29 us
    ppermute x9, starting transfers between devices: 13.7 us -> 11 us  [send(): return lax.ppermute(value, ('win', 'chan'), pairs)]
    ppermute x9, waiting for transfers between devices: 3.15 us -> 5.32 us  [send(): return lax.ppermute(value, ('win', 'chan'), pairs)]
    ppermute x4, starting transfers between devices: 7.55 us -> 6.37 us  [shards(): lax.ppermute(value, 'win', [(w, w ^ 1) for w in range(4)])]
  transfers between devices with their start and end apart: 19 -> 19, of which waited for: 9 -> 9; matrix products, arithmetic and copies ran while one was open for 0% -> 0% of each run, Pallas kernels for 20% -> 21%
where the time goes in v6:
time: 79.2 us; the launch traced here: 78.7 us
  waiting for transfers between devices  29 us (37%)
  starting transfers between devices  22.6 us (29%)
  Pallas kernels  20.9 us (26%)
  local copies, waits for them, and re-layouts  5.64 us (7%)
    pallas_call x6, Pallas kernels, correlate(): pl.pallas_call(functools.partial(correlate_kernel, steps, started, finish...  19.1 us
    ppermute x1, waiting for transfers between devices, shards(): lax.ppermute(mine, 'chan', [(8 * s + z, 8 * s + 4 + z) for s in range(4)...  13.1 us
    ppermute x9, starting transfers between devices, send(): return lax.ppermute(value, ('win', 'chan'), pairs)  11 us
    ppermute x2, waiting for transfers between devices, shards(): lax.ppermute(value, 'win', [(w, w ^ 2) for w in range(4)])  6.82 us
    ppermute x4, starting transfers between devices, shards(): lax.ppermute(value, 'win', [(w, w ^ 1) for w in range(4)])  6.37 us
    unnamed x6, local copies, waits for them, and re-layouts  5.6 us
    ppermute x9, waiting for transfers between devices, send(): return lax.ppermute(value, ('win', 'chan'), pairs)  5.32 us
    ppermute x4, waiting for transfers between devices, shards(): lax.ppermute(value, 'win', [(w, w ^ 1) for w in range(4)])  3.75 us
  transfers between devices with their start and end apart: 19, of which 9 were waited for; matrix products, arithmetic and copies ran while one was open for 0% of the time, Pallas kernels for 21%

profile of v6, /device:TPU:25, one launch (start us, length us, event | category | flops | bytes accessed | tf_op | source)
XLA Modules:
  0.0 78.7 jit_solution(6732447816908492577)
XLA Ops:
  0.0 1.2 %copy-done.2 = f32[1,2,16,8192]{3,2,1,0:T(8,128)S(1)} copy-done((f32[1,2,16,8192]{3,2,1,0:T(8,128)S(1)}, f32[1,2,16,8192]{3,2,1,0:T(8,128)}, u32[]{:S(2)}) %copy-start.2) | copy-done | bytes 1048600
  3.5 2.2 %copy-done = bf16[8,1024,256]{2,1,0:T(8,128)(2,1)S(1)} copy-done((bf16[8,1024,256]{2,1,0:T(8,128)(2,1)S(1)}, bf16[8,1024,256]{2,1,0:T(8,128)(2,1)}, u32[]{:S(2)}) %copy-start) | copy-done | bytes 4194328
  5.7 2.2 %copy-done.1 = bf16[8,1024,256]{2,1,0:T(8,128)(2,1)S(1)} copy-done((bf16[8,1024,256]{2,1,0:T(8,128)(2,1)S(1)}, bf16[8,1024,256]{2,1,0:T(8,128)(2,1)}, u32[]{:S(2)}) %copy-start.1) | copy-done | bytes 4194328
  8.6 1.3 %collective-permute-start.3 = (f32[2,4,16,512]{3,2,1,0:T(8,128)S(1)}, f32[2,4,16,512]{3,2,1,0:T(8,128)S(1)}, u32[]{:S(2)}, u32[]{:S(2)}) collective-permute-start(f32[2,4,16,512]{3,2,1,0:T(8,128)S(1)} %add_select_fusion), channel_id=1, source_target_pairs={{0,4},{1,5},{2,6},{3,7},{8,12},{9,13},{10,14},{11,15},{16,20},{17,... | collective-permute-start | bytes 786440 | tf_op jit(solution)/shard_map/ppermute | solution.py:212
  9.9 13.1 %collective-permute-done.3 = f32[2,4,16,512]{3,2,1,0:T(8,128)S(1)} collective-permute-done((f32[2,4,16,512]{3,2,1,0:T(8,128)S(1)}, f32[2,4,16,512]{3,2,1,0:T(8,128)S(1)}, u32[]{:S(2)}, u32[]{:S(2)}) %collective-permute-start.3) | collective-permute-done | bytes 262176 | tf_op jit(solution)/shard_map/ppermute | solution.py:212
  23.0 2.8 %collective-permute-start.8 = (f32[2,4,16,512]{3,2,1,0:T(8,128)S(1)}, f32[2,4,16,512]{3,2,1,0:T(8,128)S(1)}, u32[]{:S(2)}, u32[]{:S(2)}) collective-permute-start(f32[2,4,16,512]{3,2,1,0:T(8,128)S(1)} %broadcast_select_fusion), channel_id=1, source_target_pairs={{0,2},{1,3},{2,0},{3,1},{4,6},{5,7},{6,4},{7,5},{8,10},{9,11},{10,... | collective-permute-start | bytes 786440 | tf_op jit(solution)/shard_map/ppermute | solution.py:202
  26.7 3.1 %collective-permute-done.8 = f32[2,4,16,512]{3,2,1,0:T(8,128)S(1)} collective-permute-done((f32[2,4,16,512]{3,2,1,0:T(8,128)S(1)}, f32[2,4,16,512]{3,2,1,0:T(8,128)S(1)}, u32[]{:S(2)}, u32[]{:S(2)}) %collective-permute-start.8) | collective-permute-done | bytes 262176 | tf_op jit(solution)/shard_map/ppermute | solution.py:202
  29.9 2.1 %collective-permute-start.9 = (f32[2,2,4,16,512]{4,3,2,1,0:T(8,128)S(1)}, f32[2,2,4,16,512]{4,3,2,1,0:T(8,128)S(1)}, u32[]{:S(2)}, u32[]{:S(2)}) collective-permute-start(f32[2,2,4,16,512]{4,3,2,1,0:T(8,128)S(1)} %pad_maximum_fusion.1.refs_1_), channel_id=1, source_target_pairs={{0,24},{1,25},{2,26},{3,27},{4,28},{5,29},{6,30},{7,31},{8,0},{9,1... | collective-permute-start | bytes 1572872 | tf_op jit(solution)/shard_map/ppermute | solution.py:202
  32.0 1.1 %collective-permute-done.4 = f32[2,4,16,512]{3,2,1,0:T(8,128)S(1)} collective-permute-done((f32[2,4,16,512]{3,2,1,0:T(8,128)S(1)}, f32[2,4,16,512]{3,2,1,0:T(8,128)S(1)}, u32[]{:S(2)}, u32[]{:S(2)}) %collective-permute-start.4) | collective-permute-done | bytes 262176 | tf_op jit(solution)/shard_map/ppermute | solution.py:202
  33.2 3.4 %collective-permute-start.12 = (f32[2,2,4,16,512]{4,3,2,1,0:T(8,128)S(1)}, f32[2,2,4,16,512]{4,3,2,1,0:T(8,128)S(1)}, u32[]{:S(2)}, u32[]{:S(2)}) collective-permute-start(f32[2,2,4,16,512]{4,3,2,1,0:T(8,128)S(1)} %pad_maximum_fusion.1.refs_1_), channel_id=1, source_target_pairs={{0,8},{1,9},{2,10},{3,11},{4,12},{5,13},{6,14},{7,15},{8,16},{9,17... | collective-permute-start | bytes 1572872 | tf_op jit(solution)/shard_map/ppermute | solution.py:202
  36.6 4.9 %shard_map.39.refs_2_ = f32[4,16,16,256]{3,2,1,0:T(8,128)S(1)} custom-call(f32[8,4,16,512]{3,2,1,0:T(8,128)S(1)} %get-tuple-element.27.x_ref, bf16[8,1024,256]{2,1,0:T(8,128)(2,1)S(1)} %get-tuple-element.34.high_ref, bf16[8,1024,256]{2,1,0:T(8,128)(2,1)S(1)} %get-tuple-element.35.low_ref, f32[2,2,4,16,512]{4,3,2,1,0:T(8,128)S(1)} %pad_maximum_fusion.refs_0_, ...), custom_call_target="tpu_custom_call" | custom-call | flops 3221225472 | bytes 12582912 | tf_op jit(solution)/shard_map/pallas_call | solution.py:137
  41.5 1.2 %collective-permute-start.10 = (f32[2,2,4,16,512]{4,3,2,1,0:T(8,128)S(1)}, f32[2,2,4,16,512]{4,3,2,1,0:T(8,128)S(1)}, u32[]{:S(2)}, u32[]{:S(2)}) collective-permute-start(f32[2,2,4,16,512]{4,3,2,1,0:T(8,128)S(1)} %collective-permute-done.9.refs_1_), channel_id=1, source_target_pairs={{0,24},{1,25},{2,26},{3,27},{4,28},{5,29},{6,30},{7,31},{8,0},{9,1... | collective-permute-start | bytes 1572872 | tf_op jit(solution)/shard_map/ppermute | solution.py:202
  43.2 4.8 %shard_map.40.refs_2_ = f32[4,16,16,256]{3,2,1,0:T(8,128)S(1)} custom-call(f32[8,4,16,512]{3,2,1,0:T(8,128)S(1)} %get-tuple-element.27.x_ref, bf16[8,1024,256]{2,1,0:T(8,128)(2,1)S(1)} %get-tuple-element.34.high_ref, bf16[8,1024,256]{2,1,0:T(8,128)(2,1)S(1)} %get-tuple-element.35.low_ref, ...), custom_call_target="tpu_custom_call", output_to_operand_aliasing={{}: (5, {})} | custom-call | flops 3221225472 | bytes 12582912 | tf_op jit(solution)/shard_map/pallas_call | solution.py:137
  48.4 4.8 %shard_map.41.refs_2_ = f32[4,16,16,256]{3,2,1,0:T(8,128)S(1)} custom-call(f32[8,4,16,512]{3,2,1,0:T(8,128)S(1)} %get-tuple-element.27.x_ref, bf16[8,1024,256]{2,1,0:T(8,128)(2,1)S(1)} %get-tuple-element.34.high_ref, bf16[8,1024,256]{2,1,0:T(8,128)(2,1)S(1)} %get-tuple-element.35.low_ref, ...), custom_call_target="tpu_custom_call", output_to_operand_aliasing={{}: (5, {})} | custom-call | flops 3221225472 | bytes 12582912 | tf_op jit(solution)/shard_map/pallas_call | solution.py:137
  54.0 3.5 %shard_map.42 = (f32[4,16,16,256]{3,2,1,0:T(8,128)S(1)}, f32[3,8,16,256]{3,2,1,0:T(8,128)S(1)}, f32[3,8,16,256]{3,2,1,0:T(8,128)S(1)}) custom-call(f32[8,4,16,512]{3,2,1,0:T(8,128)S(1)} %get-tuple-element.27.x_ref, bf16[8,1024,256]{2,1,0:T(8,128)(2,1)S(1)} %get-tuple-element.34.high_ref, ...), custom_call_target="tpu_custom_call", output_to_operand_aliasing={{0}: (5, {})} | custom-call | flops 2415919104 | bytes 9437184 | tf_op jit(solution)/shard_map/pallas_call | solution.py:137
  57.5 2.7 %collective-permute-start.13 = (f32[3,8,16,256]{3,2,1,0:T(8,128)S(1)}, f32[3,8,16,256]{3,2,1,0:T(8,128)S(1)}, u32[]{:S(2)}, u32[]{:S(2)}) collective-permute-start(f32[3,8,16,256]{3,2,1,0:T(8,128)S(1)} %get-tuple-element.40), channel_id=1, source_target_pairs={{0,32},{32,0},{64,96},{96,64},{1,33},{33,1},{65,97},{97,65},{2,34}... | collective-permute-start | bytes 1179656 | tf_op jit(solution)/shard_map/ppermute | solution.py:204
  60.1 1.3 %collective-permute-done.13 = f32[3,8,16,256]{3,2,1,0:T(8,128)S(1)} collective-permute-done((f32[3,8,16,256]{3,2,1,0:T(8,128)S(1)}, f32[3,8,16,256]{3,2,1,0:T(8,128)S(1)}, u32[]{:S(2)}, u32[]{:S(2)}) %collective-permute-start.13) | collective-permute-done | bytes 393248 | tf_op jit(solution)/shard_map/ppermute | solution.py:204
  61.6 1.2 %shard_map.44 = (f32[4,16,16,256]{3,2,1,0:T(8,128)S(1)}, f32[1,8,16,256]{3,2,1,0:T(8,128)S(1)}, f32[1,8,16,256]{3,2,1,0:T(8,128)S(1)}) custom-call(f32[8,4,16,512]{3,2,1,0:T(8,128)S(1)} %get-tuple-element.27.x_ref, bf16[8,1024,256]{2,1,0:T(8,128)(2,1)S(1)} %get-tuple-element.34.high_ref, ...), custom_call_target="tpu_custom_call", output_to_operand_aliasing={{0}: (5, {})} | custom-call | flops 1610612736 | bytes 6291456 | tf_op jit(solution)/shard_map/pallas_call | solution.py:137
  62.8 1.9 %collective-permute-start.15 = (f32[1,8,16,256]{3,2,1,0:T(8,128)S(1)}, f32[1,8,16,256]{3,2,1,0:T(8,128)S(1)}, u32[]{:S(2)}, u32[]{:S(2)}) collective-permute-start(f32[1,8,16,256]{3,2,1,0:T(8,128)S(1)} %get-tuple-element.44), channel_id=1, source_target_pairs={{0,32},{32,0},{64,96},{96,64},{1,33},{33,1},{65,97},{97,65},{2,34}... | collective-permute-start | bytes 393224 | tf_op jit(solution)/shard_map/ppermute | solution.py:204
  65.8 1.8 %collective-permute-start.16 = (f32[1,8,16,256]{3,2,1,0:T(8,128)S(1)}, f32[1,8,16,256]{3,2,1,0:T(8,128)S(1)}, u32[]{:S(2)}, u32[]{:S(2)}) collective-permute-start(f32[1,8,16,256]{3,2,1,0:T(8,128)S(1)} %add.31), channel_id=1, source_target_pairs={{0,64},{32,96},{64,0},{96,32},{1,65},{33,97},{65,1},{97,33},{2,66}... | collective-permute-start | bytes 393224 | tf_op jit(solution)/shard_map/ppermute | solution.py:205
  67.5 6.8 %collective-permute-done.16 = f32[1,8,16,256]{3,2,1,0:T(8,128)S(1)} collective-permute-done((f32[1,8,16,256]{3,2,1,0:T(8,128)S(1)}, f32[1,8,16,256]{3,2,1,0:T(8,128)S(1)}, u32[]{:S(2)}, u32[]{:S(2)}) %collective-permute-start.16) | collective-permute-done | bytes 131104 | tf_op jit(solution)/shard_map/ppermute | solution.py:205
  74.4 1.7 %collective-permute-start.17 = (f32[3,8,16,256]{3,2,1,0:T(8,128)S(1)}, f32[3,8,16,256]{3,2,1,0:T(8,128)S(1)}, u32[]{:S(2)}, u32[]{:S(2)}) collective-permute-start(f32[3,8,16,256]{3,2,1,0:T(8,128)S(1)} %add.32.refs_0_), channel_id=1, source_target_pairs={{0,32},{32,0},{64,96},{96,64},{1,33},{33,1},{65,97},{97,65},{2,34}... | collective-permute-start | bytes 1179656 | tf_op jit(solution)/shard_map/ppermute | solution.py:204
  76.2 1.4 %collective-permute-done.18.refs_3_ = f32[1,8,16,256]{3,2,1,0:T(8,128)S(1)} collective-permute-done((f32[1,8,16,256]{3,2,1,0:T(8,128)S(1)}, f32[1,8,16,256]{3,2,1,0:T(8,128)S(1)}, u32[]{:S(2)}, u32[]{:S(2)}) %collective-permute-start.18) | collective-permute-done | bytes 131104 | tf_op jit(solution)/shard_map/ppermute | solution.py:204
  77.6 1.1 %shard_map.45 = f32[16,4,16,256]{3,2,1,0:T(8,128)} custom-call(f32[3,8,16,256]{3,2,1,0:T(8,128)S(1)} %add.32.refs_0_, f32[3,8,16,256]{3,2,1,0:T(8,128)S(1)} %collective-permute-done.17.refs_1_, f32[1,8,16,256]{3,2,1,0:T(8,128)S(1)} %add.33.refs_2_, f32[1,8,16,256]{3,2,1,0:T(8,128)S(1)} %collective-permute-done.18.refs_3_), custom_call_target="tpu_custom_call" | custom-call | tf_op jit(solution)/shard_map/pallas_call | solution.py:162
  (38 shorter events, 7.1 us)
Async XLA Ops:
  0.0 1.2 %copy-start.2 = (f32[1,2,16,8192]{3,2,1,0:T(8,128)S(1)}, f32[1,2,16,8192]{3,2,1,0:T(8,128)}, u32[]{:S(2)}) copy-start(f32[1,2,16,8192]{3,2,1,0:T(8,128)} %param.3) | copy-start | bytes 3145732
  1.5 7.0 %collective-permute-start = (f32[2,4,16,512]{3,2,1,0:T(8,128)S(1)}, f32[2,4,16,512]{3,2,1,0:T(8,128)S(1)}, u32[]{:S(2)}, u32[]{:S(2)}) collective-permute-start(f32[2,4,16,512]{3,2,1,0:T(8,128)S(1)} %get-tuple-element.29), channel_id=1, source_target_pairs={{0,1},{8,9},{16,17},{24,25},{32,33},{40,41},{48,49},{56,57},{64,65... | collective-permute-start | bytes 786440 | tf_op jit(solution)/shard_map/ppermute | solution.py:209
  2.1 6.3 %collective-permute-start.1 = (f32[2,4,16,512]{3,2,1,0:T(8,128)S(1)}, f32[2,4,16,512]{3,2,1,0:T(8,128)S(1)}, u32[]{:S(2)}, u32[]{:S(2)}) collective-permute-start(f32[2,4,16,512]{3,2,1,0:T(8,128)S(1)} %get-tuple-element.30), channel_id=1, source_target_pairs={{0,2},{8,10},{16,18},{24,26},{32,34},{40,42},{48,50},{56,58},{64,6... | collective-permute-start | bytes 786440 | tf_op jit(solution)/shard_map/ppermute | solution.py:209
  2.8 5.7 %collective-permute-start.2 = (f32[2,4,16,512]{3,2,1,0:T(8,128)S(1)}, f32[2,4,16,512]{3,2,1,0:T(8,128)S(1)}, u32[]{:S(2)}, u32[]{:S(2)}) collective-permute-start(f32[2,4,16,512]{3,2,1,0:T(8,128)S(1)} %get-tuple-element.31), channel_id=1, source_target_pairs={{0,3},{8,11},{16,19},{24,27},{32,35},{40,43},{48,51},{56,59},{64,6... | collective-permute-start | bytes 786440 | tf_op jit(solution)/shard_map/ppermute | solution.py:209
  3.5 2.2 %copy-start = (bf16[8,1024,256]{2,1,0:T(8,128)(2,1)S(1)}, bf16[8,1024,256]{2,1,0:T(8,128)(2,1)}, u32[]{:S(2)}) copy-start(bf16[8,1024,256]{2,1,0:T(8,128)(2,1)} %constant.43.clone.high_ref) | copy-start | bytes 12582916
  5.7 2.2 %copy-start.1 = (bf16[8,1024,256]{2,1,0:T(8,128)(2,1)S(1)}, bf16[8,1024,256]{2,1,0:T(8,128)(2,1)}, u32[]{:S(2)}) copy-start(bf16[8,1024,256]{2,1,0:T(8,128)(2,1)} %constant.44.clone.low_ref) | copy-start | bytes 12582916
  8.6 14.4 %collective-permute-start.3 = (f32[2,4,16,512]{3,2,1,0:T(8,128)S(1)}, f32[2,4,16,512]{3,2,1,0:T(8,128)S(1)}, u32[]{:S(2)}, u32[]{:S(2)}) collective-permute-start(f32[2,4,16,512]{3,2,1,0:T(8,128)S(1)} %add_select_fusion), channel_id=1, source_target_pairs={{0,4},{1,5},{2,6},{3,7},{8,12},{9,13},{10,14},{11,15},{16,20},{17,... | collective-permute-start | bytes 786440 | tf_op jit(solution)/shard_map/ppermute | solution.py:212
  23.0 6.8 %collective-permute-start.8 = (f32[2,4,16,512]{3,2,1,0:T(8,128)S(1)}, f32[2,4,16,512]{3,2,1,0:T(8,128)S(1)}, u32[]{:S(2)}, u32[]{:S(2)}) collective-permute-start(f32[2,4,16,512]{3,2,1,0:T(8,128)S(1)} %broadcast_select_fusion), channel_id=1, source_target_pairs={{0,2},{1,3},{2,0},{3,1},{4,6},{5,7},{6,4},{7,5},{8,10},{9,11},{10,... | collective-permute-start | bytes 786440 | tf_op jit(solution)/shard_map/ppermute | solution.py:202
  25.9 7.2 %collective-permute-start.4 = (f32[2,4,16,512]{3,2,1,0:T(8,128)S(1)}, f32[2,4,16,512]{3,2,1,0:T(8,128)S(1)}, u32[]{:S(2)}, u32[]{:S(2)}) collective-permute-start(f32[2,4,16,512]{3,2,1,0:T(8,128)S(1)} %broadcast_select_fusion), channel_id=1, source_target_pairs={{0,1},{1,0},{2,3},{3,2},{4,5},{5,4},{6,7},{7,6},{8,9},{9,8},{10,11... | collective-permute-start | bytes 786440 | tf_op jit(solution)/shard_map/ppermute | solution.py:202
  26.2 6.9 %collective-permute-start.5 = (f32[2,4,16,512]{3,2,1,0:T(8,128)S(1)}, f32[2,4,16,512]{3,2,1,0:T(8,128)S(1)}, u32[]{:S(2)}, u32[]{:S(2)}) collective-permute-start(f32[2,4,16,512]{3,2,1,0:T(8,128)S(1)} %broadcast_select_fusion), channel_id=1, source_target_pairs={{0,3},{1,2},{2,1},{3,0},{4,7},{5,6},{6,5},{7,4},{8,11},{9,10},{10,... | collective-permute-start | bytes 786440 | tf_op jit(solution)/shard_map/ppermute | solution.py:202
  29.9 11.6 %collective-permute-start.9 = (f32[2,2,4,16,512]{4,3,2,1,0:T(8,128)S(1)}, f32[2,2,4,16,512]{4,3,2,1,0:T(8,128)S(1)}, u32[]{:S(2)}, u32[]{:S(2)}) collective-permute-start(f32[2,2,4,16,512]{4,3,2,1,0:T(8,128)S(1)} %pad_maximum_fusion.1.refs_1_), channel_id=1, source_target_pairs={{0,24},{1,25},{2,26},{3,27},{4,28},{5,29},{6,30},{7,31},{8,0},{9,1... | collective-permute-start | bytes 1572872 | tf_op jit(solution)/shard_map/ppermute | solution.py:202
  33.1 9.5 %collective-permute-start.6 = (f32[2,2,4,16,512]{4,3,2,1,0:T(8,128)S(1)}, f32[2,2,4,16,512]{4,3,2,1,0:T(8,128)S(1)}, u32[]{:S(2)}, u32[]{:S(2)}) collective-permute-start(f32[2,2,4,16,512]{4,3,2,1,0:T(8,128)S(1)} %pad_maximum_fusion.refs_0_), channel_id=1, source_target_pairs={{0,8},{1,9},{2,10},{3,11},{4,12},{5,13},{6,14},{7,15},{8,16},{9,17... | collective-permute-start | bytes 1572872 | tf_op jit(solution)/shard_map/ppermute | solution.py:202
  33.2 15.1 %collective-permute-start.12 = (f32[2,2,4,16,512]{4,3,2,1,0:T(8,128)S(1)}, f32[2,2,4,16,512]{4,3,2,1,0:T(8,128)S(1)}, u32[]{:S(2)}, u32[]{:S(2)}) collective-permute-start(f32[2,2,4,16,512]{4,3,2,1,0:T(8,128)S(1)} %pad_maximum_fusion.1.refs_1_), channel_id=1, source_target_pairs={{0,8},{1,9},{2,10},{3,11},{4,12},{5,13},{6,14},{7,15},{8,16},{9,17... | collective-permute-start | bytes 1572872 | tf_op jit(solution)/shard_map/ppermute | solution.py:202
  36.6 11.8 %collective-permute-start.11 = (f32[2,2,4,16,512]{4,3,2,1,0:T(8,128)S(1)}, f32[2,2,4,16,512]{4,3,2,1,0:T(8,128)S(1)}, u32[]{:S(2)}, u32[]{:S(2)}) collective-permute-start(f32[2,2,4,16,512]{4,3,2,1,0:T(8,128)S(1)} %pad_maximum_fusion.refs_0_), channel_id=1, source_target_pairs={{0,24},{1,25},{2,26},{3,27},{4,28},{5,29},{6,30},{7,31},{8,0},{9,1... | collective-permute-start | bytes 1572872 | tf_op jit(solution)/shard_map/ppermute | solution.py:202
  41.5 11.7 %collective-permute-start.10 = (f32[2,2,4,16,512]{4,3,2,1,0:T(8,128)S(1)}, f32[2,2,4,16,512]{4,3,2,1,0:T(8,128)S(1)}, u32[]{:S(2)}, u32[]{:S(2)}) collective-permute-start(f32[2,2,4,16,512]{4,3,2,1,0:T(8,128)S(1)} %collective-permute-done.9.refs_1_), channel_id=1, source_target_pairs={{0,24},{1,25},{2,26},{3,27},{4,28},{5,29},{6,30},{7,31},{8,0},{9,1... | collective-permute-start | bytes 1572872 | tf_op jit(solution)/shard_map/ppermute | solution.py:202
  42.7 11.3 %collective-permute-start.7 = (f32[2,2,4,16,512]{4,3,2,1,0:T(8,128)S(1)}, f32[2,2,4,16,512]{4,3,2,1,0:T(8,128)S(1)}, u32[]{:S(2)}, u32[]{:S(2)}) collective-permute-start(f32[2,2,4,16,512]{4,3,2,1,0:T(8,128)S(1)} %collective-permute-done.6.refs_0_), channel_id=1, source_target_pairs={{0,8},{1,9},{2,10},{3,11},{4,12},{5,13},{6,14},{7,15},{8,16},{9,17... | collective-permute-start | bytes 1572872 | tf_op jit(solution)/shard_map/ppermute | solution.py:202
  57.5 4.0 %collective-permute-start.13 = (f32[3,8,16,256]{3,2,1,0:T(8,128)S(1)}, f32[3,8,16,256]{3,2,1,0:T(8,128)S(1)}, u32[]{:S(2)}, u32[]{:S(2)}) collective-permute-start(f32[3,8,16,256]{3,2,1,0:T(8,128)S(1)} %get-tuple-element.40), channel_id=1, source_target_pairs={{0,32},{32,0},{64,96},{96,64},{1,33},{33,1},{65,97},{97,65},{2,34}... | collective-permute-start | bytes 1179656 | tf_op jit(solution)/shard_map/ppermute | solution.py:204
  61.5 12.8 %collective-permute-start.14 = (f32[3,8,16,256]{3,2,1,0:T(8,128)S(1)}, f32[3,8,16,256]{3,2,1,0:T(8,128)S(1)}, u32[]{:S(2)}, u32[]{:S(2)}) collective-permute-start(f32[3,8,16,256]{3,2,1,0:T(8,128)S(1)} %add.30), channel_id=1, source_target_pairs={{0,64},{32,96},{64,0},{96,32},{1,65},{33,97},{65,1},{97,33},{2,66}... | collective-permute-start | bytes 1179656 | tf_op jit(solution)/shard_map/ppermute | solution.py:205
  62.8 2.9 %collective-permute-start.15 = (f32[1,8,16,256]{3,2,1,0:T(8,128)S(1)}, f32[1,8,16,256]{3,2,1,0:T(8,128)S(1)}, u32[]{:S(2)}, u32[]{:S(2)}) collective-permute-start(f32[1,8,16,256]{3,2,1,0:T(8,128)S(1)} %get-tuple-element.44), channel_id=1, source_target_pairs={{0,32},{32,0},{64,96},{96,64},{1,33},{33,1},{65,97},{97,65},{2,34}... | collective-permute-start | bytes 393224 | tf_op jit(solution)/shard_map/ppermute | solution.py:204
  65.8 8.6 %collective-permute-start.16 = (f32[1,8,16,256]{3,2,1,0:T(8,128)S(1)}, f32[1,8,16,256]{3,2,1,0:T(8,128)S(1)}, u32[]{:S(2)}, u32[]{:S(2)}) collective-permute-start(f32[1,8,16,256]{3,2,1,0:T(8,128)S(1)} %add.31), channel_id=1, source_target_pairs={{0,64},{32,96},{64,0},{96,32},{1,65},{33,97},{65,1},{97,33},{2,66}... | collective-permute-start | bytes 393224 | tf_op jit(solution)/shard_map/ppermute | solution.py:205
  74.4 3.2 %collective-permute-start.17 = (f32[3,8,16,256]{3,2,1,0:T(8,128)S(1)}, f32[3,8,16,256]{3,2,1,0:T(8,128)S(1)}, u32[]{:S(2)}, u32[]{:S(2)}) collective-permute-start(f32[3,8,16,256]{3,2,1,0:T(8,128)S(1)} %add.32.refs_0_), channel_id=1, source_target_pairs={{0,32},{32,0},{64,96},{96,64},{1,33},{33,1},{65,97},{97,65},{2,34}... | collective-permute-start | bytes 1179656 | tf_op jit(solution)/shard_map/ppermute | solution.py:204
  76.1 1.5 %collective-permute-start.18 = (f32[1,8,16,256]{3,2,1,0:T(8,128)S(1)}, f32[1,8,16,256]{3,2,1,0:T(8,128)S(1)}, u32[]{:S(2)}, u32[]{:S(2)}) collective-permute-start(f32[1,8,16,256]{3,2,1,0:T(8,128)S(1)} %add.33.refs_2_), channel_id=1, source_target_pairs={{0,32},{32,0},{64,96},{96,64},{1,33},{33,1},{65,97},{97,65},{2,34}... | collective-permute-start | bytes 393224 | tf_op jit(solution)/shard_map/ppermute | solution.py:204

commit v7 on v6

--- a/solution.py
+++ b/solution.py
@@ -149,13 +149,19 @@
 
 
 def place_kernel(*refs):
-    out_ref = refs[-1]
+    out_ref, sems = refs[-2:]
     at_x, _, core = position()
+    copies = []
     for pair, blocks in enumerate(GROUPS):
-        mine, other = refs[2 * pair : 2 * pair + 2]
-        for place, block in enumerate(blocks):
-            out_ref[pl.ds(8 * core, 8), (at_x + block) % 4] = mine[place]
-            out_ref[pl.ds(8 * (1 - core), 8), (at_x + block) % 4] = other[place]
+        for side, ref in enumerate(refs[2 * pair : 2 * pair + 2]):
+            rows = pl.ds(8 * (core if side == 0 else 1 - core), 8)
+            for place, block in enumerate(blocks):
+                target = out_ref.at[rows, (at_x + block) % 4]
+                copies.append(pltpu.make_async_copy(ref.at[place], target, sems.at[len(copies)]))
+    for copy in copies:
+        copy.start()
+    for copy in copies:
+        copy.wait()
 
 
 def place(pieces):
@@ -163,9 +169,10 @@
         place_kernel,
         out_shape=jax.ShapeDtypeStruct((CH, 4, CH, LAGS), jnp.float32),
         in_specs=[VMEM] * len(pieces),
-        out_specs=VMEM,
+        out_specs=pl.BlockSpec(memory_space=pl.ANY),
+        scratch_shapes=[pltpu.SemaphoreType.DMA((8,))],
         compiler_params=pltpu.CompilerParams(vmem_limit_bytes=8 * 2**20),
-    )(*pieces)
+    )(*[pltpu.with_memory_space_constraint(piece, pltpu.VMEM) for piece in pieces])
 
 
 def stage_kernel(high_ref, low_ref, high_out, low_out, sems):

time: 79.2 us -> 79.4 us (level)
  transfers between devices with their start and end apart: 19 -> 19, of which waited for: 9 -> 9; matrix products, arithmetic and copies ran while one was open for 0% -> 0% of each run, Pallas kernels for 21% -> 20%
where the time goes in v7:
time: 79.4 us; the launch traced here: 78.9 us
  waiting for transfers between devices  29 us (37%)
  starting transfers between devices  22.6 us (28%)
  Pallas kernels  20.9 us (26%)
  local copies, waits for them, and re-layouts  5.64 us (7%)
    pallas_call x6, Pallas kernels, correlate(): pl.pallas_call(functools.partial(correlate_kernel, steps, started, finish...  19.1 us
    ppermute x1, waiting for transfers between devices, shards(): lax.ppermute(mine, 'chan', [(8 * s + z, 8 * s + 4 + z) for s in range(4)...  13.1 us
    ppermute x9, starting transfers between devices, send(): return lax.ppermute(value, ('win', 'chan'), pairs)  11 us
    ppermute x2, waiting for transfers between devices, shards(): lax.ppermute(value, 'win', [(w, w ^ 2) for w in range(4)])  6.82 us
    ppermute x4, starting transfers between devices, shards(): lax.ppermute(value, 'win', [(w, w ^ 1) for w in range(4)])  6.37 us
    unnamed x6, local copies, waits for them, and re-layouts  5.6 us
    ppermute x9, waiting for transfers between devices, send(): return lax.ppermute(value, ('win', 'chan'), pairs)  5.32 us
    ppermute x4, waiting for transfers between devices, shards(): lax.ppermute(value, 'win', [(w, w ^ 1) for w in range(4)])  3.75 us
  transfers between devices with their start and end apart: 19, of which 9 were waited for; matrix products, arithmetic and copies ran while one was open for 0% of the time, Pallas kernels for 20%

profile of v7, /device:TPU:25, one launch (start us, length us, event | category | flops | bytes accessed | tf_op | source)
XLA Modules:
  0.0 78.9 jit_solution(641698214908183930)
XLA Ops:
  0.0 1.2 %copy-done.2 = f32[1,2,16,8192]{3,2,1,0:T(8,128)S(1)} copy-done((f32[1,2,16,8192]{3,2,1,0:T(8,128)S(1)}, f32[1,2,16,8192]{3,2,1,0:T(8,128)}, u32[]{:S(2)}) %copy-start.2) | copy-done | bytes 1048600
  3.5 2.2 %copy-done = bf16[8,1024,256]{2,1,0:T(8,128)(2,1)S(1)} copy-done((bf16[8,1024,256]{2,1,0:T(8,128)(2,1)S(1)}, bf16[8,1024,256]{2,1,0:T(8,128)(2,1)}, u32[]{:S(2)}) %copy-start) | copy-done | bytes 4194328
  5.7 2.2 %copy-done.1 = bf16[8,1024,256]{2,1,0:T(8,128)(2,1)S(1)} copy-done((bf16[8,1024,256]{2,1,0:T(8,128)(2,1)S(1)}, bf16[8,1024,256]{2,1,0:T(8,128)(2,1)}, u32[]{:S(2)}) %copy-start.1) | copy-done | bytes 4194328
  8.6 1.3 %collective-permute-start.3 = (f32[2,4,16,512]{3,2,1,0:T(8,128)S(1)}, f32[2,4,16,512]{3,2,1,0:T(8,128)S(1)}, u32[]{:S(2)}, u32[]{:S(2)}) collective-permute-start(f32[2,4,16,512]{3,2,1,0:T(8,128)S(1)} %add_select_fusion), channel_id=1, source_target_pairs={{0,4},{1,5},{2,6},{3,7},{8,12},{9,13},{10,14},{11,15},{16,20},{17,... | collective-permute-start | bytes 786440 | tf_op jit(solution)/shard_map/ppermute | solution.py:219
  9.9 13.1 %collective-permute-done.3 = f32[2,4,16,512]{3,2,1,0:T(8,128)S(1)} collective-permute-done((f32[2,4,16,512]{3,2,1,0:T(8,128)S(1)}, f32[2,4,16,512]{3,2,1,0:T(8,128)S(1)}, u32[]{:S(2)}, u32[]{:S(2)}) %collective-permute-start.3) | collective-permute-done | bytes 262176 | tf_op jit(solution)/shard_map/ppermute | solution.py:219
  23.0 2.8 %collective-permute-start.8 = (f32[2,4,16,512]{3,2,1,0:T(8,128)S(1)}, f32[2,4,16,512]{3,2,1,0:T(8,128)S(1)}, u32[]{:S(2)}, u32[]{:S(2)}) collective-permute-start(f32[2,4,16,512]{3,2,1,0:T(8,128)S(1)} %broadcast_select_fusion), channel_id=1, source_target_pairs={{0,2},{1,3},{2,0},{3,1},{4,6},{5,7},{6,4},{7,5},{8,10},{9,11},{10,... | collective-permute-start | bytes 786440 | tf_op jit(solution)/shard_map/ppermute | solution.py:209
  26.7 3.1 %collective-permute-done.8 = f32[2,4,16,512]{3,2,1,0:T(8,128)S(1)} collective-permute-done((f32[2,4,16,512]{3,2,1,0:T(8,128)S(1)}, f32[2,4,16,512]{3,2,1,0:T(8,128)S(1)}, u32[]{:S(2)}, u32[]{:S(2)}) %collective-permute-start.8) | collective-permute-done | bytes 262176 | tf_op jit(solution)/shard_map/ppermute | solution.py:209
  29.9 2.1 %collective-permute-start.9 = (f32[2,2,4,16,512]{4,3,2,1,0:T(8,128)S(1)}, f32[2,2,4,16,512]{4,3,2,1,0:T(8,128)S(1)}, u32[]{:S(2)}, u32[]{:S(2)}) collective-permute-start(f32[2,2,4,16,512]{4,3,2,1,0:T(8,128)S(1)} %pad_maximum_fusion.1.refs_1_), channel_id=1, source_target_pairs={{0,24},{1,25},{2,26},{3,27},{4,28},{5,29},{6,30},{7,31},{8,0},{9,1... | collective-permute-start | bytes 1572872 | tf_op jit(solution)/shard_map/ppermute | solution.py:209
  32.0 1.1 %collective-permute-done.4 = f32[2,4,16,512]{3,2,1,0:T(8,128)S(1)} collective-permute-done((f32[2,4,16,512]{3,2,1,0:T(8,128)S(1)}, f32[2,4,16,512]{3,2,1,0:T(8,128)S(1)}, u32[]{:S(2)}, u32[]{:S(2)}) %collective-permute-start.4) | collective-permute-done | bytes 262176 | tf_op jit(solution)/shard_map/ppermute | solution.py:209
  33.2 3.4 %collective-permute-start.12 = (f32[2,2,4,16,512]{4,3,2,1,0:T(8,128)S(1)}, f32[2,2,4,16,512]{4,3,2,1,0:T(8,128)S(1)}, u32[]{:S(2)}, u32[]{:S(2)}) collective-permute-start(f32[2,2,4,16,512]{4,3,2,1,0:T(8,128)S(1)} %pad_maximum_fusion.1.refs_1_), channel_id=1, source_target_pairs={{0,8},{1,9},{2,10},{3,11},{4,12},{5,13},{6,14},{7,15},{8,16},{9,17... | collective-permute-start | bytes 1572872 | tf_op jit(solution)/shard_map/ppermute | solution.py:209
  36.6 4.9 %shard_map.39.refs_2_ = f32[4,16,16,256]{3,2,1,0:T(8,128)S(1)} custom-call(f32[8,4,16,512]{3,2,1,0:T(8,128)S(1)} %get-tuple-element.27.x_ref, bf16[8,1024,256]{2,1,0:T(8,128)(2,1)S(1)} %get-tuple-element.34.high_ref, bf16[8,1024,256]{2,1,0:T(8,128)(2,1)S(1)} %get-tuple-element.35.low_ref, f32[2,2,4,16,512]{4,3,2,1,0:T(8,128)S(1)} %pad_maximum_fusion.refs_0_, ...), custom_call_target="tpu_custom_call" | custom-call | flops 3221225472 | bytes 12582912 | tf_op jit(solution)/shard_map/pallas_call | solution.py:137
  41.5 1.2 %collective-permute-start.10 = (f32[2,2,4,16,512]{4,3,2,1,0:T(8,128)S(1)}, f32[2,2,4,16,512]{4,3,2,1,0:T(8,128)S(1)}, u32[]{:S(2)}, u32[]{:S(2)}) collective-permute-start(f32[2,2,4,16,512]{4,3,2,1,0:T(8,128)S(1)} %collective-permute-done.9.refs_1_), channel_id=1, source_target_pairs={{0,24},{1,25},{2,26},{3,27},{4,28},{5,29},{6,30},{7,31},{8,0},{9,1... | collective-permute-start | bytes 1572872 | tf_op jit(solution)/shard_map/ppermute | solution.py:209
  43.2 4.8 %shard_map.40.refs_2_ = f32[4,16,16,256]{3,2,1,0:T(8,128)S(1)} custom-call(f32[8,4,16,512]{3,2,1,0:T(8,128)S(1)} %get-tuple-element.27.x_ref, bf16[8,1024,256]{2,1,0:T(8,128)(2,1)S(1)} %get-tuple-element.34.high_ref, bf16[8,1024,256]{2,1,0:T(8,128)(2,1)S(1)} %get-tuple-element.35.low_ref, ...), custom_call_target="tpu_custom_call", output_to_operand_aliasing={{}: (5, {})} | custom-call | flops 3221225472 | bytes 12582912 | tf_op jit(solution)/shard_map/pallas_call | solution.py:137
  48.4 4.8 %shard_map.41.refs_2_ = f32[4,16,16,256]{3,2,1,0:T(8,128)S(1)} custom-call(f32[8,4,16,512]{3,2,1,0:T(8,128)S(1)} %get-tuple-element.27.x_ref, bf16[8,1024,256]{2,1,0:T(8,128)(2,1)S(1)} %get-tuple-element.34.high_ref, bf16[8,1024,256]{2,1,0:T(8,128)(2,1)S(1)} %get-tuple-element.35.low_ref, ...), custom_call_target="tpu_custom_call", output_to_operand_aliasing={{}: (5, {})} | custom-call | flops 3221225472 | bytes 12582912 | tf_op jit(solution)/shard_map/pallas_call | solution.py:137
  54.0 3.5 %shard_map.42 = (f32[4,16,16,256]{3,2,1,0:T(8,128)S(1)}, f32[3,8,16,256]{3,2,1,0:T(8,128)S(1)}, f32[3,8,16,256]{3,2,1,0:T(8,128)S(1)}) custom-call(f32[8,4,16,512]{3,2,1,0:T(8,128)S(1)} %get-tuple-element.27.x_ref, bf16[8,1024,256]{2,1,0:T(8,128)(2,1)S(1)} %get-tuple-element.34.high_ref, ...), custom_call_target="tpu_custom_call", output_to_operand_aliasing={{0}: (5, {})} | custom-call | flops 2415919104 | bytes 9437184 | tf_op jit(solution)/shard_map/pallas_call | solution.py:137
  57.5 2.7 %collective-permute-start.13 = (f32[3,8,16,256]{3,2,1,0:T(8,128)S(1)}, f32[3,8,16,256]{3,2,1,0:T(8,128)S(1)}, u32[]{:S(2)}, u32[]{:S(2)}) collective-permute-start(f32[3,8,16,256]{3,2,1,0:T(8,128)S(1)} %get-tuple-element.40), channel_id=1, source_target_pairs={{0,32},{32,0},{64,96},{96,64},{1,33},{33,1},{65,97},{97,65},{2,34}... | collective-permute-start | bytes 1179656 | tf_op jit(solution)/shard_map/ppermute | solution.py:211
  60.1 1.3 %collective-permute-done.13 = f32[3,8,16,256]{3,2,1,0:T(8,128)S(1)} collective-permute-done((f32[3,8,16,256]{3,2,1,0:T(8,128)S(1)}, f32[3,8,16,256]{3,2,1,0:T(8,128)S(1)}, u32[]{:S(2)}, u32[]{:S(2)}) %collective-permute-start.13) | collective-permute-done | bytes 393248 | tf_op jit(solution)/shard_map/ppermute | solution.py:211
  61.6 1.2 %shard_map.44 = (f32[4,16,16,256]{3,2,1,0:T(8,128)S(1)}, f32[1,8,16,256]{3,2,1,0:T(8,128)S(1)}, f32[1,8,16,256]{3,2,1,0:T(8,128)S(1)}) custom-call(f32[8,4,16,512]{3,2,1,0:T(8,128)S(1)} %get-tuple-element.27.x_ref, bf16[8,1024,256]{2,1,0:T(8,128)(2,1)S(1)} %get-tuple-element.34.high_ref, ...), custom_call_target="tpu_custom_call", output_to_operand_aliasing={{0}: (5, {})} | custom-call | flops 1610612736 | bytes 6291456 | tf_op jit(solution)/shard_map/pallas_call | solution.py:137
  62.8 1.9 %collective-permute-start.15 = (f32[1,8,16,256]{3,2,1,0:T(8,128)S(1)}, f32[1,8,16,256]{3,2,1,0:T(8,128)S(1)}, u32[]{:S(2)}, u32[]{:S(2)}) collective-permute-start(f32[1,8,16,256]{3,2,1,0:T(8,128)S(1)} %get-tuple-element.44), channel_id=1, source_target_pairs={{0,32},{32,0},{64,96},{96,64},{1,33},{33,1},{65,97},{97,65},{2,34}... | collective-permute-start | bytes 393224 | tf_op jit(solution)/shard_map/ppermute | solution.py:211
  65.8 1.8 %collective-permute-start.16 = (f32[1,8,16,256]{3,2,1,0:T(8,128)S(1)}, f32[1,8,16,256]{3,2,1,0:T(8,128)S(1)}, u32[]{:S(2)}, u32[]{:S(2)}) collective-permute-start(f32[1,8,16,256]{3,2,1,0:T(8,128)S(1)} %add.31), channel_id=1, source_target_pairs={{0,64},{32,96},{64,0},{96,32},{1,65},{33,97},{65,1},{97,33},{2,66}... | collective-permute-start | bytes 393224 | tf_op jit(solution)/shard_map/ppermute | solution.py:212
  67.5 6.8 %collective-permute-done.16 = f32[1,8,16,256]{3,2,1,0:T(8,128)S(1)} collective-permute-done((f32[1,8,16,256]{3,2,1,0:T(8,128)S(1)}, f32[1,8,16,256]{3,2,1,0:T(8,128)S(1)}, u32[]{:S(2)}, u32[]{:S(2)}) %collective-permute-start.16) | collective-permute-done | bytes 131104 | tf_op jit(solution)/shard_map/ppermute | solution.py:212
  74.4 1.7 %collective-permute-start.17 = (f32[3,8,16,256]{3,2,1,0:T(8,128)S(1)}, f32[3,8,16,256]{3,2,1,0:T(8,128)S(1)}, u32[]{:S(2)}, u32[]{:S(2)}) collective-permute-start(f32[3,8,16,256]{3,2,1,0:T(8,128)S(1)} %add.32.refs_0_), channel_id=1, source_target_pairs={{0,32},{32,0},{64,96},{96,64},{1,33},{33,1},{65,97},{97,65},{2,34}... | collective-permute-start | bytes 1179656 | tf_op jit(solution)/shard_map/ppermute | solution.py:211
  76.2 1.4 %collective-permute-done.18.refs_3_ = f32[1,8,16,256]{3,2,1,0:T(8,128)S(1)} collective-permute-done((f32[1,8,16,256]{3,2,1,0:T(8,128)S(1)}, f32[1,8,16,256]{3,2,1,0:T(8,128)S(1)}, u32[]{:S(2)}, u32[]{:S(2)}) %collective-permute-start.18) | collective-permute-done | bytes 131104 | tf_op jit(solution)/shard_map/ppermute | solution.py:211
  77.6 1.0 %shard_map.45 = f32[16,4,16,256]{3,2,1,0:T(8,128)} custom-call(f32[3,8,16,256]{3,2,1,0:T(8,128)S(1)} %add.32.refs_0_, f32[3,8,16,256]{3,2,1,0:T(8,128)S(1)} %collective-permute-done.17.refs_1_, f32[1,8,16,256]{3,2,1,0:T(8,128)S(1)} %add.33.refs_2_, f32[1,8,16,256]{3,2,1,0:T(8,128)S(1)} %collective-permute-done.18.refs_3_), custom_call_target="tpu_custom_call" | custom-call | tf_op jit(solution)/shard_map/pallas_call | solution.py:168
  (38 shorter events, 7.1 us)
Async XLA Ops:
  0.0 1.2 %copy-start.2 = (f32[1,2,16,8192]{3,2,1,0:T(8,128)S(1)}, f32[1,2,16,8192]{3,2,1,0:T(8,128)}, u32[]{:S(2)}) copy-start(f32[1,2,16,8192]{3,2,1,0:T(8,128)} %param.3) | copy-start | bytes 3145732
  1.5 7.0 %collective-permute-start = (f32[2,4,16,512]{3,2,1,0:T(8,128)S(1)}, f32[2,4,16,512]{3,2,1,0:T(8,128)S(1)}, u32[]{:S(2)}, u32[]{:S(2)}) collective-permute-start(f32[2,4,16,512]{3,2,1,0:T(8,128)S(1)} %get-tuple-element.29), channel_id=1, source_target_pairs={{0,1},{8,9},{16,17},{24,25},{32,33},{40,41},{48,49},{56,57},{64,65... | collective-permute-start | bytes 786440 | tf_op jit(solution)/shard_map/ppermute | solution.py:216
  2.1 6.3 %collective-permute-start.1 = (f32[2,4,16,512]{3,2,1,0:T(8,128)S(1)}, f32[2,4,16,512]{3,2,1,0:T(8,128)S(1)}, u32[]{:S(2)}, u32[]{:S(2)}) collective-permute-start(f32[2,4,16,512]{3,2,1,0:T(8,128)S(1)} %get-tuple-element.30), channel_id=1, source_target_pairs={{0,2},{8,10},{16,18},{24,26},{32,34},{40,42},{48,50},{56,58},{64,6... | collective-permute-start | bytes 786440 | tf_op jit(solution)/shard_map/ppermute | solution.py:216
  2.8 5.7 %collective-permute-start.2 = (f32[2,4,16,512]{3,2,1,0:T(8,128)S(1)}, f32[2,4,16,512]{3,2,1,0:T(8,128)S(1)}, u32[]{:S(2)}, u32[]{:S(2)}) collective-permute-start(f32[2,4,16,512]{3,2,1,0:T(8,128)S(1)} %get-tuple-element.31), channel_id=1, source_target_pairs={{0,3},{8,11},{16,19},{24,27},{32,35},{40,43},{48,51},{56,59},{64,6... | collective-permute-start | bytes 786440 | tf_op jit(solution)/shard_map/ppermute | solution.py:216
  3.5 2.2 %copy-start = (bf16[8,1024,256]{2,1,0:T(8,128)(2,1)S(1)}, bf16[8,1024,256]{2,1,0:T(8,128)(2,1)}, u32[]{:S(2)}) copy-start(bf16[8,1024,256]{2,1,0:T(8,128)(2,1)} %constant.43.clone.high_ref) | copy-start | bytes 12582916
  5.7 2.2 %copy-start.1 = (bf16[8,1024,256]{2,1,0:T(8,128)(2,1)S(1)}, bf16[8,1024,256]{2,1,0:T(8,128)(2,1)}, u32[]{:S(2)}) copy-start(bf16[8,1024,256]{2,1,0:T(8,128)(2,1)} %constant.44.clone.low_ref) | copy-start | bytes 12582916
  8.6 14.4 %collective-permute-start.3 = (f32[2,4,16,512]{3,2,1,0:T(8,128)S(1)}, f32[2,4,16,512]{3,2,1,0:T(8,128)S(1)}, u32[]{:S(2)}, u32[]{:S(2)}) collective-permute-start(f32[2,4,16,512]{3,2,1,0:T(8,128)S(1)} %add_select_fusion), channel_id=1, source_target_pairs={{0,4},{1,5},{2,6},{3,7},{8,12},{9,13},{10,14},{11,15},{16,20},{17,... | collective-permute-start | bytes 786440 | tf_op jit(solution)/shard_map/ppermute | solution.py:219
  23.0 6.8 %collective-permute-start.8 = (f32[2,4,16,512]{3,2,1,0:T(8,128)S(1)}, f32[2,4,16,512]{3,2,1,0:T(8,128)S(1)}, u32[]{:S(2)}, u32[]{:S(2)}) collective-permute-start(f32[2,4,16,512]{3,2,1,0:T(8,128)S(1)} %broadcast_select_fusion), channel_id=1, source_target_pairs={{0,2},{1,3},{2,0},{3,1},{4,6},{5,7},{6,4},{7,5},{8,10},{9,11},{10,... | collective-permute-start | bytes 786440 | tf_op jit(solution)/shard_map/ppermute | solution.py:209
  25.9 7.2 %collective-permute-start.4 = (f32[2,4,16,512]{3,2,1,0:T(8,128)S(1)}, f32[2,4,16,512]{3,2,1,0:T(8,128)S(1)}, u32[]{:S(2)}, u32[]{:S(2)}) collective-permute-start(f32[2,4,16,512]{3,2,1,0:T(8,128)S(1)} %broadcast_select_fusion), channel_id=1, source_target_pairs={{0,1},{1,0},{2,3},{3,2},{4,5},{5,4},{6,7},{7,6},{8,9},{9,8},{10,11... | collective-permute-start | bytes 786440 | tf_op jit(solution)/shard_map/ppermute | solution.py:209
  26.2 6.9 %collective-permute-start.5 = (f32[2,4,16,512]{3,2,1,0:T(8,128)S(1)}, f32[2,4,16,512]{3,2,1,0:T(8,128)S(1)}, u32[]{:S(2)}, u32[]{:S(2)}) collective-permute-start(f32[2,4,16,512]{3,2,1,0:T(8,128)S(1)} %broadcast_select_fusion), channel_id=1, source_target_pairs={{0,3},{1,2},{2,1},{3,0},{4,7},{5,6},{6,5},{7,4},{8,11},{9,10},{10,... | collective-permute-start | bytes 786440 | tf_op jit(solution)/shard_map/ppermute | solution.py:209
  29.9 11.6 %collective-permute-start.9 = (f32[2,2,4,16,512]{4,3,2,1,0:T(8,128)S(1)}, f32[2,2,4,16,512]{4,3,2,1,0:T(8,128)S(1)}, u32[]{:S(2)}, u32[]{:S(2)}) collective-permute-start(f32[2,2,4,16,512]{4,3,2,1,0:T(8,128)S(1)} %pad_maximum_fusion.1.refs_1_), channel_id=1, source_target_pairs={{0,24},{1,25},{2,26},{3,27},{4,28},{5,29},{6,30},{7,31},{8,0},{9,1... | collective-permute-start | bytes 1572872 | tf_op jit(solution)/shard_map/ppermute | solution.py:209
  33.1 9.5 %collective-permute-start.6 = (f32[2,2,4,16,512]{4,3,2,1,0:T(8,128)S(1)}, f32[2,2,4,16,512]{4,3,2,1,0:T(8,128)S(1)}, u32[]{:S(2)}, u32[]{:S(2)}) collective-permute-start(f32[2,2,4,16,512]{4,3,2,1,0:T(8,128)S(1)} %pad_maximum_fusion.refs_0_), channel_id=1, source_target_pairs={{0,8},{1,9},{2,10},{3,11},{4,12},{5,13},{6,14},{7,15},{8,16},{9,17... | collective-permute-start | bytes 1572872 | tf_op jit(solution)/shard_map/ppermute | solution.py:209
  33.2 15.1 %collective-permute-start.12 = (f32[2,2,4,16,512]{4,3,2,1,0:T(8,128)S(1)}, f32[2,2,4,16,512]{4,3,2,1,0:T(8,128)S(1)}, u32[]{:S(2)}, u32[]{:S(2)}) collective-permute-start(f32[2,2,4,16,512]{4,3,2,1,0:T(8,128)S(1)} %pad_maximum_fusion.1.refs_1_), channel_id=1, source_target_pairs={{0,8},{1,9},{2,10},{3,11},{4,12},{5,13},{6,14},{7,15},{8,16},{9,17... | collective-permute-start | bytes 1572872 | tf_op jit(solution)/shard_map/ppermute | solution.py:209
  36.6 11.8 %collective-permute-start.11 = (f32[2,2,4,16,512]{4,3,2,1,0:T(8,128)S(1)}, f32[2,2,4,16,512]{4,3,2,1,0:T(8,128)S(1)}, u32[]{:S(2)}, u32[]{:S(2)}) collective-permute-start(f32[2,2,4,16,512]{4,3,2,1,0:T(8,128)S(1)} %pad_maximum_fusion.refs_0_), channel_id=1, source_target_pairs={{0,24},{1,25},{2,26},{3,27},{4,28},{5,29},{6,30},{7,31},{8,0},{9,1... | collective-permute-start | bytes 1572872 | tf_op jit(solution)/shard_map/ppermute | solution.py:209
  41.5 11.7 %collective-permute-start.10 = (f32[2,2,4,16,512]{4,3,2,1,0:T(8,128)S(1)}, f32[2,2,4,16,512]{4,3,2,1,0:T(8,128)S(1)}, u32[]{:S(2)}, u32[]{:S(2)}) collective-permute-start(f32[2,2,4,16,512]{4,3,2,1,0:T(8,128)S(1)} %collective-permute-done.9.refs_1_), channel_id=1, source_target_pairs={{0,24},{1,25},{2,26},{3,27},{4,28},{5,29},{6,30},{7,31},{8,0},{9,1... | collective-permute-start | bytes 1572872 | tf_op jit(solution)/shard_map/ppermute | solution.py:209
  42.7 11.3 %collective-permute-start.7 = (f32[2,2,4,16,512]{4,3,2,1,0:T(8,128)S(1)}, f32[2,2,4,16,512]{4,3,2,1,0:T(8,128)S(1)}, u32[]{:S(2)}, u32[]{:S(2)}) collective-permute-start(f32[2,2,4,16,512]{4,3,2,1,0:T(8,128)S(1)} %collective-permute-done.6.refs_0_), channel_id=1, source_target_pairs={{0,8},{1,9},{2,10},{3,11},{4,12},{5,13},{6,14},{7,15},{8,16},{9,17... | collective-permute-start | bytes 1572872 | tf_op jit(solution)/shard_map/ppermute | solution.py:209
  57.5 4.0 %collective-permute-start.13 = (f32[3,8,16,256]{3,2,1,0:T(8,128)S(1)}, f32[3,8,16,256]{3,2,1,0:T(8,128)S(1)}, u32[]{:S(2)}, u32[]{:S(2)}) collective-permute-start(f32[3,8,16,256]{3,2,1,0:T(8,128)S(1)} %get-tuple-element.40), channel_id=1, source_target_pairs={{0,32},{32,0},{64,96},{96,64},{1,33},{33,1},{65,97},{97,65},{2,34}... | collective-permute-start | bytes 1179656 | tf_op jit(solution)/shard_map/ppermute | solution.py:211
  61.5 12.8 %collective-permute-start.14 = (f32[3,8,16,256]{3,2,1,0:T(8,128)S(1)}, f32[3,8,16,256]{3,2,1,0:T(8,128)S(1)}, u32[]{:S(2)}, u32[]{:S(2)}) collective-permute-start(f32[3,8,16,256]{3,2,1,0:T(8,128)S(1)} %add.30), channel_id=1, source_target_pairs={{0,64},{32,96},{64,0},{96,32},{1,65},{33,97},{65,1},{97,33},{2,66}... | collective-permute-start | bytes 1179656 | tf_op jit(solution)/shard_map/ppermute | solution.py:212
  62.8 2.9 %collective-permute-start.15 = (f32[1,8,16,256]{3,2,1,0:T(8,128)S(1)}, f32[1,8,16,256]{3,2,1,0:T(8,128)S(1)}, u32[]{:S(2)}, u32[]{:S(2)}) collective-permute-start(f32[1,8,16,256]{3,2,1,0:T(8,128)S(1)} %get-tuple-element.44), channel_id=1, source_target_pairs={{0,32},{32,0},{64,96},{96,64},{1,33},{33,1},{65,97},{97,65},{2,34}... | collective-permute-start | bytes 393224 | tf_op jit(solution)/shard_map/ppermute | solution.py:211
  65.8 8.6 %collective-permute-start.16 = (f32[1,8,16,256]{3,2,1,0:T(8,128)S(1)}, f32[1,8,16,256]{3,2,1,0:T(8,128)S(1)}, u32[]{:S(2)}, u32[]{:S(2)}) collective-permute-start(f32[1,8,16,256]{3,2,1,0:T(8,128)S(1)} %add.31), channel_id=1, source_target_pairs={{0,64},{32,96},{64,0},{96,32},{1,65},{33,97},{65,1},{97,33},{2,66}... | collective-permute-start | bytes 393224 | tf_op jit(solution)/shard_map/ppermute | solution.py:212
  74.4 3.2 %collective-permute-start.17 = (f32[3,8,16,256]{3,2,1,0:T(8,128)S(1)}, f32[3,8,16,256]{3,2,1,0:T(8,128)S(1)}, u32[]{:S(2)}, u32[]{:S(2)}) collective-permute-start(f32[3,8,16,256]{3,2,1,0:T(8,128)S(1)} %add.32.refs_0_), channel_id=1, source_target_pairs={{0,32},{32,0},{64,96},{96,64},{1,33},{33,1},{65,97},{97,65},{2,34}... | collective-permute-start | bytes 1179656 | tf_op jit(solution)/shard_map/ppermute | solution.py:211
  76.1 1.5 %collective-permute-start.18 = (f32[1,8,16,256]{3,2,1,0:T(8,128)S(1)}, f32[1,8,16,256]{3,2,1,0:T(8,128)S(1)}, u32[]{:S(2)}, u32[]{:S(2)}) collective-permute-start(f32[1,8,16,256]{3,2,1,0:T(8,128)S(1)} %add.33.refs_2_), channel_id=1, source_target_pairs={{0,32},{32,0},{64,96},{96,64},{1,33},{33,1},{65,97},{97,65},{2,34}... | collective-permute-start | bytes 393224 | tf_op jit(solution)/shard_map/ppermute | solution.py:211
